TPU v7x, 128 devices: a whole 4x4x4 slice. The times are simulated.
128 devices in a mesh: slab: 128 (over x, z, y, core).
Axes of the slice: x: 4, y: 4, z: 4, core: 2. Of those that a mesh axis runs over, the one named last changes fastest.
Arguments:
- velocity: float32 [3, 1024, 32, 128], P(None, 'slab'), may hold values from -6 to 6
- node_coords: float32 [16384, 3, 128], P('slab'), may hold values from 0 to 1
- node_force: float32 [16384, 3, 128], P('slab'), may hold values from -12 to 12
- block_slab: int32 [16384, 1], P('slab'), may hold values from 0 to 127; in each aligned block of 128 rows (0 to 127, 128 to 255, ...) at most 2 rows name the same one
- block_offset: int32 [16384, 2], P('slab'), may hold values from 1 to 25
Outputs:
- new_velocity: float32 [3, 1024, 32, 128], P(None, 'slab')
- node_velocity: float32 [16384, 3, 128], P('slab')
Inputs may be any that keep to these rules, and one draw needn't show every extreme that they name: `block_slab`: among the 128 blocks of one device at most 2 name the same slab, and in every draw some device has exactly 2 blocks in one slab.
All inputs are finite; a program needn't handle non-finite values.
Results may differ from a plain program's by a relative error of at most 0.0003.
Values sent between devices are 32-bit elements; how exact they have to be, the bound alone decides.
No kernel may reach another device: no remote copies, remote signals or barrier semaphores. Data moves between devices by JAX's collectives and lax.ppermute only.
A program may use at most 128 MiB of HBM per device.

v0:
```python
import functools

import jax
import jax.numpy as jnp
from jax import lax
from jax.experimental import pallas as pl
from jax.experimental.pallas import tpu as pltpu
from jax.sharding import PartitionSpec as P

CX = 8
NY = 32
NZ = 128
SUBSTEPS = 3
LANES = 128
WINDOWS = 25
UNROLL = 4

time_step = 0.1
viscosity = 0.2

f32 = jnp.float32
bf16 = jnp.bfloat16

COS_TERMS = (
    0.7071067481276141,
    -0.21808909214261787,
    0.011209883548645258,
    -0.0002299265021950359,
    2.3703615380631122e-06,
)

VMEM_LIMIT = 48 * 1024 * 1024


def vmem():
    return pl.BlockSpec(memory_space=pltpu.VMEM)


def params():
    return pltpu.CompilerParams(vmem_limit_bytes=VMEM_LIMIT)


def phi(distance):
    t = jnp.minimum(distance * distance, 4.0)
    total = COS_TERMS[4] * t + COS_TERMS[3]
    for term in (COS_TERMS[2], COS_TERMS[1], COS_TERMS[0]):
        total = total * t + term
    return total * total


def split_2(values):
    high = values.astype(bf16).astype(f32)
    return high, values - high


def split_3(values):
    high = values.astype(bf16)
    rest = values - high.astype(f32)
    middle = rest.astype(bf16)
    low = (rest - middle.astype(f32)).astype(bf16)
    return high, middle, low


def dot(a, b, dims):
    return lax.dot_general(a, b, (dims, ((), ())), preferred_element_type=f32)


NN = ((1,), (0,))
NT = ((1,), (1,))


def prep_kernel(coords, force, slab, offset, out, back):
    row = lax.broadcasted_iota(jnp.int32, (LANES, LANES), 0)
    col = lax.broadcasted_iota(jnp.int32, (LANES, LANES), 1)
    hot = (jnp.broadcast_to(slab[...], (LANES, LANES)) == row).astype(f32)
    before = (row < col).astype(f32).astype(bf16)
    rank = dot(hot.astype(bf16), before, NN)
    first = jnp.where(rank < 0.5, hot, 0.0)
    second = hot - first
    back[:, :LANES] = first.T.astype(bf16)
    back[:, LANES:] = second.T.astype(bf16)
    both = jnp.concatenate([first, second], axis=0).astype(bf16)
    for quantity in range(6):
        source = coords if quantity < 3 else force
        high, middle, low = split_3(source[quantity % 3])
        placed = dot(both, high, NN) + dot(both, middle, NN) + dot(both, low, NN)
        for slot in range(2):
            start = (slot * 6 + quantity) * LANES
            out[:, 0, start : start + LANES] = placed[slot * LANES : (slot + 1) * LANES]
    offsets = offset[...].astype(f32)
    rows = lax.broadcasted_iota(jnp.int32, (8, LANES), 0)
    spread_y = jnp.broadcast_to(offsets[0:1], (8, LANES))
    spread_z = jnp.broadcast_to(offsets[1:2], (8, LANES))
    tail = jnp.zeros((LANES, LANES), f32)
    empty = jnp.zeros((LANES - 8, LANES), f32)
    for slot, chosen in ((0, first), (1, second)):
        table = jnp.where(rows == 2 * slot, spread_y, 0.0) + jnp.where(
            rows == 2 * slot + 1, spread_z, 0.0
        )
        table = jnp.concatenate([table, empty], axis=0).astype(bf16)
        tail = tail + dot(chosen.astype(bf16), table, NT)
    out[:, 0, 12 * LANES :] = tail


def prep(coords, force, slab, offset):
    return pl.pallas_call(
        prep_kernel,
        out_shape=(
            jax.ShapeDtypeStruct((LANES, 1, 13 * LANES), f32),
            jax.ShapeDtypeStruct((LANES, 2 * LANES), bf16),
        ),
        in_specs=[vmem()] * 4,
        out_specs=(vmem(), vmem()),
        compiler_params=params(),
    )(coords, force, slab, offset)


def node_weights(got, device, slot):
    taps = lax.broadcasted_iota(jnp.int32, (8, LANES), 0).astype(f32) - 1.0
    parts = []
    for dim, reach in ((0, CX - 4.0), (1, 5.0), (2, 5.0)):
        start = (slot * 6 + dim) * LANES
        place = got[device, :, start : start + LANES]
        parts.append(phi(taps - reach * place))
    weight_x, weight_y, weight_z = parts
    joint = jnp.concatenate([weight_y[i : i + 1] * weight_x for i in range(8)], axis=0)
    high, low = split_2(joint)
    stacked = jnp.concatenate([high, low], axis=0).astype(bf16)
    return stacked, weight_z


def window(offsets, device, slot):
    y = offsets[device, 0, 2 * slot].astype(jnp.int32) - 1
    z = offsets[device, 0, 2 * slot + 1].astype(jnp.int32) - 1
    return jnp.clip(y, 0, WINDOWS - 1), jnp.clip(z, 0, WINDOWS - 1)


def spread_kernel(got, grid, total, rows_yx, offsets, sem):
    copy = pltpu.make_async_copy(got.at[:, :, pl.ds(12 * LANES, LANES)], offsets, sem)
    copy.start()
    total[...] = jnp.zeros_like(total)
    copy.wait()

    def step(index, carry):
        pieces = []
        for sub in range(UNROLL):
            device = index * UNROLL + sub
            for slot in range(2):
                stacked, weight_z = node_weights(got, device, slot)
                loads = []
                for c in range(3):
                    start = (slot * 6 + 3 + c) * LANES
                    loads.append(got[device, :, start : start + LANES] * weight_z)
                high, low = split_2(jnp.concatenate(loads, axis=0))
                load = jnp.concatenate([high, low], axis=0).astype(bf16)
                out = dot(load, stacked, NT)
                pieces.append((device, slot, out[:24] + out[24:]))
        for device, slot, out in pieces:
            y, z = window(offsets, device, slot)
            for c in range(3):
                total[y, c, pl.ds(z, 8), :] += out[c * 8 : (c + 1) * 8]
        return carry

    lax.fori_loop(0, LANES // UNROLL, step, 0)
    left = jnp.zeros((96, LANES), f32)
    right = jnp.zeros((96, LANES), f32)
    lane = lax.broadcasted_iota(jnp.int32, (96, LANES), 1)
    for y in range(WINDOWS):
        part = total[y].reshape(96, LANES)
        part = part + pltpu.roll(part, 64, 1)
        part = jnp.where(lane < 64, part, 0.0)
        shift = 8 * y % LANES
        moved = pltpu.roll(part, shift, 1) if shift else part
        if 8 * y >= LANES:
            right = right + moved
        elif 8 * y + 64 <= LANES:
            left = left + moved
        else:
            left = left + jnp.where(lane >= shift, moved, 0.0)
            right = right + jnp.where(lane < shift, moved, 0.0)
    pad = jnp.zeros((32, LANES), f32)
    rows_yx[:LANES] = jnp.concatenate([left, pad], axis=0).T
    rows_yx[LANES:] = jnp.concatenate([right, pad], axis=0).T
    for a in range(CX):
        grid[a] = rows_yx[pl.ds(a, NY, stride=CX), :]


def spread(got):
    return pl.pallas_call(
        spread_kernel,
        out_shape=jax.ShapeDtypeStruct((CX, NY, LANES), f32),
        in_specs=[vmem()],
        out_specs=vmem(),
        scratch_shapes=[
            pltpu.VMEM((WINDOWS, 3, 32, LANES), f32),
            pltpu.VMEM((NY * CX, LANES), f32),
            pltpu.SMEM((LANES, 1, LANES), f32),
            pltpu.SemaphoreType.DMA,
        ],
        compiler_params=params(),
    )(got)


def fluid_kernel(velocity, behind, ahead, grid, grid_behind, grid_ahead, out, step_1, step_2):
    lane = lax.broadcasted_iota(jnp.int32, (NY, NZ), 1)

    def load_0(c, p):
        if p < 0:
            return behind[c, p + 3]
        if p >= CX:
            return ahead[c, p - CX]
        return velocity[c, p]

    def load_1(c, p):
        return step_1[c, p + 2]

    def load_2(c, p):
        return step_2[c, p + 1]

    def store_1(c, p, value):
        step_1[c, p + 2] = value

    def store_2(c, p, value):
        step_2[c, p + 1] = value

    def store_3(c, p, value):
        out[c, p] = value

    def forcing(c, p):
        if p < 0:
            cells = grid_behind[p + 2]
        elif p >= CX:
            cells = grid_ahead[p - CX]
        else:
            cells = grid[p]
        if c:
            cells = pltpu.roll(cells, LANES - 32 * c, 1)
        return jnp.where(lane < 32, cells, 0.0)

    stages = ((load_0, store_1, 2), (load_1, store_2, 1), (load_2, store_3, 0))
    for load, store, width in stages:
        for p in range(-width, CX + width):
            centers = [load(c, p) for c in range(3)]
            for c in range(3):
                center = centers[c]
                x_plus, x_minus = load(c, p + 1), load(c, p - 1)
                y_plus, y_minus = pltpu.roll(center, NY - 1, 0), pltpu.roll(center, 1, 0)
                z_plus, z_minus = pltpu.roll(center, NZ - 1, 1), pltpu.roll(center, 1, 1)
                laplace = x_plus + x_minus + y_plus + y_minus + z_plus + z_minus - 6.0 * center
                advect = 0.5 * (
                    centers[0] * (x_plus - x_minus)
                    + centers[1] * (y_plus - y_minus)
                    + centers[2] * (z_plus - z_minus)
                )
                store(
                    c, p, center + time_step * (viscosity * laplace - advect + forcing(c, p))
                )


def fluid(velocity, behind, ahead, grid, grid_behind, grid_ahead):
    return pl.pallas_call(
        fluid_kernel,
        out_shape=jax.ShapeDtypeStruct((3, CX, NY, NZ), f32),
        in_specs=[vmem()] * 6,
        out_specs=vmem(),
        scratch_shapes=[
            pltpu.VMEM((3, CX + 4, NY, NZ), f32),
            pltpu.VMEM((3, CX + 2, NY, NZ), f32),
        ],
        compiler_params=params(),
    )(velocity, behind, ahead, grid, grid_behind, grid_ahead)


def interpolate_kernel(field, got, out, rows_yx, table_high, table_low, offsets, sem):
    copy = pltpu.make_async_copy(got.at[:, :, pl.ds(12 * LANES, LANES)], offsets, sem)
    copy.start()
    lane = lax.broadcasted_iota(jnp.int32, (NY, LANES), 1)
    for a in range(CX):
        cells = jnp.where(lane < 32, field[0, a], 0.0)
        for c in (1, 2):
            moved = pltpu.roll(field[c, a], 32 * c, 1)
            cells = jnp.where((lane >= 32 * c) & (lane < 32 * c + 32), moved, cells)
        rows_yx[pl.ds(a, NY, stride=CX), :] = cells
    left = rows_yx[:LANES].T[:96]
    right = rows_yx[LANES:].T[:96]
    wide = lax.broadcasted_iota(jnp.int32, (96, LANES), 1)

    def rolled(values, shift):
        shift = shift % LANES
        return pltpu.roll(values, shift, 1) if shift else values

    for y in range(WINDOWS):
        shift = 8 * y
        if shift + 64 <= LANES:
            once, again = rolled(left, -shift), rolled(left, 64 - shift)
        elif shift >= LANES:
            once, again = rolled(right, LANES - shift), rolled(right, LANES + 64 - shift)
        else:
            edge = LANES - shift
            once = jnp.where(wide < edge, rolled(left, -shift), rolled(right, -shift))
            again = jnp.where(
                wide < 64 + edge, rolled(left, 64 - shift), rolled(right, 64 - shift)
            )
        high, low = split_2(jnp.where(wide < 64, once, again))
        table_high[y] = high.reshape(3, 32, LANES)
        table_low[y] = low.reshape(3, 32, LANES)
    copy.wait()

    def step(index, carry):
        for sub in range(UNROLL):
            device = index * UNROLL + sub
            for slot in range(2):
                stacked, weight_z = node_weights(got, device, slot)
                y, z = window(offsets, device, slot)
                cells = [table_high[y, c, pl.ds(z, 8), :] for c in range(3)]
                cells += [table_low[y, c, pl.ds(z, 8), :] for c in range(3)]
                values = dot(jnp.concatenate(cells, axis=0).astype(bf16), stacked, NN)
                values = values[:24] + values[24:]
                for c in range(3):
                    start = (slot * 3 + c) * LANES
                    out[device, :, start : start + LANES] = jnp.sum(
                        values[c * 8 : (c + 1) * 8] * weight_z, axis=0, keepdims=True
                    )
        return carry

    lax.fori_loop(0, LANES // UNROLL, step, 0)


def interpolate(field, got):
    return pl.pallas_call(
        interpolate_kernel,
        out_shape=jax.ShapeDtypeStruct((LANES, 1, 6 * LANES), f32),
        in_specs=[vmem()] * 2,
        out_specs=vmem(),
        scratch_shapes=[
            pltpu.VMEM((NY * CX, LANES), f32),
            pltpu.VMEM((WINDOWS, 3, 32, LANES), f32),
            pltpu.VMEM((WINDOWS, 3, 32, LANES), f32),
            pltpu.SMEM((LANES, 1, LANES), f32),
            pltpu.SemaphoreType.DMA,
        ],
        compiler_params=params(),
    )(field, got)


def pick_kernel(returned, back, out):
    chosen = back[...]
    for c in range(3):
        start = c * LANES
        both = jnp.concatenate(
            [
                returned[:, 0, start : start + LANES],
                returned[:, 0, 3 * LANES + start : 4 * LANES + start],
            ],
            axis=0,
        )
        high, middle, low = split_3(both)
        out[c] = dot(chosen, high, NN) + dot(chosen, middle, NN) + dot(chosen, low, NN)


def pick(returned, back):
    return pl.pallas_call(
        pick_kernel,
        out_shape=jax.ShapeDtypeStruct((3, LANES, LANES), f32),
        in_specs=[vmem()] * 2,
        out_specs=vmem(),
        compiler_params=params(),
    )(returned, back)


def exchange(values):
    return lax.all_to_all(values, "slab", split_axis=0, concat_axis=0, tiled=True)


def from_behind(values):
    count = lax.axis_size("slab")
    return lax.ppermute(values, "slab", [(i, (i + 1) % count) for i in range(count)])


def from_ahead(values):
    count = lax.axis_size("slab")
    return lax.ppermute(values, "slab", [((i + 1) % count, i) for i in range(count)])


def body(velocity, node_coords, node_force, block_slab, block_offset):
    sent, back = prep(
        jnp.transpose(node_coords, (1, 0, 2)),
        jnp.transpose(node_force, (1, 0, 2)),
        jnp.transpose(block_slab, (1, 0)),
        jnp.transpose(block_offset, (1, 0)),
    )
    got = exchange(sent)
    behind = from_behind(velocity[:, CX - 3 :])
    ahead = from_ahead(velocity[:, :3])
    grid = spread(got)
    grid_behind = from_behind(grid[CX - 2 :])
    grid_ahead = from_ahead(grid[:2])
    field = fluid(velocity, behind, ahead, grid, grid_behind, grid_ahead)
    returned = exchange(interpolate(field, got))
    node_velocity = pick(returned, back)
    return field, jnp.transpose(node_velocity, (1, 0, 2))


def solution(mesh):
    return jax.shard_map(
        body,
        mesh=mesh,
        in_specs=(
            P(None, "slab", None, None),
            P("slab", None, None),
            P("slab", None, None),
            P("slab", None),
            P("slab", None),
        ),
        out_specs=(P(None, "slab", None, None), P("slab", None, None)),
        check_vma=False,
    )
```

profile of v0, /device:TPU:1, one launch (start us, length us, event | category | flops | bytes accessed | tf_op | source)
XLA Modules:
  0.0 90.9 jit_solution(9468827982366335318)
XLA Ops:
  0.6 0.0 copy-start.4
  0.6 0.0 copy-start.5
  0.7 0.7 copy-done.4
  1.3 0.0 copy-done.5
  1.3 0.0 copy-start.2
  1.3 0.9 %copy-done.2 = f32[128,3,128]{2,0,1:T(8,128)S(1)} copy-done((f32[128,3,128]{2,0,1:T(8,128)S(1)}, f32[128,3,128]{2,0,1:T(8,128)}, u32[]{:S(2)}) %copy-start.2) | copy-done | bytes 196632
  2.2 0.0 copy-start.3
  2.2 0.9 %copy-done.3 = f32[128,3,128]{2,0,1:T(8,128)S(1)} copy-done((f32[128,3,128]{2,0,1:T(8,128)S(1)}, f32[128,3,128]{2,0,1:T(8,128)}, u32[]{:S(2)}) %copy-start.3) | copy-done | bytes 196632
  3.2 1.8 %shard_map.68 = (f32[128,1,1664]{2,1,0:T(1,128)}, bf16[128,256]{1,0:T(8,128)(2,1)S(1)}) custom-call(f32[3,128,128]{2,1,0:T(8,128)S(1)} %bitcast.5, f32[3,128,128]{2,1,0:T(8,128)S(1)} %bitcast.6, s32[1,128]{1,0:T(1,128)S(1)} %bitcast.8, s32[2,128]{1,0:T(2,128)S(1)} %bitcast.7), custom_call_target="tpu_custom_call" | custom-call | tf_op jit(solution)/shard_map/pallas_call | solution.py:106
  4.9 0.0 copy-start.1
  4.9 11.5 %all-to-all-start = ((f32[128,1,1664]{2,1,0:T(1,128)}), f32[128,1,1664]{2,1,0:T(1,128)S(1)}, u32[]{:S(2)}, u32[]{:S(2)}) async-start(f32[128,1,1664]{2,1,0:T(1,128)} %get-tuple-element.4), calls=%async_computation | async-start | bytes 1703936 | tf_op jit(solution)/shard_map/all_to_all | solution.py:372
  16.5 0.0 copy-done.1
  16.5 1.7 %collective-permute-start = (f32[3,3,32,128]{3,2,1,0:T(8,128)S(1)}, f32[3,3,32,128]{3,2,1,0:T(8,128)S(1)}, u32[]{:S(2)}, u32[]{:S(2)}) collective-permute-start(f32[3,3,32,128]{3,2,1,0:T(8,128)S(1)} %get-tuple-element.7), channel_id=1, source_target_pairs={{0,1},{1,2},{2,3},{3,4},{4,5},{5,6},{6,7},{7,8},{8,9},{9,10},{10,1... | collective-permute-start | bytes 442376 | tf_op jit(solution)/shard_map/ppermute | solution.py:377
  18.2 0.0 collective-permute-start.1
  18.2 15.4 %all-to-all-done.got = f32[128,1,1664]{2,1,0:T(1,128)S(1)} async-done(((f32[128,1,1664]{2,1,0:T(1,128)}), f32[128,1,1664]{2,1,0:T(1,128)S(1)}, u32[]{:S(2)}, u32[]{:S(2)}) %all-to-all-start) | async-done | bytes 852000 | tf_op jit(solution)/shard_map/all_to_all | solution.py:372
  33.6 13.6 %shard_map.69.grid = f32[8,32,128]{2,1,0:T(8,128)S(1)} custom-call(f32[128,1,1664]{2,1,0:T(1,128)S(1)} %all-to-all-done.got), custom_call_target="tpu_custom_call" | custom-call | tf_op jit(solution)/shard_map/pallas_call | solution.py:189
  47.2 1.5 %collective-permute-start.2 = (f32[2,32,128]{2,1,0:T(8,128)S(1)}, f32[2,32,128]{2,1,0:T(8,128)S(1)}, u32[]{:S(2)}, u32[]{:S(2)}) collective-permute-start(f32[2,32,128]{2,1,0:T(8,128)S(1)} %get-tuple-element.9), channel_id=1, source_target_pairs={{0,1},{1,2},{2,3},{3,4},{4,5},{5,6},{6,7},{7,8},{8,9},{9,10},{10,1... | collective-permute-start | bytes 98312 | tf_op jit(solution)/shard_map/ppermute | solution.py:377
  48.7 0.0 collective-permute-start.3
  48.7 0.0 collective-permute-done.behind
  48.7 0.0 collective-permute-done.1.ahead
  48.8 1.0 %collective-permute-done.2.grid_behind = f32[2,32,128]{2,1,0:T(8,128)S(1)} collective-permute-done((f32[2,32,128]{2,1,0:T(8,128)S(1)}, f32[2,32,128]{2,1,0:T(8,128)S(1)}, u32[]{:S(2)}, u32[]{:S(2)}) %collective-permute-start.2) | collective-permute-done | bytes 32800 | tf_op jit(solution)/shard_map/ppermute | solution.py:377
  49.8 2.3 %collective-permute-done.3.grid_ahead = f32[2,32,128]{2,1,0:T(8,128)S(1)} collective-permute-done((f32[2,32,128]{2,1,0:T(8,128)S(1)}, f32[2,32,128]{2,1,0:T(8,128)S(1)}, u32[]{:S(2)}, u32[]{:S(2)}) %collective-permute-start.3) | collective-permute-done | bytes 32800 | tf_op jit(solution)/shard_map/ppermute | solution.py:382
  52.1 2.0 %shard_map.70.field = f32[3,8,32,128]{3,2,1,0:T(8,128)} custom-call(f32[3,8,32,128]{3,2,1,0:T(8,128)S(1)} %copy-done.1, f32[3,3,32,128]{3,2,1,0:T(8,128)S(1)} %collective-permute-done.behind, f32[3,3,32,128]{3,2,1,0:T(8,128)S(1)} %collective-permute-done.1.ahead, f32[8,32,128]{2,1,0:T(8,128)S(1)} %shard_map.69.grid, ...), custom_call_target="tpu_custom_call" | custom-call | tf_op jit(solution)/shard_map/pallas_call | solution.py:261
  54.1 0.0 copy-start
  54.1 1.0 %copy-done = f32[3,8,32,128]{3,2,1,0:T(8,128)S(1)} copy-done((f32[3,8,32,128]{3,2,1,0:T(8,128)S(1)}, f32[3,8,32,128]{3,2,1,0:T(8,128)}, u32[]{:S(2)}) %copy-start) | copy-done | bytes 393240
  55.1 9.7 %shard_map.71 = f32[128,1,768]{2,1,0:T(1,128)S(1)} custom-call(f32[3,8,32,128]{3,2,1,0:T(8,128)S(1)} %copy-done, f32[128,1,1664]{2,1,0:T(1,128)S(1)} %all-to-all-done.got), custom_call_target="tpu_custom_call" | custom-call | tf_op jit(solution)/shard_map/pallas_call | solution.py:330
  64.8 25.0 %all_to_all.10.returned = f32[128,1,768]{2,1,0:T(1,128)S(1)} all-to-all(f32[128,1,768]{2,1,0:T(1,128)S(1)} %shard_map.71), channel_id=1, replica_groups=mesh['slab'=128] {'slab'}, dimensions={0} | all-to-all | bytes 786432 | tf_op jit(solution)/shard_map/all_to_all | solution.py:372
  89.8 1.1 %shard_map.72 = f32[3,128,128]{2,1,0:T(8,128)} custom-call(f32[128,1,768]{2,1,0:T(1,128)S(1)} %all_to_all.10.returned, bf16[128,256]{1,0:T(8,128)(2,1)S(1)} %get-tuple-element.5.back), custom_call_target="tpu_custom_call" | custom-call | tf_op jit(solution)/shard_map/pallas_call | solution.py:362
  (2 shorter events, 0.0 us)
Async XLA Ops:
  0.6 0.7 copy-start.4
  0.6 0.7 copy-start.5
  1.3 0.9 %copy-start.2 = (f32[128,3,128]{2,0,1:T(8,128)S(1)}, f32[128,3,128]{2,0,1:T(8,128)}, u32[]{:S(2)}) copy-start(f32[128,3,128]{2,0,1:T(8,128)} %param.6) | copy-start | bytes 589828
  2.2 0.9 %copy-start.3 = (f32[128,3,128]{2,0,1:T(8,128)S(1)}, f32[128,3,128]{2,0,1:T(8,128)}, u32[]{:S(2)}) copy-start(f32[128,3,128]{2,0,1:T(8,128)} %param.7) | copy-start | bytes 589828
  4.9 11.5 %copy-start.1 = (f32[3,8,32,128]{3,2,1,0:T(8,128)S(1)}, f32[3,8,32,128]{3,2,1,0:T(8,128)}, u32[]{:S(2)}) copy-start(f32[3,8,32,128]{3,2,1,0:T(8,128)} %velocity.1) | copy-start | bytes 1179652
  4.9 28.7 %all-to-all-start = ((f32[128,1,1664]{2,1,0:T(1,128)}), f32[128,1,1664]{2,1,0:T(1,128)S(1)}, u32[]{:S(2)}, u32[]{:S(2)}) async-start(f32[128,1,1664]{2,1,0:T(1,128)} %get-tuple-element.4), calls=%async_computation | async-start | bytes 1703936 | tf_op jit(solution)/shard_map/all_to_all | solution.py:372
  16.5 32.2 %collective-permute-start = (f32[3,3,32,128]{3,2,1,0:T(8,128)S(1)}, f32[3,3,32,128]{3,2,1,0:T(8,128)S(1)}, u32[]{:S(2)}, u32[]{:S(2)}) collective-permute-start(f32[3,3,32,128]{3,2,1,0:T(8,128)S(1)} %get-tuple-element.7), channel_id=1, source_target_pairs={{0,1},{1,2},{2,3},{3,4},{4,5},{5,6},{6,7},{7,8},{8,9},{9,10},{10,1... | collective-permute-start | bytes 442376 | tf_op jit(solution)/shard_map/ppermute | solution.py:377
  18.2 30.5 %collective-permute-start.1 = (f32[3,3,32,128]{3,2,1,0:T(8,128)S(1)}, f32[3,3,32,128]{3,2,1,0:T(8,128)S(1)}, u32[]{:S(2)}, u32[]{:S(2)}) collective-permute-start(f32[3,3,32,128]{3,2,1,0:T(8,128)S(1)} %get-tuple-element.6), channel_id=1, source_target_pairs={{1,0},{2,1},{3,2},{4,3},{5,4},{6,5},{7,6},{8,7},{9,8},{10,9},{11,1... | collective-permute-start | bytes 442376 | tf_op jit(solution)/shard_map/ppermute | solution.py:382
  47.2 2.5 %collective-permute-start.2 = (f32[2,32,128]{2,1,0:T(8,128)S(1)}, f32[2,32,128]{2,1,0:T(8,128)S(1)}, u32[]{:S(2)}, u32[]{:S(2)}) collective-permute-start(f32[2,32,128]{2,1,0:T(8,128)S(1)} %get-tuple-element.9), channel_id=1, source_target_pairs={{0,1},{1,2},{2,3},{3,4},{4,5},{5,6},{6,7},{7,8},{8,9},{9,10},{10,1... | collective-permute-start | bytes 98312 | tf_op jit(solution)/shard_map/ppermute | solution.py:377
  48.7 3.3 %collective-permute-start.3 = (f32[2,32,128]{2,1,0:T(8,128)S(1)}, f32[2,32,128]{2,1,0:T(8,128)S(1)}, u32[]{:S(2)}, u32[]{:S(2)}) collective-permute-start(f32[2,32,128]{2,1,0:T(8,128)S(1)} %get-tuple-element.8), channel_id=1, source_target_pairs={{1,0},{2,1},{3,2},{4,3},{5,4},{6,5},{7,6},{8,7},{9,8},{10,9},{11,1... | collective-permute-start | bytes 98312 | tf_op jit(solution)/shard_map/ppermute | solution.py:382
  54.1 1.0 %copy-start = (f32[3,8,32,128]{3,2,1,0:T(8,128)S(1)}, f32[3,8,32,128]{3,2,1,0:T(8,128)}, u32[]{:S(2)}) copy-start(f32[3,8,32,128]{3,2,1,0:T(8,128)} %shard_map.70.field) | copy-start | bytes 1179652
where the time goes:
time: 91.2 us; the launch traced here: 90.9 us
  Pallas kernels  28.2 us (31%)
  blocking collectives  25 us (27%)
  waiting for transfers between devices  18.7 us (21%)
  starting transfers between devices  14.7 us (16%)
  local copies, waits for them, and re-layouts  3.55 us (4%)
    all_to_all x1, blocking collectives, exchange(): lax.all_to_all(values, 'slab', split_axis=0, concat_axis=0, tiled=True)  25 us
    all_to_all x1, waiting for transfers between devices, exchange(): lax.all_to_all(values, 'slab', split_axis=0, concat_axis=0, tiled=True)  15.4 us
    pallas_call x1, Pallas kernels, spread(): pl.pallas_call(spread_kernel, out_shape=jax.ShapeDtypeStruct((CX, NY, LAN...  13.6 us
    all_to_all x1, starting transfers between devices, exchange(): lax.all_to_all(values, 'slab', split_axis=0, concat_axis=0, tiled=True)  11.5 us
    pallas_call x1, Pallas kernels, interpolate(): pl.pallas_call(interpolate_kernel, out_shape=jax.ShapeDtypeStruct((LANES,...  9.65 us
    unnamed x12, local copies, waits for them, and re-layouts  3.52 us
    ppermute x2, starting transfers between devices, from_behind(): lax.ppermute(values, 'slab', [(i, (i + 1) % count) for i in range(count)])  3.2 us
    ppermute x2, waiting for transfers between devices, from_ahead(): lax.ppermute(values, 'slab', [((i + 1) % count, i) for i in range(count)])  2.32 us
  transfers between devices with their start and end apart: 5, of which 3 were waited for; matrix products, arithmetic and copies ran while one was open for 0% of the time, Pallas kernels for 15%

commit v1 on v0

v1 whole, which is shorter than its diff:
```python
import jax
import jax.numpy as jnp
from jax import lax
from jax.experimental import pallas as pl
from jax.experimental.pallas import tpu as pltpu
from jax.sharding import PartitionSpec as P

CX = 8
NY = 32
NZ = 128
SUBSTEPS = 3
LANES = 128
WINDOWS = 25
SPREAD_UNROLL = 16
INNER_UNROLL = 8
EDGE_UNROLL = 16

time_step = 0.1
viscosity = 0.2

f32 = jnp.float32
bf16 = jnp.bfloat16

COS_TERMS = (
    0.7071067481276141,
    -0.21808909214261787,
    0.011209883548645258,
    -0.0002299265021950359,
    2.3703615380631122e-06,
)

VMEM_LIMIT = 24 * 1024 * 1024
VMEM_ALL = 60 * 1024 * 1024


def vmem():
    return pl.BlockSpec(memory_space=pltpu.VMEM)


def anywhere():
    return pl.BlockSpec(memory_space=pl.ANY)


def params(limit=VMEM_LIMIT):
    return pltpu.CompilerParams(vmem_limit_bytes=limit)


def phi(distance):
    t = jnp.minimum(distance * distance, 4.0)
    total = COS_TERMS[4] * t + COS_TERMS[3]
    for term in (COS_TERMS[2], COS_TERMS[1], COS_TERMS[0]):
        total = total * t + term
    return total * total


def split_2(values):
    high = values.astype(bf16).astype(f32)
    return high, values - high


def split_3(values):
    high = values.astype(bf16)
    rest = values - high.astype(f32)
    middle = rest.astype(bf16)
    low = (rest - middle.astype(f32)).astype(bf16)
    return high, middle, low


def dot(a, b, dims):
    return lax.dot_general(a, b, (dims, ((), ())), preferred_element_type=f32)


NN = ((1,), (0,))
NT = ((1,), (1,))


TABLE = WINDOWS * 96
EDGES = (0, 1, 6, 7)
MIDDLE = (2, 3, 4, 5)


def picks_kernel(out):
    source = lax.broadcasted_iota(jnp.int32, (2 * LANES, LANES), 0)
    lane = lax.broadcasted_iota(jnp.int32, (2 * LANES, LANES), 1)
    wanted = (lane >> 6) * 128 + ((lane >> 3) & 3) * 32 + (lane & 7)
    apart = source - wanted
    for start in range(WINDOWS):
        chosen = jnp.where(apart == start, 1.0, 0.0)
        out[:, start * LANES : (start + 1) * LANES] = chosen.astype(bf16)


def window_picks():
    return pl.pallas_call(
        picks_kernel,
        out_shape=jax.ShapeDtypeStruct((2 * LANES, WINDOWS * LANES), bf16),
        out_specs=vmem(),
        compiler_params=params(),
        cost_estimate=pl.CostEstimate(
            flops=2_000_000_000, bytes_accessed=2_000_000, transcendentals=0
        ),
    )()


def prep_kernel(coords_in, force_in, slab_in, offset_in, out, back, coords, force, slab, offset, sems):
    copies = [
        pltpu.make_async_copy(source, target, sems.at[i])
        for i, (source, target) in enumerate(
            ((slab_in, slab), (offset_in, offset), (coords_in, coords), (force_in, force))
        )
    ]
    for copy in copies:
        copy.start()
    row = lax.broadcasted_iota(jnp.int32, (LANES, LANES), 0)
    col = lax.broadcasted_iota(jnp.int32, (LANES, LANES), 1)
    before = (row < col).astype(f32).astype(bf16)
    copies[0].wait()
    hot = (jnp.broadcast_to(slab[...], (LANES, LANES)) == row).astype(f32)
    rank = dot(hot.astype(bf16), before, NN)
    first = jnp.where(rank < 0.5, hot, 0.0)
    second = hot - first
    both = jnp.concatenate([first, second], axis=0).astype(bf16)
    copies[1].wait()
    offsets = offset[...].astype(f32)
    rows = lax.broadcasted_iota(jnp.int32, (8, LANES), 0)
    spread_y = jnp.broadcast_to(offsets[0:1], (8, LANES))
    spread_z = jnp.broadcast_to(offsets[1:2], (8, LANES))
    tail = jnp.zeros((LANES, LANES), f32)
    empty = jnp.zeros((LANES - 8, LANES), f32)
    for slot, chosen in ((0, first), (1, second)):
        table = jnp.where(rows == 2 * slot, spread_y, 0.0) + jnp.where(
            rows == 2 * slot + 1, spread_z, 0.0
        )
        table = jnp.concatenate([table, empty], axis=0).astype(bf16)
        tail = tail + dot(chosen.astype(bf16), table, NT)
    out[:, 0, 12 * LANES :] = tail
    for quantity in range(6):
        source = coords if quantity < 3 else force
        if quantity % 3 == 0:
            copies[2 + quantity // 3].wait()
        high, middle, low = split_3(source[quantity % 3])
        placed = dot(both, high, NN) + dot(both, middle, NN) + dot(both, low, NN)
        for slot in range(2):
            start = (slot * 6 + quantity) * LANES
            out[:, 0, start : start + LANES] = placed[slot * LANES : (slot + 1) * LANES]
    back[:, :LANES] = first.T.astype(bf16)
    back[:, LANES:] = second.T.astype(bf16)


def prep(coords, force, slab, offset):
    return pl.pallas_call(
        prep_kernel,
        out_shape=(
            jax.ShapeDtypeStruct((LANES, 1, 13 * LANES), f32),
            jax.ShapeDtypeStruct((LANES, 2 * LANES), bf16),
        ),
        in_specs=[anywhere()] * 4,
        out_specs=(vmem(), vmem()),
        scratch_shapes=[
            pltpu.VMEM((3, LANES, LANES), f32),
            pltpu.VMEM((3, LANES, LANES), f32),
            pltpu.VMEM((1, LANES), jnp.int32),
            pltpu.VMEM((2, LANES), jnp.int32),
            pltpu.SemaphoreType.DMA((4,)),
        ],
        compiler_params=params(VMEM_ALL),
    )(coords, force, slab, offset)


def axis_weights(got, device, slot):
    taps = lax.broadcasted_iota(jnp.int32, (8, LANES), 0).astype(f32) - 1.0
    parts = []
    for dim, reach in ((0, CX - 4.0), (1, 5.0), (2, 5.0)):
        start = (slot * 6 + dim) * LANES
        place = got[device, :, start : start + LANES]
        parts.append(phi(taps - reach * place))
    return parts


def stack_2(values):
    high, low = split_2(values)
    return jnp.concatenate([high, low], axis=0).astype(bf16)


def spread_kernel(got, grid, near, far, rows_out, total, rows_yx, rows, sem):
    tail = got[:, 0, 12 * LANES :].T
    y = jnp.concatenate([tail[0:1], tail[2:3]], axis=0)
    z = jnp.concatenate([tail[1:2], tail[3:4]], axis=0)
    y = jnp.clip(y - 1.0, 0.0, WINDOWS - 1.0)
    z = jnp.clip(z - 1.0, 0.0, WINDOWS - 1.0)
    start = (y * 96.0 + z).astype(jnp.int32)
    rows_out[...] = jnp.concatenate([start, jnp.zeros((6, LANES), jnp.int32)], axis=0)
    copy = pltpu.make_async_copy(rows_out, rows, sem)
    copy.start()
    total[...] = jnp.zeros_like(total)
    copy.wait()

    def step(index, carry):
        pieces = []
        for sub in range(SPREAD_UNROLL):
            device = index * SPREAD_UNROLL + sub
            loads, stacks = [], []
            for slot in range(2):
                weight_x, weight_y, weight_z = axis_weights(got, device, slot)
                stacks.append(
                    stack_2(
                        jnp.concatenate([weight_y[i : i + 1] * weight_x for i in range(8)], axis=0)
                    )
                )
                parts = []
                for c in range(3):
                    start = (slot * 6 + 3 + c) * LANES
                    parts.append(got[device, :, start : start + LANES] * weight_z)
                loads.append(stack_2(jnp.concatenate(parts, axis=0)))
            out = dot(jnp.concatenate(loads, axis=0), jnp.concatenate(stacks, axis=0), NT)
            pieces.append((device, 0, out[:24, :LANES] + out[24:48, :LANES]))
            pieces.append((device, 1, out[48:72, LANES:] + out[72:, LANES:]))
        for device, slot, out in pieces:
            row = rows[slot, device]
            for c in range(3):
                total[pl.ds(row + 32 * c, 8), :] += out[c * 8 : (c + 1) * 8]
        return carry

    lax.fori_loop(0, LANES // SPREAD_UNROLL, step, 0)
    left = jnp.zeros((96, LANES), f32)
    right = jnp.zeros((96, LANES), f32)
    lane = lax.broadcasted_iota(jnp.int32, (96, LANES), 1)
    for y in range(WINDOWS):
        part = total[y * 96 : (y + 1) * 96]
        part = part + pltpu.roll(part, 64, 1)
        part = jnp.where(lane < 64, part, 0.0)
        shift = 8 * y % LANES
        moved = pltpu.roll(part, shift, 1) if shift else part
        if 8 * y >= LANES:
            right = right + moved
        elif 8 * y + 64 <= LANES:
            left = left + moved
        else:
            left = left + jnp.where(lane >= shift, moved, 0.0)
            right = right + jnp.where(lane < shift, moved, 0.0)
    pad = jnp.zeros((32, LANES), f32)
    rows_yx[:LANES] = jnp.concatenate([left, pad], axis=0).T
    rows_yx[LANES:] = jnp.concatenate([right, pad], axis=0).T
    planes = [rows_yx[pl.ds(a, NY, stride=CX), :] for a in range(CX)]
    odd = lax.axis_index("slab") % 2 == 1
    for a in range(CX):
        grid[a] = planes[a]
    for a in range(2):
        near[a] = jnp.where(odd, planes[a], planes[CX - 2 + a])
        far[a] = jnp.where(odd, planes[CX - 2 + a], planes[a])


def spread(got):
    return pl.pallas_call(
        spread_kernel,
        out_shape=(
            jax.ShapeDtypeStruct((CX, NY, LANES), f32),
            jax.ShapeDtypeStruct((2, NY, LANES), f32),
            jax.ShapeDtypeStruct((2, NY, LANES), f32),
            jax.ShapeDtypeStruct((8, LANES), jnp.int32),
        ),
        in_specs=[vmem()],
        out_specs=(vmem(),) * 4,
        scratch_shapes=[
            pltpu.VMEM((TABLE, LANES), f32),
            pltpu.VMEM((NY * CX, LANES), f32),
            pltpu.SMEM((8, LANES), jnp.int32),
            pltpu.SemaphoreType.DMA,
        ],
        compiler_params=params(),
    )(got)


def forcing_of(cells, c):
    lane = lax.broadcasted_iota(jnp.int32, (NY, NZ), 1)
    if c:
        cells = pltpu.roll(cells, LANES - 32 * c, 1)
    return jnp.where(lane < 32, cells, 0.0)


def fluid_plane(load, cells, p):
    centers = [load(c, p) for c in range(3)]
    results = []
    for c in range(3):
        center = centers[c]
        x_plus, x_minus = load(c, p + 1), load(c, p - 1)
        y_plus, y_minus = pltpu.roll(center, NY - 1, 0), pltpu.roll(center, 1, 0)
        z_plus, z_minus = pltpu.roll(center, NZ - 1, 1), pltpu.roll(center, 1, 1)
        laplace = x_plus + x_minus + y_plus + y_minus + z_plus + z_minus - 6.0 * center
        advect = 0.5 * (
            centers[0] * (x_plus - x_minus)
            + centers[1] * (y_plus - y_minus)
            + centers[2] * (z_plus - z_minus)
        )
        results.append(
            center + time_step * (viscosity * laplace - advect + forcing_of(cells, c))
        )
    return results


def packed_plane(parts):
    lane = lax.broadcasted_iota(jnp.int32, (NY, LANES), 1)
    cells = jnp.where(lane < 32, parts[0], 0.0)
    for c in (1, 2):
        moved = pltpu.roll(parts[c], 32 * c, 1)
        cells = jnp.where((lane >= 32 * c) & (lane < 32 * c + 32), moved, cells)
    return cells


def fill_table(table, planes, picks):
    cells = jnp.concatenate([packed_plane(parts) for parts in planes], axis=0).T[:96]
    high, low = split_2(cells)
    split = jnp.concatenate([high, low], axis=1).astype(bf16)
    for y in range(0, WINDOWS, 2):
        wide = min(2, WINDOWS - y)
        both = dot(split, picks[:, y * LANES : (y + wide) * LANES], NN)
        for i in range(wide):
            table[(y + i) * 96 : (y + i + 1) * 96] = both[:, i * LANES : (i + 1) * LANES]


def window_sums(table, rows, device, weights, weights_z):
    cells = []
    for slot in range(2):
        row = rows[slot, device]
        for c in range(3):
            cells.append(table[pl.ds(row + 32 * c, 8), :])
    values = dot(jnp.concatenate(cells, axis=0).astype(bf16), weights, NN)
    sums = []
    for slot in range(2):
        for c in range(3):
            start = slot * 24 + c * 8
            part = values[start : start + 8, slot * LANES : (slot + 1) * LANES]
            sums.append(jnp.sum(part * weights_z[slot], axis=0, keepdims=True))
    return sums


def halo_reader(inside, same, cross, depth):
    odd = lax.axis_index("slab") % 2 == 1

    def load(c, p):
        if p < 0:
            return jnp.where(odd, same[c, p + depth], cross[c, p + depth])
        if p >= CX:
            return jnp.where(odd, cross[c, p - CX], same[c, p - CX])
        return inside[c, p]

    return load


def inner_kernel(
    velocity, same, cross, grid, got, rows_in, picks,
    step_1, step_2, middle, edge_weights, z_weights, partial, table, rows, sem
):
    copy = pltpu.make_async_copy(rows_in, rows, sem)
    copy.start()
    load_0 = halo_reader(velocity, same, cross, SUBSTEPS)
    for p in range(CX):
        for c, value in enumerate(fluid_plane(load_0, grid[p], p)):
            step_1[c, p] = value
    for p in range(1, CX - 1):
        for c, value in enumerate(fluid_plane(lambda c, p: step_1[c, p], grid[p], p)):
            step_2[c, p] = value
    planes = []
    for p in MIDDLE:
        planes.append(fluid_plane(lambda c, p: step_2[c, p], grid[p], p))
        for c in range(3):
            middle[c, p - MIDDLE[0]] = planes[-1][c]
    fill_table(table, planes, picks)
    copy.wait()

    def step(index, carry):
        for sub in range(INNER_UNROLL):
            device = index * INNER_UNROLL + sub
            weights, weights_z = [], []
            for slot in range(2):
                weight_x, weight_y, weight_z = axis_weights(got, device, slot)
                weights.append(
                    stack_2(
                        jnp.concatenate([weight_x[a : a + 1] * weight_y for a in MIDDLE], axis=0)
                    )
                )
                edge_weights[device, :, slot * LANES : (slot + 1) * LANES] = stack_2(
                    jnp.concatenate([weight_x[a : a + 1] * weight_y for a in EDGES], axis=0)
                )
                z_weights[device, :, slot * LANES : (slot + 1) * LANES] = weight_z
                weights_z.append(weight_z)
            both = jnp.concatenate(weights, axis=1)
            sums = window_sums(
                table, rows, device, jnp.concatenate([both, both], axis=0), weights_z
            )
            for i in range(6):
                partial[device, :, i * LANES : (i + 1) * LANES] = sums[i]
        return carry

    lax.fori_loop(0, LANES // INNER_UNROLL, step, 0)


def inner(velocity, same, cross, grid, got, rows, picks):
    return pl.pallas_call(
        inner_kernel,
        out_shape=(
            jax.ShapeDtypeStruct((3, CX, NY, NZ), f32),
            jax.ShapeDtypeStruct((3, CX, NY, NZ), f32),
            jax.ShapeDtypeStruct((3, len(MIDDLE), NY, NZ), f32),
            jax.ShapeDtypeStruct((LANES, 64, 2 * LANES), bf16),
            jax.ShapeDtypeStruct((LANES, 8, 2 * LANES), f32),
            jax.ShapeDtypeStruct((LANES, 1, 6 * LANES), f32),
        ),
        in_specs=[vmem()] * 7,
        out_specs=(vmem(),) * 6,
        scratch_shapes=[
            pltpu.VMEM((TABLE, LANES), f32),
            pltpu.SMEM((8, LANES), jnp.int32),
            pltpu.SemaphoreType.DMA,
        ],
        compiler_params=params(),
        cost_estimate=pl.CostEstimate(
            flops=6_000_000_000, bytes_accessed=8_000_000, transcendentals=0
        ),
    )(velocity, same, cross, grid, got, rows, picks)


def edge_kernel(
    velocity, same, cross, grid, near, far, rows_in, picks,
    step_1, step_2, middle, edge_weights, z_weights, partial,
    field, out, ends_1, ends_2, ends_3, table, rows, sems
):
    copies = [pltpu.make_async_copy(rows_in, rows, sems.at[0])]
    copies.append(
        pltpu.make_async_copy(middle, field.at[:, pl.ds(MIDDLE[0], len(MIDDLE))], sems.at[1])
    )
    for i, p in enumerate((0, CX - 2)):
        copies.append(
            pltpu.make_async_copy(ends_3.at[:, pl.ds(2 * i, 2)], field.at[:, pl.ds(p, 2)], sems.at[2 + i])
        )
    copies[0].start()
    copies[1].start()
    odd = lax.axis_index("slab") % 2 == 1

    def cells(p):
        if p < 0:
            return jnp.where(odd, near[p + 2], far[p + 2])
        if p >= CX:
            return jnp.where(odd, far[p - CX], near[p - CX])
        return grid[p]

    def reader(ends, inside, low):
        def load(c, p):
            for i, q in enumerate(low):
                if p == q:
                    return ends[c, i]
            return inside[c, p]

        return load

    planes_1 = (-2, -1, CX, CX + 1)
    planes_2 = (-1, 0, CX - 1, CX)
    load_0 = halo_reader(velocity, same, cross, SUBSTEPS)
    for i, p in enumerate(planes_1):
        for c, value in enumerate(fluid_plane(load_0, cells(p), p)):
            ends_1[c, i] = value
    load_1 = reader(ends_1, step_1, planes_1)
    for i, p in enumerate(planes_2):
        for c, value in enumerate(fluid_plane(load_1, cells(p), p)):
            ends_2[c, i] = value
    load_2 = reader(ends_2, step_2, planes_2)
    planes = []
    for i, p in enumerate(EDGES):
        planes.append(fluid_plane(load_2, cells(p), p))
        for c in range(3):
            ends_3[c, i] = planes[-1][c]
    copies[2].start()
    copies[3].start()
    fill_table(table, planes, picks)
    copies[0].wait()

    def step(index, carry):
        for sub in range(EDGE_UNROLL):
            device = index * EDGE_UNROLL + sub
            both = edge_weights[device]
            weights_z = [
                z_weights[device, :, slot * LANES : (slot + 1) * LANES] for slot in range(2)
            ]
            sums = window_sums(
                table, rows, device, jnp.concatenate([both, both], axis=0), weights_z
            )
            for i in range(6):
                lanes = slice(i * LANES, (i + 1) * LANES)
                out[device, :, lanes] = partial[device, :, lanes] + sums[i]
        return carry

    lax.fori_loop(0, LANES // EDGE_UNROLL, step, 0)
    for copy in copies[1:]:
        copy.wait()


def edge(*arguments):
    return pl.pallas_call(
        edge_kernel,
        out_shape=(
            jax.ShapeDtypeStruct((3, CX, NY, NZ), f32),
            jax.ShapeDtypeStruct((LANES, 1, 6 * LANES), f32),
        ),
        in_specs=[vmem()] * 14,
        out_specs=(anywhere(), vmem()),
        scratch_shapes=[
            pltpu.VMEM((3, 4, NY, NZ), f32),
            pltpu.VMEM((3, 4, NY, NZ), f32),
            pltpu.VMEM((3, 4, NY, NZ), f32),
            pltpu.VMEM((TABLE, LANES), f32),
            pltpu.SMEM((8, LANES), jnp.int32),
            pltpu.SemaphoreType.DMA((4,)),
        ],
        compiler_params=params(),
    )(*arguments)


def pick_kernel(returned, back, out):
    chosen = back[...]
    for c in range(3):
        start = c * LANES
        both = jnp.concatenate(
            [
                returned[:, 0, start : start + LANES],
                returned[:, 0, 3 * LANES + start : 4 * LANES + start],
            ],
            axis=0,
        )
        high, middle, low = split_3(both)
        out[c] = dot(chosen, high, NN) + dot(chosen, middle, NN) + dot(chosen, low, NN)


def pick(returned, back):
    return pl.pallas_call(
        pick_kernel,
        out_shape=jax.ShapeDtypeStruct((3, LANES, LANES), f32),
        in_specs=[vmem()] * 2,
        out_specs=vmem(),
        compiler_params=params(),
    )(returned, back)


def exchange(values):
    return lax.all_to_all(values, "slab", split_axis=0, concat_axis=0, tiled=True)


def swap(values, first):
    count = lax.axis_size("slab")
    pairs = []
    for i in range(first, count + first, 2):
        a, b = i % count, (i + 1) % count
        pairs += [(a, b), (b, a)]
    return lax.ppermute(values, "slab", pairs)


def body(velocity, node_coords, node_force, block_slab, block_offset):
    picks = window_picks()
    sent, back = prep(
        jnp.transpose(node_coords, (1, 0, 2)),
        jnp.transpose(node_force, (1, 0, 2)),
        jnp.transpose(block_slab, (1, 0)),
        jnp.transpose(block_offset, (1, 0)),
    )
    got = exchange(sent)
    odd = lax.axis_index("slab") % 2 == 1
    first, last = velocity[:, :SUBSTEPS], velocity[:, CX - SUBSTEPS :]
    cross = swap(jnp.where(odd, last, first), 1)
    same = swap(jnp.where(odd, first, last), 0)
    grid, near, far, rows = spread(got)
    far = swap(far, 1)
    near = swap(near, 0)
    inside = inner(velocity, same, cross, grid, got, rows, picks)
    field, sums = edge(velocity, same, cross, grid, near, far, rows, picks, *inside)
    node_velocity = pick(exchange(sums), back)
    return field, jnp.transpose(node_velocity, (1, 0, 2))


def solution(mesh):
    return jax.shard_map(
        body,
        mesh=mesh,
        in_specs=(
            P(None, "slab", None, None),
            P("slab", None, None),
            P("slab", None, None),
            P("slab", None),
            P("slab", None),
        ),
        out_specs=(P(None, "slab", None, None), P("slab", None, None)),
        check_vma=False,
    )
```

time: 91.2 us -> 72.2 us (0.79)
  waiting for transfers between devices: 18.7 us -> 7.48 us
  starting transfers between devices: 14.7 us -> 21.3 us
  Pallas kernels: 28.2 us -> 21.8 us
  blocking collectives: 25 us -> 19.6 us
  local copies, waits for them, and re-layouts: 3.55 us -> 0.01 us
  other arithmetic: 0 us -> 1.01 us
    all_to_all x1, waiting for transfers between devices: 15.4 us -> 7.47 us  [exchange(): lax.all_to_all(values, 'slab', split_axis=0, concat_axis=0, tiled=True)]
    pallas_call x3 -> x4, Pallas kernels: 25.3 us -> 17.9 us  [the longest x1 7.44 us: spread(): pl.pallas_call(spread_kernel, out_shape=(jax.ShapeDtypeStruct((CX, NY, LA...]
    ppermute x4, starting transfers between devices: 3.21 us -> 9.8 us  [swap(): return lax.ppermute(values, 'slab', pairs)]
    all_to_all x1, blocking collectives: 25 us -> 19.6 us  [exchange(): lax.all_to_all(values, 'slab', split_axis=0, concat_axis=0, tiled=True)]
    unnamed x12 -> x4, local copies, waits for them, and re-layouts: 3.52 us -> 0.01 us
    ppermute x4, waiting for transfers between devices: 3.33 us -> 0.01 us  [swap(): return lax.ppermute(values, 'slab', pairs)]
    pallas_call x1, Pallas kernels: 1.78 us -> 2.83 us  [prep(): pl.pallas_call(prep_kernel, out_shape=(jax.ShapeDtypeStruct((LANES, 1, 13...]
    select_n x0 -> x1, other arithmetic: none -> 1.01 us  [body(): cross = swap(jnp.where(odd, last, first), 1)]
  transfers between devices with their start and end apart: 5 -> 5, of which waited for: 3 -> 1; matrix products, arithmetic and copies ran while one was open for 0% -> 1% of each run, Pallas kernels for 15% -> 20%
where the time goes in v1:
time: 72.2 us; the launch traced here: 72 us
  Pallas kernels  21.8 us (30%)
  starting transfers between devices  21.3 us (30%)
  blocking collectives  19.6 us (27%)
  waiting for transfers between devices  7.48 us (10%)
  other arithmetic  1.01 us (1%)
  between operations  0.73 us (1%)
    all_to_all x1, blocking collectives, exchange(): lax.all_to_all(values, 'slab', split_axis=0, concat_axis=0, tiled=True)  19.6 us
    all_to_all x1, starting transfers between devices, exchange(): lax.all_to_all(values, 'slab', split_axis=0, concat_axis=0, tiled=True)  11.5 us
    ppermute x4, starting transfers between devices, swap(): return lax.ppermute(values, 'slab', pairs)  9.8 us
    all_to_all x1, waiting for transfers between devices, exchange(): lax.all_to_all(values, 'slab', split_axis=0, concat_axis=0, tiled=True)  7.47 us
    pallas_call x1, Pallas kernels, spread(): pl.pallas_call(spread_kernel, out_shape=(jax.ShapeDtypeStruct((CX, NY, LA...  7.44 us
    pallas_call x1, Pallas kernels, inner(): pl.pallas_call(inner_kernel, out_shape=(jax.ShapeDtypeStruct((3, CX, NY,...  6.47 us
    pallas_call x1, Pallas kernels, edge(): pl.pallas_call(edge_kernel, out_shape=(jax.ShapeDtypeStruct((3, CX, NY, N...  3.51 us
    pallas_call x1, Pallas kernels, prep(): pl.pallas_call(prep_kernel, out_shape=(jax.ShapeDtypeStruct((LANES, 1, 13...  2.83 us
  transfers between devices with their start and end apart: 5, of which 1 were waited for; matrix products, arithmetic and copies ran while one was open for 1% of the time, Pallas kernels for 20%

profile of v1, /device:TPU:1, one launch (start us, length us, event | category | flops | bytes accessed | tf_op | source)
XLA Modules:
  0.0 72.0 jit_solution(10879455874359739408)
XLA Ops:
  0.6 2.8 %shard_map.68 = (f32[128,1,1664]{2,1,0:T(1,128)}, bf16[128,256]{1,0:T(8,128)(2,1)}) custom-call(f32[3,128,128]{2,1,0:T(8,128)} %bitcast.5, f32[3,128,128]{2,1,0:T(8,128)} %bitcast.6, s32[1,128]{1,0:T(1,128)} %bitcast.9, s32[2,128]{1,0:T(2,128)} %bitcast.8), custom_call_target="tpu_custom_call" | custom-call | tf_op jit(solution)/shard_map/pallas_call | solution.py:150
  3.5 11.5 %all-to-all-start = ((f32[128,1,1664]{2,1,0:T(1,128)}), f32[128,1,1664]{2,1,0:T(1,128)S(1)}, u32[]{:S(2)}, u32[]{:S(2)}) async-start(f32[128,1,1664]{2,1,0:T(1,128)} %get-tuple-element.16), calls=%async_computation | async-start | bytes 1703936 | tf_op jit(solution)/shard_map/all_to_all | solution.py:543
  15.0 1.0 %slice_select_fusion = (f32[3,3,32,128]{3,2,1,0:T(8,128)S(1)}, f32[3,3,32,128]{3,2,1,0:T(8,128)S(1)}) fusion(f32[3,8,32,128]{3,2,1,0:T(8,128)} %velocity.3, pred[]{:T(512)S(6)} %eq.5), kind=kLoop, calls=%fused_computation | loop fusion | flops 73728 | bytes 589825 | tf_op jit(solution)/shard_map/jit(_where)/select_n | solution.py:566
  16.0 0.0 copy-start
  16.0 1.7 %collective-permute-start.1 = (f32[3,3,32,128]{3,2,1,0:T(8,128)S(1)}, f32[3,3,32,128]{3,2,1,0:T(8,128)S(1)}, u32[]{:S(2)}, u32[]{:S(2)}) collective-permute-start(f32[3,3,32,128]{3,2,1,0:T(8,128)S(1)} %get-tuple-element.30), channel_id=1, source_target_pairs={{1,2},{2,1},{3,4},{4,3},{5,6},{6,5},{7,8},{8,7},{9,10},{10,9},{11,... | collective-permute-start | bytes 442376 | tf_op jit(solution)/shard_map/ppermute | solution.py:552
  17.7 6.5 %collective-permute-start = (f32[3,3,32,128]{3,2,1,0:T(8,128)S(1)}, f32[3,3,32,128]{3,2,1,0:T(8,128)S(1)}, u32[]{:S(2)}, u32[]{:S(2)}) collective-permute-start(f32[3,3,32,128]{3,2,1,0:T(8,128)S(1)} %get-tuple-element.31), channel_id=1, source_target_pairs={{0,1},{1,0},{2,3},{3,2},{4,5},{5,4},{6,7},{7,6},{8,9},{9,8},{10,11... | collective-permute-start | bytes 442376 | tf_op jit(solution)/shard_map/ppermute | solution.py:552
  24.2 0.4 shard_map.70.picks
  24.7 7.5 %all-to-all-done.got = f32[128,1,1664]{2,1,0:T(1,128)S(1)} async-done(((f32[128,1,1664]{2,1,0:T(1,128)}), f32[128,1,1664]{2,1,0:T(1,128)S(1)}, u32[]{:S(2)}, u32[]{:S(2)}) %all-to-all-start) | async-done | bytes 852000 | tf_op jit(solution)/shard_map/all_to_all | solution.py:543
  32.1 7.4 %shard_map.69 = (f32[8,32,128]{2,1,0:T(8,128)S(1)}, f32[2,32,128]{2,1,0:T(8,128)S(1)}, f32[2,32,128]{2,1,0:T(8,128)S(1)}, s32[8,128]{1,0:T(8,128)S(1)}) custom-call(f32[128,1,1664]{2,1,0:T(1,128)S(1)} %all-to-all-done.got), custom_call_target="tpu_custom_call" | custom-call | tf_op jit(solution)/shard_map/pallas_call | solution.py:253
  39.6 1.1 %collective-permute-start.2 = (f32[2,32,128]{2,1,0:T(8,128)S(1)}, f32[2,32,128]{2,1,0:T(8,128)S(1)}, u32[]{:S(2)}, u32[]{:S(2)}) collective-permute-start(f32[2,32,128]{2,1,0:T(8,128)S(1)} %get-tuple-element.18), channel_id=1, source_target_pairs={{0,1},{1,0},{2,3},{3,2},{4,5},{5,4},{6,7},{7,6},{8,9},{9,8},{10,11... | collective-permute-start | bytes 98312 | tf_op jit(solution)/shard_map/ppermute | solution.py:552
  40.7 0.5 collective-permute-start.3
  41.2 0.0 collective-permute-done.1.cross
  41.2 0.0 collective-permute-done.same
  41.2 0.0 copy-done
  41.2 6.5 %shard_map.71 = (f32[3,8,32,128]{3,2,1,0:T(8,128)S(1)}, f32[3,8,32,128]{3,2,1,0:T(8,128)S(1)}, f32[3,4,32,128]{3,2,1,0:T(8,128)S(1)}, bf16[128,64,256]{2,1,0:T(8...) custom-call(f32[3,8,32,128]{3,2,1,0:T(8,128)S(1)} %copy-done, ...), custom_call_target="tpu_custom_call" | custom-call | flops 6000000000 | bytes 8000000 | tf_op jit(solution)/shard_map/pallas_call | solution.py:398
  47.7 0.0 collective-permute-done.2.near
  47.7 0.0 collective-permute-done.3.far
  47.7 0.0 copy-start.1
  47.7 3.5 %shard_map.72 = (f32[3,8,32,128]{3,2,1,0:T(8,128)}, f32[128,1,768]{2,1,0:T(1,128)S(1)}) custom-call(f32[3,8,32,128]{3,2,1,0:T(8,128)S(1)} %copy-done, f32[3,3,32,128]{3,2,1,0:T(8,128)S(1)} %collective-permute-done.same, f32[3,3,32,128]{3,2,1,0:T(8,128)S(1)} %collective-permute-done.1.cross, f32[8,32,128]{2,1,0:T(8,128)S(1)} %get-tuple-element.17.grid, ...), custom_call_target="tpu_custom_call" | custom-call | tf_op jit(solution)/shard_map/pallas_call | solution.py:497
  51.2 19.6 %all_to_all.10.returned = f32[128,1,768]{2,1,0:T(1,128)S(1)} all-to-all(f32[128,1,768]{2,1,0:T(1,128)S(1)} %get-tuple-element.28), channel_id=1, replica_groups=mesh['slab'=128] {'slab'}, dimensions={0} | all-to-all | bytes 786432 | tf_op jit(solution)/shard_map/all_to_all | solution.py:543
  70.8 0.0 copy-done.1
  70.9 1.1 %shard_map.73 = f32[3,128,128]{2,1,0:T(8,128)} custom-call(f32[128,1,768]{2,1,0:T(1,128)S(1)} %all_to_all.10.returned, bf16[128,256]{1,0:T(8,128)(2,1)S(1)} %copy-done.1), custom_call_target="tpu_custom_call" | custom-call | tf_op jit(solution)/shard_map/pallas_call | solution.py:533
Async XLA Ops:
  3.5 28.7 %all-to-all-start = ((f32[128,1,1664]{2,1,0:T(1,128)}), f32[128,1,1664]{2,1,0:T(1,128)S(1)}, u32[]{:S(2)}, u32[]{:S(2)}) async-start(f32[128,1,1664]{2,1,0:T(1,128)} %get-tuple-element.16), calls=%async_computation | async-start | bytes 1703936 | tf_op jit(solution)/shard_map/all_to_all | solution.py:543
  16.0 25.2 %copy-start = (f32[3,8,32,128]{3,2,1,0:T(8,128)S(1)}, f32[3,8,32,128]{3,2,1,0:T(8,128)}, u32[]{:S(2)}) copy-start(f32[3,8,32,128]{3,2,1,0:T(8,128)} %velocity.3) | copy-start | bytes 1179652
  16.0 25.2 %collective-permute-start.1 = (f32[3,3,32,128]{3,2,1,0:T(8,128)S(1)}, f32[3,3,32,128]{3,2,1,0:T(8,128)S(1)}, u32[]{:S(2)}, u32[]{:S(2)}) collective-permute-start(f32[3,3,32,128]{3,2,1,0:T(8,128)S(1)} %get-tuple-element.30), channel_id=1, source_target_pairs={{1,2},{2,1},{3,4},{4,3},{5,6},{6,5},{7,8},{8,7},{9,10},{10,9},{11,... | collective-permute-start | bytes 442376 | tf_op jit(solution)/shard_map/ppermute | solution.py:552
  17.7 23.4 %collective-permute-start = (f32[3,3,32,128]{3,2,1,0:T(8,128)S(1)}, f32[3,3,32,128]{3,2,1,0:T(8,128)S(1)}, u32[]{:S(2)}, u32[]{:S(2)}) collective-permute-start(f32[3,3,32,128]{3,2,1,0:T(8,128)S(1)} %get-tuple-element.31), channel_id=1, source_target_pairs={{0,1},{1,0},{2,3},{3,2},{4,5},{5,4},{6,7},{7,6},{8,9},{9,8},{10,11... | collective-permute-start | bytes 442376 | tf_op jit(solution)/shard_map/ppermute | solution.py:552
  39.6 8.1 %collective-permute-start.2 = (f32[2,32,128]{2,1,0:T(8,128)S(1)}, f32[2,32,128]{2,1,0:T(8,128)S(1)}, u32[]{:S(2)}, u32[]{:S(2)}) collective-permute-start(f32[2,32,128]{2,1,0:T(8,128)S(1)} %get-tuple-element.18), channel_id=1, source_target_pairs={{0,1},{1,0},{2,3},{3,2},{4,5},{5,4},{6,7},{7,6},{8,9},{9,8},{10,11... | collective-permute-start | bytes 98312 | tf_op jit(solution)/shard_map/ppermute | solution.py:552
  40.7 7.0 %collective-permute-start.3 = (f32[2,32,128]{2,1,0:T(8,128)S(1)}, f32[2,32,128]{2,1,0:T(8,128)S(1)}, u32[]{:S(2)}, u32[]{:S(2)}) collective-permute-start(f32[2,32,128]{2,1,0:T(8,128)S(1)} %get-tuple-element.19), channel_id=1, source_target_pairs={{1,2},{2,1},{3,4},{4,3},{5,6},{6,5},{7,8},{8,7},{9,10},{10,9},{11,... | collective-permute-start | bytes 98312 | tf_op jit(solution)/shard_map/ppermute | solution.py:552
  47.7 23.2 %copy-start.1 = (bf16[128,256]{1,0:T(8,128)(2,1)S(1)}, bf16[128,256]{1,0:T(8,128)(2,1)}, u32[]{:S(2)}) copy-start(bf16[128,256]{1,0:T(8,128)(2,1)} %get-tuple-element.29.back) | copy-start | bytes 196612

commit v2 on v1

v2 whole, which is shorter than its diff:
```python
import jax
import jax.numpy as jnp
from jax import lax
from jax.experimental import pallas as pl
from jax.experimental.pallas import tpu as pltpu
from jax.sharding import PartitionSpec as P

CX = 8
NY = 32
NZ = 128
SUBSTEPS = 3
LANES = 128
WINDOWS = 25
SPREAD_UNROLL = 32
MIDDLE_UNROLL = 32
INNER_UNROLL = 32
EDGE_UNROLL = 32

time_step = 0.1
viscosity = 0.2

f32 = jnp.float32
bf16 = jnp.bfloat16

COS_TERMS = (
    0.7071067481276141,
    -0.21808909214261787,
    0.011209883548645258,
    -0.0002299265021950359,
    2.3703615380631122e-06,
)

VMEM_LIMIT = 24 * 1024 * 1024
VMEM_ALL = 60 * 1024 * 1024


def vmem():
    return pl.BlockSpec(memory_space=pltpu.VMEM)


def anywhere():
    return pl.BlockSpec(memory_space=pl.ANY)


def params(limit=VMEM_LIMIT):
    return pltpu.CompilerParams(vmem_limit_bytes=limit)


def phi(distance):
    t = jnp.minimum(distance * distance, 4.0)
    total = COS_TERMS[4] * t + COS_TERMS[3]
    for term in (COS_TERMS[2], COS_TERMS[1], COS_TERMS[0]):
        total = total * t + term
    return total * total


def split_2(values):
    high = values.astype(bf16).astype(f32)
    return high, values - high


def split_3(values):
    high = values.astype(bf16)
    rest = values - high.astype(f32)
    middle = rest.astype(bf16)
    low = (rest - middle.astype(f32)).astype(bf16)
    return high, middle, low


def dot(a, b, dims):
    return lax.dot_general(a, b, (dims, ((), ())), preferred_element_type=f32)


NN = ((1,), (0,))
NT = ((1,), (1,))


TABLE = WINDOWS * 96
EDGES = (0, 1, 6, 7)
MIDDLE = (2, 3, 4, 5)
SENT = 13
REACH = (CX - 4.0, 5.0, 5.0)


def picks_kernel(out):
    source = lax.broadcasted_iota(jnp.int32, (LANES, LANES), 0)
    lane = lax.broadcasted_iota(jnp.int32, (LANES, LANES), 1)
    apart = source - ((lane >> 3) & 3) * 32 - (lane & 7)
    for start in range(WINDOWS):
        chosen = jnp.where(apart == start, 1.0, 0.0)
        out[:, start * LANES : (start + 1) * LANES] = chosen.astype(bf16)


def window_picks():
    return pl.pallas_call(
        picks_kernel,
        out_shape=jax.ShapeDtypeStruct((LANES, WINDOWS * LANES), bf16),
        out_specs=vmem(),
        compiler_params=params(),
        cost_estimate=pl.CostEstimate(
            flops=2_000_000_000, bytes_accessed=2_000_000, transcendentals=0
        ),
    )()


def prep_kernel(coords_in, force_in, slab_in, offset_in, out, back, coords, force, slab, offset, sems):
    copies = [
        pltpu.make_async_copy(source, target, sems.at[i])
        for i, (source, target) in enumerate(
            ((slab_in, slab), (offset_in, offset), (coords_in, coords), (force_in, force))
        )
    ]
    for copy in copies:
        copy.start()
    row = lax.broadcasted_iota(jnp.int32, (LANES, LANES), 0)
    col = lax.broadcasted_iota(jnp.int32, (LANES, LANES), 1)
    before = (row < col).astype(f32).astype(bf16)
    copies[0].wait()
    hot = (jnp.broadcast_to(slab[...], (LANES, LANES)) == row).astype(f32)
    rank = dot(hot.astype(bf16), before, NN)
    first = jnp.where(rank < 0.5, hot, 0.0)
    second = hot - first
    both = jnp.concatenate([first, second], axis=0).astype(bf16)
    copies[1].wait()
    offsets = offset[...].astype(f32)
    rows = lax.broadcasted_iota(jnp.int32, (8, LANES), 0)
    spread_y = jnp.broadcast_to(offsets[0:1], (8, LANES))
    spread_z = jnp.broadcast_to(offsets[1:2], (8, LANES))
    tail = jnp.zeros((LANES, LANES), f32)
    empty = jnp.zeros((LANES - 8, LANES), f32)
    for slot, chosen in ((0, first), (1, second)):
        table = jnp.where(rows == 2 * slot, spread_y, 0.0) + jnp.where(
            rows == 2 * slot + 1, spread_z, 0.0
        )
        table = jnp.concatenate([table, empty], axis=0).astype(bf16)
        tail = tail + dot(chosen.astype(bf16), table, NT)
    out[pl.ds(12, LANES, stride=SENT), :] = tail
    for quantity in range(6):
        if quantity % 3 == 0:
            copies[2 + quantity // 3].wait()
        if quantity < 3:
            source = coords[quantity] * REACH[quantity]
        else:
            source = force[quantity - 3]
        high, middle, low = split_3(source)
        placed = dot(both, high, NN) + dot(both, middle, NN) + dot(both, low, NN)
        for slot in range(2):
            out[pl.ds(slot * 6 + quantity, LANES, stride=SENT), :] = placed[
                slot * LANES : (slot + 1) * LANES
            ]
    back[:, :LANES] = first.T.astype(bf16)
    back[:, LANES:] = second.T.astype(bf16)


def prep(coords, force, slab, offset):
    return pl.pallas_call(
        prep_kernel,
        out_shape=(
            jax.ShapeDtypeStruct((SENT * LANES, LANES), f32),
            jax.ShapeDtypeStruct((LANES, 2 * LANES), bf16),
        ),
        in_specs=[anywhere()] * 4,
        out_specs=(vmem(), vmem()),
        scratch_shapes=[
            pltpu.VMEM((3, LANES, LANES), f32),
            pltpu.VMEM((3, LANES, LANES), f32),
            pltpu.VMEM((1, LANES), jnp.int32),
            pltpu.VMEM((2, LANES), jnp.int32),
            pltpu.SemaphoreType.DMA((4,)),
        ],
        compiler_params=params(VMEM_ALL),
    )(coords, force, slab, offset)


def stack_2(values):
    high, low = split_2(values)
    return jnp.concatenate([high, low], axis=0).astype(bf16)


def plane_stack(weight_x, weight_y, planes):
    return stack_2(jnp.concatenate([weight_x[a : a + 1] * weight_y for a in planes], axis=0))


def own_halves(out):
    row = lax.broadcasted_iota(jnp.int32, (48, LANES), 0)
    lane = lax.broadcasted_iota(jnp.int32, (48, LANES), 1)
    return jnp.where((row < 24) == (lane < 64), out, 0.0)


def spread_pair(load, stack):
    turned = stack.T
    return own_halves(dot(load, jnp.concatenate([turned, turned], axis=0), NN))


def gather_windows(total, rows, parts, index, unroll):
    for sub in range(unroll):
        for slot in range(2):
            row = rows[slot, index * unroll + sub]
            for c in range(3):
                start = slot * 24 + c * 8
                total[pl.ds(row + 32 * c, 8), :] += parts[sub, start : start + 8]


def spread_planes(total, picks):
    cells = jnp.zeros((96, LANES), f32)
    for y in range(0, WINDOWS, 2):
        wide = min(2, WINDOWS - y)
        both = [total[(y + i) * 96 : (y + i + 1) * 96] for i in range(wide)]
        both = both[0] if wide == 1 else jnp.concatenate(both, axis=1)
        chosen = picks[:, y * LANES : (y + wide) * LANES]
        high, low = split_2(both)
        cells = cells + dot(high.astype(bf16), chosen, NT) + dot(low.astype(bf16), chosen, NT)
    cells = jnp.concatenate([cells * time_step, jnp.zeros((32, LANES), f32)], axis=0).T
    return [cells[i * NY : (i + 1) * NY] for i in range(4)]


def spread_kernel(
    got, picks, grid, near, far, rows_out, weights, loads, stacks, total, parts, rows, sem
):
    tail = got[pl.ds(12, LANES, stride=SENT), :].T
    y = jnp.concatenate([tail[0:1], tail[2:3]], axis=0)
    z = jnp.concatenate([tail[1:2], tail[3:4]], axis=0)
    y = jnp.clip(y - 1.0, 0.0, WINDOWS - 1.0)
    z = jnp.clip(z - 1.0, 0.0, WINDOWS - 1.0)
    start = (y * 96.0 + z).astype(jnp.int32)
    rows_out[...] = jnp.concatenate([start, jnp.zeros((6, LANES), jnp.int32)], axis=0)
    copy = pltpu.make_async_copy(rows_out, rows, sem)
    copy.start()
    total[...] = jnp.zeros_like(total)
    taps = lax.broadcasted_iota(jnp.int32, (8, LANES), 0).astype(f32) - 1.0

    def compute(index):
        for sub in range(SPREAD_UNROLL):
            device = index * SPREAD_UNROLL + sub
            load, stack = [], []
            for slot in range(2):
                source = device * SENT + slot * 6
                weight_x, weight_y, weight_z = [
                    phi(taps - got[pl.ds(source + dim, 1), :]) for dim in range(3)
                ]
                weights[device, slot, 0:8] = weight_x
                weights[device, slot, 8:16] = weight_y
                weights[device, slot, 16:24] = weight_z
                stack.append(plane_stack(weight_x, weight_y, EDGES))
                load += [got[pl.ds(source + 3 + c, 1), :] * weight_z for c in range(3)]
            load = jnp.concatenate(split_2(jnp.concatenate(load, axis=0)), axis=1).astype(bf16)
            stack = jnp.concatenate(stack, axis=0)
            loads[device] = load
            stacks[device] = stack
            parts[sub] = spread_pair(load, stack)

    def step(index, carry):
        gather_windows(total, rows, parts, index - 1, SPREAD_UNROLL)
        compute(index)
        return carry

    compute(0)
    copy.wait()
    lax.fori_loop(1, LANES // SPREAD_UNROLL, step, 0)
    gather_windows(total, rows, parts, LANES // SPREAD_UNROLL - 1, SPREAD_UNROLL)
    planes = spread_planes(total, picks)
    odd = lax.axis_index("slab") % 2 == 1
    for i in range(4):
        grid[i] = planes[i]
    for i in range(2):
        near[i] = jnp.where(odd, planes[i], planes[2 + i])
        far[i] = jnp.where(odd, planes[2 + i], planes[i])


def spread(got, picks):
    return pl.pallas_call(
        spread_kernel,
        out_shape=(
            jax.ShapeDtypeStruct((4, NY, LANES), f32),
            jax.ShapeDtypeStruct((2, NY, LANES), f32),
            jax.ShapeDtypeStruct((2, NY, LANES), f32),
            jax.ShapeDtypeStruct((8, LANES), jnp.int32),
            jax.ShapeDtypeStruct((LANES, 2, 24, LANES), f32),
            jax.ShapeDtypeStruct((LANES, 48, 2 * LANES), bf16),
            jax.ShapeDtypeStruct((LANES, 128, LANES), bf16),
        ),
        in_specs=[vmem()] * 2,
        out_specs=(vmem(),) * 7,
        scratch_shapes=[
            pltpu.VMEM((TABLE, LANES), f32),
            pltpu.VMEM((SPREAD_UNROLL, 48, LANES), f32),
            pltpu.SMEM((8, LANES), jnp.int32),
            pltpu.SemaphoreType.DMA,
        ],
        compiler_params=params(),
    )(got, picks)


def forcing_of(cells, c):
    lane = lax.broadcasted_iota(jnp.int32, (NY, NZ), 1)
    if c:
        cells = pltpu.roll(cells, LANES - 32 * c, 1)
    return jnp.where(lane < 32, cells, 0.0)


def fluid_plane(load, cells, p):
    centers = [load(c, p) for c in range(3)]
    results = []
    for c in range(3):
        center = centers[c]
        x_plus, x_minus = load(c, p + 1), load(c, p - 1)
        y_plus, y_minus = pltpu.roll(center, NY - 1, 0), pltpu.roll(center, 1, 0)
        z_plus, z_minus = pltpu.roll(center, NZ - 1, 1), pltpu.roll(center, 1, 1)
        around = (x_plus + x_minus) + (y_plus + y_minus) + (z_plus + z_minus)
        advect = (
            centers[0] * (x_plus - x_minus)
            + centers[1] * (y_plus - y_minus)
            + centers[2] * (z_plus - z_minus)
        )
        results.append(
            (1.0 - 6.0 * time_step * viscosity) * center
            + (time_step * viscosity) * around
            - (0.5 * time_step) * advect
            + forcing_of(cells, c)
        )
    return results


def packed_plane(parts):
    lane = lax.broadcasted_iota(jnp.int32, (NY, LANES), 1)
    cells = jnp.where(lane < 32, parts[0], 0.0)
    for c in (1, 2):
        moved = pltpu.roll(parts[c], 32 * c, 1)
        cells = jnp.where((lane >= 32 * c) & (lane < 32 * c + 32), moved, cells)
    return cells


def fill_table(table, planes, picks):
    cells = jnp.concatenate([packed_plane(parts) for parts in planes], axis=0).T[:96]
    split = stack_2(cells)
    lane = lax.broadcasted_iota(jnp.int32, (96, LANES), 1)
    for y in range(0, WINDOWS, 2):
        wide = min(2, WINDOWS - y)
        both = dot(split, picks[:, y * LANES : (y + wide) * LANES], NN)
        for i in range(wide):
            part = both[:, i * LANES : (i + 1) * LANES]
            table[(y + i) * 96 : (y + i + 1) * 96] = jnp.where(lane < 64, part[:96], part[96:])


def fold(a, b, width):
    if b is None:
        return a + pltpu.roll(a, width, 0)
    bit = (lax.broadcasted_iota(jnp.int32, (8, LANES), 0) & width) == 0
    return jnp.where(bit, a, b) + pltpu.roll(jnp.where(bit, b, a), width, 0)


def window_sums(table, rows, device, stack, weights):
    cells = []
    for slot in range(2):
        row = rows[slot, device]
        for c in range(3):
            cells.append(table[pl.ds(row + 32 * c, 8), :])
    both = jnp.concatenate([stack[:64], stack[64:]], axis=1)
    both = jnp.concatenate([both, both], axis=0)
    values = dot(jnp.concatenate(cells, axis=0).astype(bf16), both, NN)
    v = []
    for slot in range(2):
        weight_z = weights[device, slot, 16:24]
        for c in range(3):
            start = slot * 24 + c * 8
            v.append(values[start : start + 8, slot * LANES : (slot + 1) * LANES] * weight_z)
    low = fold(fold(v[0], v[1], 1), fold(v[2], v[3], 1), 2)
    high = fold(fold(v[4], v[5], 1), None, 2)
    return fold(low, high, 4)[:6]


def halo_reader(inside, same, cross, depth):
    odd = lax.axis_index("slab") % 2 == 1

    def load(c, p):
        if p < 0:
            return jnp.where(odd, same[c, p + depth], cross[c, p + depth])
        if p >= CX:
            return jnp.where(odd, cross[c, p - CX], same[c, p - CX])
        return inside[c, p]

    return load


def inner_kernel(
    velocity, same, cross, grid, rows_in, weights, loads, picks,
    step_1, step_2, middle, partial, stacks, total, parts, table, rows, sem
):
    copy = pltpu.make_async_copy(rows_in, rows, sem)
    copy.start()
    total[...] = jnp.zeros_like(total)

    def compute(index):
        for sub in range(MIDDLE_UNROLL):
            device = index * MIDDLE_UNROLL + sub
            stack = jnp.concatenate(
                [
                    plane_stack(weights[device, slot, 0:8], weights[device, slot, 8:16], MIDDLE)
                    for slot in range(2)
                ],
                axis=0,
            )
            stacks[device] = stack
            parts[sub] = spread_pair(loads[device], stack)

    def spread_step(index, carry):
        gather_windows(total, rows, parts, index - 1, MIDDLE_UNROLL)
        compute(index)
        return carry

    compute(0)
    copy.wait()
    lax.fori_loop(1, LANES // MIDDLE_UNROLL, spread_step, 0)
    gather_windows(total, rows, parts, LANES // MIDDLE_UNROLL - 1, MIDDLE_UNROLL)
    forces = dict(zip(MIDDLE, spread_planes(total, picks)))
    for i, p in enumerate(EDGES):
        forces[p] = grid[i]

    load_0 = halo_reader(velocity, same, cross, SUBSTEPS)
    for p in range(CX):
        for c, value in enumerate(fluid_plane(load_0, forces[p], p)):
            step_1[c, p] = value
    for p in range(1, CX - 1):
        for c, value in enumerate(fluid_plane(lambda c, p: step_1[c, p], forces[p], p)):
            step_2[c, p] = value
    planes = []
    for p in MIDDLE:
        planes.append(fluid_plane(lambda c, p: step_2[c, p], forces[p], p))
        for c in range(3):
            middle[c, p - MIDDLE[0]] = planes[-1][c]
    fill_table(table, planes, picks)

    def step(index, carry):
        for sub in range(INNER_UNROLL):
            device = index * INNER_UNROLL + sub
            partial[pl.ds(device * 6, 6), :] = window_sums(
                table, rows, device, stacks[device], weights
            )
        return carry

    lax.fori_loop(0, LANES // INNER_UNROLL, step, 0)


def inner(*arguments):
    return pl.pallas_call(
        inner_kernel,
        out_shape=(
            jax.ShapeDtypeStruct((3, CX, NY, NZ), f32),
            jax.ShapeDtypeStruct((3, CX, NY, NZ), f32),
            jax.ShapeDtypeStruct((3, len(MIDDLE), NY, NZ), f32),
            jax.ShapeDtypeStruct((6 * LANES, LANES), f32),
        ),
        in_specs=[vmem()] * 8,
        out_specs=(vmem(),) * 4,
        scratch_shapes=[
            pltpu.VMEM((LANES, 128, LANES), bf16),
            pltpu.VMEM((TABLE, LANES), f32),
            pltpu.VMEM((MIDDLE_UNROLL, 48, LANES), f32),
            pltpu.VMEM((TABLE, LANES), f32),
            pltpu.SMEM((8, LANES), jnp.int32),
            pltpu.SemaphoreType.DMA,
        ],
        compiler_params=params(),
        cost_estimate=pl.CostEstimate(
            flops=6_000_000_000, bytes_accessed=8_000_000, transcendentals=0
        ),
    )(*arguments)


def edge_kernel(
    velocity, same, cross, grid, near, far, rows_in, weights, stacks, picks,
    step_1, step_2, middle, partial,
    field, out, ends_1, ends_2, ends_3, table, rows, sems
):
    copies = [pltpu.make_async_copy(rows_in, rows, sems.at[0])]
    copies.append(
        pltpu.make_async_copy(middle, field.at[:, pl.ds(MIDDLE[0], len(MIDDLE))], sems.at[1])
    )
    for i, p in enumerate((0, CX - 2)):
        source, target = ends_3.at[:, pl.ds(2 * i, 2)], field.at[:, pl.ds(p, 2)]
        copies.append(pltpu.make_async_copy(source, target, sems.at[2 + i]))
    copies[0].start()
    copies[1].start()
    odd = lax.axis_index("slab") % 2 == 1

    def cells(p):
        if p < 0:
            return jnp.where(odd, near[p + 2], far[p + 2])
        if p >= CX:
            return jnp.where(odd, far[p - CX], near[p - CX])
        return grid[EDGES.index(p)]

    def reader(ends, inside, low):
        def load(c, p):
            for i, q in enumerate(low):
                if p == q:
                    return ends[c, i]
            return inside[c, p]

        return load

    planes_1 = (-2, -1, CX, CX + 1)
    planes_2 = (-1, 0, CX - 1, CX)
    load_0 = halo_reader(velocity, same, cross, SUBSTEPS)
    for i, p in enumerate(planes_1):
        for c, value in enumerate(fluid_plane(load_0, cells(p), p)):
            ends_1[c, i] = value
    load_1 = reader(ends_1, step_1, planes_1)
    for i, p in enumerate(planes_2):
        for c, value in enumerate(fluid_plane(load_1, cells(p), p)):
            ends_2[c, i] = value
    load_2 = reader(ends_2, step_2, planes_2)
    planes = []
    for i, p in enumerate(EDGES):
        planes.append(fluid_plane(load_2, cells(p), p))
        for c in range(3):
            ends_3[c, i] = planes[-1][c]
    copies[2].start()
    copies[3].start()
    fill_table(table, planes, picks)
    copies[0].wait()

    def step(index, carry):
        for sub in range(EDGE_UNROLL):
            device = index * EDGE_UNROLL + sub
            own = pl.ds(device * 6, 6)
            out[own, :] = partial[own, :] + window_sums(
                table, rows, device, stacks[device], weights
            )
        return carry

    lax.fori_loop(0, LANES // EDGE_UNROLL, step, 0)
    for copy in copies[1:]:
        copy.wait()


def edge(*arguments):
    return pl.pallas_call(
        edge_kernel,
        out_shape=(
            jax.ShapeDtypeStruct((3, CX, NY, NZ), f32),
            jax.ShapeDtypeStruct((6 * LANES, LANES), f32),
        ),
        in_specs=[vmem()] * 14,
        out_specs=(anywhere(), vmem()),
        scratch_shapes=[
            pltpu.VMEM((3, 4, NY, NZ), f32),
            pltpu.VMEM((3, 4, NY, NZ), f32),
            pltpu.VMEM((3, 4, NY, NZ), f32),
            pltpu.VMEM((TABLE, LANES), f32),
            pltpu.SMEM((8, LANES), jnp.int32),
            pltpu.SemaphoreType.DMA((4,)),
        ],
        compiler_params=params(),
    )(*arguments)


def pick_kernel(returned, back, out):
    chosen = back[...]
    for c in range(3):
        both = jnp.concatenate(
            [returned[pl.ds(3 * slot + c, LANES, stride=6), :] for slot in range(2)], axis=0
        )
        high, middle, low = split_3(both)
        out[c] = dot(chosen, high, NN) + dot(chosen, middle, NN) + dot(chosen, low, NN)


def pick(returned, back):
    return pl.pallas_call(
        pick_kernel,
        out_shape=jax.ShapeDtypeStruct((3, LANES, LANES), f32),
        in_specs=[vmem()] * 2,
        out_specs=vmem(),
        compiler_params=params(),
    )(returned, back)


def exchange(values):
    shape = values.shape
    values = values.reshape(LANES, 1, -1)
    values = lax.all_to_all(values, "slab", split_axis=0, concat_axis=0, tiled=True)
    return values.reshape(shape)


def swap(values, first):
    count = lax.axis_size("slab")
    pairs = []
    for i in range(first, count + first, 2):
        a, b = i % count, (i + 1) % count
        pairs += [(a, b), (b, a)]
    return lax.ppermute(values, "slab", pairs)


def body(velocity, node_coords, node_force, block_slab, block_offset):
    picks = window_picks()
    sent, back = prep(
        jnp.transpose(node_coords, (1, 0, 2)),
        jnp.transpose(node_force, (1, 0, 2)),
        jnp.transpose(block_slab, (1, 0)),
        jnp.transpose(block_offset, (1, 0)),
    )
    got = exchange(sent)
    odd = lax.axis_index("slab") % 2 == 1
    first, last = velocity[:, :SUBSTEPS], velocity[:, CX - SUBSTEPS :]
    cross = swap(jnp.where(odd, last, first), 1)
    same = swap(jnp.where(odd, first, last), 0)
    grid, near, far, rows, weights, loads, stacks = spread(got, picks)
    far = swap(far, 1)
    near = swap(near, 0)
    inside = inner(velocity, same, cross, grid, rows, weights, loads, picks)
    field, sums = edge(
        velocity, same, cross, grid, near, far, rows, weights, stacks, picks, *inside
    )
    node_velocity = pick(exchange(sums), back)
    return field, jnp.transpose(node_velocity, (1, 0, 2))


def solution(mesh):
    return jax.shard_map(
        body,
        mesh=mesh,
        in_specs=(
            P(None, "slab", None, None),
            P("slab", None, None),
            P("slab", None, None),
            P("slab", None),
            P("slab", None),
        ),
        out_specs=(P(None, "slab", None, None), P("slab", None, None)),
        check_vma=False,
    )
```

time: 72.2 us -> 69 us (0.956)
  Pallas kernels: 21.8 us -> 18.5 us
    pallas_call x3, Pallas kernels: 10.7 us -> 8.05 us  [the longest x1 5.2 us: spread(): pl.pallas_call(spread_kernel, out_shape=(jax.ShapeDtypeStruct((4, NY, LAN...]
  transfers between devices with their start and end apart: 5 -> 5, of which waited for: 1 -> 1; matrix products, arithmetic and copies ran while one was open for 1% -> 1% of each run, Pallas kernels for 20% -> 17%
where the time goes in v2:
time: 69 us; the launch traced here: 68.8 us
  starting transfers between devices  21.3 us (31%)
  blocking collectives  19.6 us (28%)
  Pallas kernels  18.5 us (27%)
  waiting for transfers between devices  7.7 us (11%)
  other arithmetic  1.01 us (1%)
  between operations  0.72 us (1%)
    all_to_all x1, blocking collectives, exchange(): lax.all_to_all(values, 'slab', split_axis=0, concat_axis=0, tiled=True)  19.6 us
    all_to_all x1, starting transfers between devices, exchange(): lax.all_to_all(values, 'slab', split_axis=0, concat_axis=0, tiled=True)  11.5 us
    ppermute x4, starting transfers between devices, swap(): return lax.ppermute(values, 'slab', pairs)  9.81 us
    all_to_all x1, waiting for transfers between devices, exchange(): lax.all_to_all(values, 'slab', split_axis=0, concat_axis=0, tiled=True)  7.69 us
    pallas_call x1, Pallas kernels, inner(): pl.pallas_call(inner_kernel, out_shape=(jax.ShapeDtypeStruct((3, CX, NY,...  6.54 us
    pallas_call x1, Pallas kernels, spread(): pl.pallas_call(spread_kernel, out_shape=(jax.ShapeDtypeStruct((4, NY, LAN...  5.2 us
    pallas_call x1, Pallas kernels, edge(): pl.pallas_call(edge_kernel, out_shape=(jax.ShapeDtypeStruct((3, CX, NY, N...  2.92 us
    pallas_call x1, Pallas kernels, prep(): pl.pallas_call(prep_kernel, out_shape=(jax.ShapeDtypeStruct((SENT * LANES...  2.64 us
  transfers between devices with their start and end apart: 5, of which 1 were waited for; matrix products, arithmetic and copies ran while one was open for 1% of the time, Pallas kernels for 17%

profile of v2, /device:TPU:1, one launch (start us, length us, event | category | flops | bytes accessed | tf_op | source)
XLA Modules:
  0.0 68.8 jit_solution(2720339667736404686)
XLA Ops:
  0.6 2.6 %shard_map.68 = (f32[1664,128]{1,0:T(8,128)}, bf16[128,256]{1,0:T(8,128)(2,1)}) custom-call(f32[3,128,128]{2,1,0:T(8,128)} %bitcast.13, f32[3,128,128]{2,1,0:T(8,128)} %bitcast.14, s32[1,128]{1,0:T(1,128)} %bitcast.17, s32[2,128]{1,0:T(2,128)} %bitcast.16), custom_call_target="tpu_custom_call" | custom-call | tf_op jit(solution)/shard_map/pallas_call | solution.py:156
  3.3 11.5 %all-to-all-start = ((f32[128,1,1664]{2,1,0:T(1,128)}), f32[128,1,1664]{2,1,0:T(1,128)S(1)}, u32[]{:S(2)}, u32[]{:S(2)}) async-start(f32[128,1,1664]{2,1,0:T(1,128)} %bitcast.12), calls=%async_computation | async-start | bytes 1703936 | tf_op jit(solution)/shard_map/all_to_all | solution.py:581
  14.8 1.0 %slice_select_fusion = (f32[3,3,32,128]{3,2,1,0:T(8,128)S(1)}, f32[3,3,32,128]{3,2,1,0:T(8,128)S(1)}) fusion(f32[3,8,32,128]{3,2,1,0:T(8,128)} %velocity.3, pred[]{:T(512)S(6)} %eq.5), kind=kLoop, calls=%fused_computation | loop fusion | flops 73728 | bytes 589825 | tf_op jit(solution)/shard_map/jit(_where)/select_n | solution.py:605
  15.8 1.7 %collective-permute-start.1 = (f32[3,3,32,128]{3,2,1,0:T(8,128)S(1)}, f32[3,3,32,128]{3,2,1,0:T(8,128)S(1)}, u32[]{:S(2)}, u32[]{:S(2)}) collective-permute-start(f32[3,3,32,128]{3,2,1,0:T(8,128)S(1)} %get-tuple-element.32), channel_id=1, source_target_pairs={{1,2},{2,1},{3,4},{4,3},{5,6},{6,5},{7,8},{8,7},{9,10},{10,9},{11,... | collective-permute-start | bytes 442376 | tf_op jit(solution)/shard_map/ppermute | solution.py:591
  17.5 0.0 copy-start
  17.5 6.5 %collective-permute-start = (f32[3,3,32,128]{3,2,1,0:T(8,128)S(1)}, f32[3,3,32,128]{3,2,1,0:T(8,128)S(1)}, u32[]{:S(2)}, u32[]{:S(2)}) collective-permute-start(f32[3,3,32,128]{3,2,1,0:T(8,128)S(1)} %get-tuple-element.33), channel_id=1, source_target_pairs={{0,1},{1,0},{2,3},{3,2},{4,5},{5,4},{6,7},{7,6},{8,9},{9,8},{10,11... | collective-permute-start | bytes 442376 | tf_op jit(solution)/shard_map/ppermute | solution.py:591
  24.0 0.2 shard_map.69.picks
  24.2 7.7 %all-to-all-done = f32[128,1,1664]{2,1,0:T(1,128)S(1)} async-done(((f32[128,1,1664]{2,1,0:T(1,128)}), f32[128,1,1664]{2,1,0:T(1,128)S(1)}, u32[]{:S(2)}, u32[]{:S(2)}) %all-to-all-start) | async-done | bytes 852000 | tf_op jit(solution)/shard_map/all_to_all | solution.py:581
  31.9 5.2 %shard_map.70 = (f32[4,32,128]{2,1,0:T(8,128)S(1)}, f32[2,32,128]{2,1,0:T(8,128)S(1)}, f32[2,32,128]{2,1,0:T(8,128)S(1)}, s32[8,128]{1,0:T(8,128)S(1)}, f32[128,...) custom-call(f32[1664,128]{1,0:T(8,128)S(1)} %bitcast.9, ...), custom_call_target="tpu_custom_call" | custom-call | tf_op jit(solution)/shard_map/pallas_call | solution.py:271
  37.1 1.1 %collective-permute-start.2 = (f32[2,32,128]{2,1,0:T(8,128)S(1)}, f32[2,32,128]{2,1,0:T(8,128)S(1)}, u32[]{:S(2)}, u32[]{:S(2)}) collective-permute-start(f32[2,32,128]{2,1,0:T(8,128)S(1)} %get-tuple-element.19), channel_id=1, source_target_pairs={{0,1},{1,0},{2,3},{3,2},{4,5},{5,4},{6,7},{7,6},{8,9},{9,8},{10,11... | collective-permute-start | bytes 98312 | tf_op jit(solution)/shard_map/ppermute | solution.py:591
  38.2 0.5 collective-permute-start.3
  38.7 0.0 collective-permute-done.1.cross
  38.7 0.0 collective-permute-done.same
  38.7 0.0 copy-done
  38.8 6.5 %shard_map.71 = (f32[3,8,32,128]{3,2,1,0:T(8,128)S(1)}, f32[3,8,32,128]{3,2,1,0:T(8,128)S(1)}, f32[3,4,32,128]{3,2,1,0:T(8,128)S(1)}, f32[768,128]{1,0:T(8,128)S(1)}) custom-call(f32[3,8,32,128]{3,2,1,0:T(8,128)S(1)} %copy-done, f32[3,3,32,128]{3,2,1,0:T(8,128)S(1)} %collective-permute-done.same, f32[3,3,32,128]{3,2,1,0:T(8,128)S(1)} %collective-permute-done.1.cross, ...), custom_call_target="tpu_custom_call" | custom-call | flops 6000000000 | bytes 8000000 | tf_op jit(solution)/shard_map/pallas_call | solution.py:445
  45.3 0.0 collective-permute-done.2.near
  45.3 0.0 collective-permute-done.3.far
  45.3 0.0 copy-start.1
  45.3 2.9 %shard_map.72 = (f32[3,8,32,128]{3,2,1,0:T(8,128)}, f32[768,128]{1,0:T(8,128)S(1)}) custom-call(f32[3,8,32,128]{3,2,1,0:T(8,128)S(1)} %copy-done, f32[3,3,32,128]{3,2,1,0:T(8,128)S(1)} %collective-permute-done.same, f32[3,3,32,128]{3,2,1,0:T(8,128)S(1)} %collective-permute-done.1.cross, f32[4,32,128]{2,1,0:T(8,128)S(1)} %get-tuple-element.18.grid, ...), custom_call_target="tpu_custom_call" | custom-call | tf_op jit(solution)/shard_map/pallas_call | solution.py:538
  48.3 19.6 %all_to_all.10 = f32[128,1,768]{2,1,0:T(1,128)S(1)} all-to-all(f32[128,1,768]{2,1,0:T(1,128)S(1)} %bitcast.11), channel_id=1, replica_groups=mesh['slab'=128] {'slab'}, dimensions={0} | all-to-all | bytes 786432 | tf_op jit(solution)/shard_map/all_to_all | solution.py:581
  67.8 0.0 copy-done.1
  67.8 1.0 %shard_map.73 = f32[3,128,128]{2,1,0:T(8,128)} custom-call(f32[768,128]{1,0:T(8,128)S(1)} %bitcast.10, bf16[128,256]{1,0:T(8,128)(2,1)S(1)} %copy-done.1), custom_call_target="tpu_custom_call" | custom-call | tf_op jit(solution)/shard_map/pallas_call | solution.py:569
Async XLA Ops:
  3.3 28.7 %all-to-all-start = ((f32[128,1,1664]{2,1,0:T(1,128)}), f32[128,1,1664]{2,1,0:T(1,128)S(1)}, u32[]{:S(2)}, u32[]{:S(2)}) async-start(f32[128,1,1664]{2,1,0:T(1,128)} %bitcast.12), calls=%async_computation | async-start | bytes 1703936 | tf_op jit(solution)/shard_map/all_to_all | solution.py:581
  15.8 22.9 %collective-permute-start.1 = (f32[3,3,32,128]{3,2,1,0:T(8,128)S(1)}, f32[3,3,32,128]{3,2,1,0:T(8,128)S(1)}, u32[]{:S(2)}, u32[]{:S(2)}) collective-permute-start(f32[3,3,32,128]{3,2,1,0:T(8,128)S(1)} %get-tuple-element.32), channel_id=1, source_target_pairs={{1,2},{2,1},{3,4},{4,3},{5,6},{6,5},{7,8},{8,7},{9,10},{10,9},{11,... | collective-permute-start | bytes 442376 | tf_op jit(solution)/shard_map/ppermute | solution.py:591
  17.5 21.2 %copy-start = (f32[3,8,32,128]{3,2,1,0:T(8,128)S(1)}, f32[3,8,32,128]{3,2,1,0:T(8,128)}, u32[]{:S(2)}) copy-start(f32[3,8,32,128]{3,2,1,0:T(8,128)} %velocity.3) | copy-start | bytes 1179652
  17.5 21.2 %collective-permute-start = (f32[3,3,32,128]{3,2,1,0:T(8,128)S(1)}, f32[3,3,32,128]{3,2,1,0:T(8,128)S(1)}, u32[]{:S(2)}, u32[]{:S(2)}) collective-permute-start(f32[3,3,32,128]{3,2,1,0:T(8,128)S(1)} %get-tuple-element.33), channel_id=1, source_target_pairs={{0,1},{1,0},{2,3},{3,2},{4,5},{5,4},{6,7},{7,6},{8,9},{9,8},{10,11... | collective-permute-start | bytes 442376 | tf_op jit(solution)/shard_map/ppermute | solution.py:591
  37.1 8.2 %collective-permute-start.2 = (f32[2,32,128]{2,1,0:T(8,128)S(1)}, f32[2,32,128]{2,1,0:T(8,128)S(1)}, u32[]{:S(2)}, u32[]{:S(2)}) collective-permute-start(f32[2,32,128]{2,1,0:T(8,128)S(1)} %get-tuple-element.19), channel_id=1, source_target_pairs={{0,1},{1,0},{2,3},{3,2},{4,5},{5,4},{6,7},{7,6},{8,9},{9,8},{10,11... | collective-permute-start | bytes 98312 | tf_op jit(solution)/shard_map/ppermute | solution.py:591
  38.2 7.1 %collective-permute-start.3 = (f32[2,32,128]{2,1,0:T(8,128)S(1)}, f32[2,32,128]{2,1,0:T(8,128)S(1)}, u32[]{:S(2)}, u32[]{:S(2)}) collective-permute-start(f32[2,32,128]{2,1,0:T(8,128)S(1)} %get-tuple-element.20), channel_id=1, source_target_pairs={{1,2},{2,1},{3,4},{4,3},{5,6},{6,5},{7,8},{8,7},{9,10},{10,9},{11,... | collective-permute-start | bytes 98312 | tf_op jit(solution)/shard_map/ppermute | solution.py:591
  45.3 22.5 %copy-start.1 = (bf16[128,256]{1,0:T(8,128)(2,1)S(1)}, bf16[128,256]{1,0:T(8,128)(2,1)}, u32[]{:S(2)}) copy-start(bf16[128,256]{1,0:T(8,128)(2,1)} %get-tuple-element.31.back) | copy-start | bytes 196612

commit v3 on v2

--- a/solution.py
+++ b/solution.py
@@ -12,7 +12,6 @@
 LANES = 128
 WINDOWS = 25
 SPREAD_UNROLL = 32
-MIDDLE_UNROLL = 32
 INNER_UNROLL = 32
 EDGE_UNROLL = 32
 
@@ -78,27 +77,37 @@
 TABLE = WINDOWS * 96
 EDGES = (0, 1, 6, 7)
 MIDDLE = (2, 3, 4, 5)
+ORDER = EDGES + MIDDLE
 SENT = 13
 REACH = (CX - 4.0, 5.0, 5.0)
 
 
-def picks_kernel(out):
-    source = lax.broadcasted_iota(jnp.int32, (LANES, LANES), 0)
+def fill_picks(picks):
+    row = lax.broadcasted_iota(jnp.int32, (LANES, LANES), 0)
     lane = lax.broadcasted_iota(jnp.int32, (LANES, LANES), 1)
-    apart = source - ((lane >> 3) & 3) * 32 - (lane & 7)
+    apart = row - ((lane >> 3) & 3) * 32 - (lane & 7)
     for start in range(WINDOWS):
         chosen = jnp.where(apart == start, 1.0, 0.0)
-        out[:, start * LANES : (start + 1) * LANES] = chosen.astype(bf16)
+        picks[:, start * LANES : (start + 1) * LANES] = chosen.astype(bf16)
+
+
+def turned_picks_kernel(turned):
+    row = lax.broadcasted_iota(jnp.int32, (LANES, 2 * LANES), 0)
+    lane = lax.broadcasted_iota(jnp.int32, (LANES, 2 * LANES), 1)
+    apart = lane - ((row >> 3) & 7) * 32 - (row & 7)
+    for start in range(WINDOWS):
+        chosen = jnp.where(apart == start, 1.0, 0.0)
+        turned[start * LANES : (start + 1) * LANES] = chosen.astype(bf16)
 
 
 def window_picks():
     return pl.pallas_call(
-        picks_kernel,
-        out_shape=jax.ShapeDtypeStruct((LANES, WINDOWS * LANES), bf16),
+        turned_picks_kernel,
+        out_shape=jax.ShapeDtypeStruct((WINDOWS * LANES, 2 * LANES), bf16),
         out_specs=vmem(),
         compiler_params=params(),
         cost_estimate=pl.CostEstimate(
-            flops=2_000_000_000, bytes_accessed=2_000_000, transcendentals=0
+            flops=2_000_000_000, bytes_accessed=4_000_000, transcendentals=0
         ),
     )()
 
@@ -177,19 +186,14 @@
     return jnp.concatenate([high, low], axis=0).astype(bf16)
 
 
-def plane_stack(weight_x, weight_y, planes):
-    return stack_2(jnp.concatenate([weight_x[a : a + 1] * weight_y for a in planes], axis=0))
-
-
-def own_halves(out):
-    row = lax.broadcasted_iota(jnp.int32, (48, LANES), 0)
-    lane = lax.broadcasted_iota(jnp.int32, (48, LANES), 1)
-    return jnp.where((row < 24) == (lane < 64), out, 0.0)
+def joint_stack(weight_x, weight_y):
+    return stack_2(jnp.concatenate([weight_x[a : a + 1] * weight_y for a in ORDER], axis=0))
 
 
 def spread_pair(load, stack):
     turned = stack.T
-    return own_halves(dot(load, jnp.concatenate([turned, turned], axis=0), NN))
+    out = dot(load, jnp.concatenate([turned, turned], axis=0), NN)
+    return jnp.concatenate([out[:24, :LANES], out[24:, LANES:]], axis=0)
 
 
 def gather_windows(total, rows, parts, index, unroll):
@@ -201,21 +205,21 @@
                 total[pl.ds(row + 32 * c, 8), :] += parts[sub, start : start + 8]
 
 
-def spread_planes(total, picks):
-    cells = jnp.zeros((96, LANES), f32)
+def spread_planes(total, turned_picks):
+    cells = jnp.zeros((192, 2 * LANES), f32)
     for y in range(0, WINDOWS, 2):
         wide = min(2, WINDOWS - y)
         both = [total[(y + i) * 96 : (y + i + 1) * 96] for i in range(wide)]
         both = both[0] if wide == 1 else jnp.concatenate(both, axis=1)
-        chosen = picks[:, y * LANES : (y + wide) * LANES]
-        high, low = split_2(both)
-        cells = cells + dot(high.astype(bf16), chosen, NT) + dot(low.astype(bf16), chosen, NT)
-    cells = jnp.concatenate([cells * time_step, jnp.zeros((32, LANES), f32)], axis=0).T
-    return [cells[i * NY : (i + 1) * NY] for i in range(4)]
+        chosen = turned_picks[y * LANES : (y + wide) * LANES]
+        cells = cells + dot(stack_2(both), chosen, NN)
+    cells = (cells[:96] + cells[96:]) * time_step
+    cells = jnp.concatenate([cells, jnp.zeros((32, 2 * LANES), f32)], axis=0).T
+    return {p: cells[i * NY : (i + 1) * NY] for i, p in enumerate(ORDER)}
 
 
 def spread_kernel(
-    got, picks, grid, near, far, rows_out, weights, loads, stacks, total, parts, rows, sem
+    got, turned_picks, grid, near, far, rows_out, weights_z, stacks, total, parts, rows, sem
 ):
     tail = got[pl.ds(12, LANES, stride=SENT), :].T
     y = jnp.concatenate([tail[0:1], tail[2:3]], axis=0)
@@ -238,14 +242,11 @@
                 weight_x, weight_y, weight_z = [
                     phi(taps - got[pl.ds(source + dim, 1), :]) for dim in range(3)
                 ]
-                weights[device, slot, 0:8] = weight_x
-                weights[device, slot, 8:16] = weight_y
-                weights[device, slot, 16:24] = weight_z
-                stack.append(plane_stack(weight_x, weight_y, EDGES))
+                weights_z[device, slot] = weight_z
+                stack.append(joint_stack(weight_x, weight_y))
                 load += [got[pl.ds(source + 3 + c, 1), :] * weight_z for c in range(3)]
             load = jnp.concatenate(split_2(jnp.concatenate(load, axis=0)), axis=1).astype(bf16)
             stack = jnp.concatenate(stack, axis=0)
-            loads[device] = load
             stacks[device] = stack
             parts[sub] = spread_pair(load, stack)
 
@@ -258,29 +259,28 @@
     copy.wait()
     lax.fori_loop(1, LANES // SPREAD_UNROLL, step, 0)
     gather_windows(total, rows, parts, LANES // SPREAD_UNROLL - 1, SPREAD_UNROLL)
-    planes = spread_planes(total, picks)
+    planes = spread_planes(total, turned_picks)
     odd = lax.axis_index("slab") % 2 == 1
-    for i in range(4):
-        grid[i] = planes[i]
-    for i in range(2):
-        near[i] = jnp.where(odd, planes[i], planes[2 + i])
-        far[i] = jnp.where(odd, planes[2 + i], planes[i])
-
-
-def spread(got, picks):
+    for a in range(CX):
+        grid[a] = planes[a]
+    for a in range(2):
+        near[a] = jnp.where(odd, planes[a], planes[CX - 2 + a])
+        far[a] = jnp.where(odd, planes[CX - 2 + a], planes[a])
+
+
+def spread(got, turned_picks):
     return pl.pallas_call(
         spread_kernel,
         out_shape=(
-            jax.ShapeDtypeStruct((4, NY, LANES), f32),
+            jax.ShapeDtypeStruct((CX, NY, LANES), f32),
             jax.ShapeDtypeStruct((2, NY, LANES), f32),
             jax.ShapeDtypeStruct((2, NY, LANES), f32),
             jax.ShapeDtypeStruct((8, LANES), jnp.int32),
-            jax.ShapeDtypeStruct((LANES, 2, 24, LANES), f32),
-            jax.ShapeDtypeStruct((LANES, 48, 2 * LANES), bf16),
-            jax.ShapeDtypeStruct((LANES, 128, LANES), bf16),
+            jax.ShapeDtypeStruct((LANES, 2, 8, LANES), f32),
+            jax.ShapeDtypeStruct((LANES, 256, LANES), bf16),
         ),
         in_specs=[vmem()] * 2,
-        out_specs=(vmem(),) * 7,
+        out_specs=(vmem(),) * 6,
         scratch_shapes=[
             pltpu.VMEM((TABLE, LANES), f32),
             pltpu.VMEM((SPREAD_UNROLL, 48, LANES), f32),
@@ -288,7 +288,7 @@
             pltpu.SemaphoreType.DMA,
         ],
         compiler_params=params(),
-    )(got, picks)
+    )(got, turned_picks)
 
 
 def forcing_of(cells, c):
@@ -349,18 +349,19 @@
     return jnp.where(bit, a, b) + pltpu.roll(jnp.where(bit, b, a), width, 0)
 
 
-def window_sums(table, rows, device, stack, weights):
+def window_sums(table, rows, device, stack, weights_z, first):
     cells = []
     for slot in range(2):
         row = rows[slot, device]
         for c in range(3):
             cells.append(table[pl.ds(row + 32 * c, 8), :])
-    both = jnp.concatenate([stack[:64], stack[64:]], axis=1)
-    both = jnp.concatenate([both, both], axis=0)
+    high = jnp.concatenate([stack[first : first + 32], stack[128 + first : 160 + first]], axis=1)
+    low = jnp.concatenate([stack[64 + first : 96 + first], stack[192 + first : 224 + first]], axis=1)
+    both = jnp.concatenate([high, low, high, low], axis=0)
     values = dot(jnp.concatenate(cells, axis=0).astype(bf16), both, NN)
     v = []
     for slot in range(2):
-        weight_z = weights[device, slot, 16:24]
+        weight_z = weights_z[device, slot]
         for c in range(3):
             start = slot * 24 + c * 8
             v.append(values[start : start + 8, slot * LANES : (slot + 1) * LANES] * weight_z)
@@ -383,58 +384,32 @@
 
 
 def inner_kernel(
-    velocity, same, cross, grid, rows_in, weights, loads, picks,
-    step_1, step_2, middle, partial, stacks, total, parts, table, rows, sem
+    velocity, same, cross, grid, rows_in, weights_z, stacks,
+    step_1, step_2, middle, partial, picks, table, rows, sem
 ):
     copy = pltpu.make_async_copy(rows_in, rows, sem)
     copy.start()
-    total[...] = jnp.zeros_like(total)
-
-    def compute(index):
-        for sub in range(MIDDLE_UNROLL):
-            device = index * MIDDLE_UNROLL + sub
-            stack = jnp.concatenate(
-                [
-                    plane_stack(weights[device, slot, 0:8], weights[device, slot, 8:16], MIDDLE)
-                    for slot in range(2)
-                ],
-                axis=0,
-            )
-            stacks[device] = stack
-            parts[sub] = spread_pair(loads[device], stack)
-
-    def spread_step(index, carry):
-        gather_windows(total, rows, parts, index - 1, MIDDLE_UNROLL)
-        compute(index)
-        return carry
-
-    compute(0)
-    copy.wait()
-    lax.fori_loop(1, LANES // MIDDLE_UNROLL, spread_step, 0)
-    gather_windows(total, rows, parts, LANES // MIDDLE_UNROLL - 1, MIDDLE_UNROLL)
-    forces = dict(zip(MIDDLE, spread_planes(total, picks)))
-    for i, p in enumerate(EDGES):
-        forces[p] = grid[i]
-
+    fill_picks(picks)
     load_0 = halo_reader(velocity, same, cross, SUBSTEPS)
     for p in range(CX):
-        for c, value in enumerate(fluid_plane(load_0, forces[p], p)):
+        for c, value in enumerate(fluid_plane(load_0, grid[p], p)):
             step_1[c, p] = value
     for p in range(1, CX - 1):
-        for c, value in enumerate(fluid_plane(lambda c, p: step_1[c, p], forces[p], p)):
+        for c, value in enumerate(fluid_plane(lambda c, p: step_1[c, p], grid[p], p)):
             step_2[c, p] = value
     planes = []
     for p in MIDDLE:
-        planes.append(fluid_plane(lambda c, p: step_2[c, p], forces[p], p))
+        planes.append(fluid_plane(lambda c, p: step_2[c, p], grid[p], p))
         for c in range(3):
             middle[c, p - MIDDLE[0]] = planes[-1][c]
     fill_table(table, planes, picks)
+    copy.wait()
 
     def step(index, carry):
         for sub in range(INNER_UNROLL):
             device = index * INNER_UNROLL + sub
             partial[pl.ds(device * 6, 6), :] = window_sums(
-                table, rows, device, stacks[device], weights
+                table, rows, device, stacks[device], weights_z, 32
             )
         return carry
 
@@ -449,13 +424,11 @@
             jax.ShapeDtypeStruct((3, CX, NY, NZ), f32),
             jax.ShapeDtypeStruct((3, len(MIDDLE), NY, NZ), f32),
             jax.ShapeDtypeStruct((6 * LANES, LANES), f32),
+            jax.ShapeDtypeStruct((LANES, WINDOWS * LANES), bf16),
         ),
-        in_specs=[vmem()] * 8,
-        out_specs=(vmem(),) * 4,
+        in_specs=[vmem()] * 7,
+        out_specs=(vmem(),) * 5,
         scratch_shapes=[
-            pltpu.VMEM((LANES, 128, LANES), bf16),
-            pltpu.VMEM((TABLE, LANES), f32),
-            pltpu.VMEM((MIDDLE_UNROLL, 48, LANES), f32),
             pltpu.VMEM((TABLE, LANES), f32),
             pltpu.SMEM((8, LANES), jnp.int32),
             pltpu.SemaphoreType.DMA,
@@ -468,8 +441,8 @@
 
 
 def edge_kernel(
-    velocity, same, cross, grid, near, far, rows_in, weights, stacks, picks,
-    step_1, step_2, middle, partial,
+    velocity, same, cross, grid, near, far, rows_in, weights_z, stacks,
+    step_1, step_2, middle, partial, picks,
     field, out, ends_1, ends_2, ends_3, table, rows, sems
 ):
     copies = [pltpu.make_async_copy(rows_in, rows, sems.at[0])]
@@ -488,7 +461,7 @@
             return jnp.where(odd, near[p + 2], far[p + 2])
         if p >= CX:
             return jnp.where(odd, far[p - CX], near[p - CX])
-        return grid[EDGES.index(p)]
+        return grid[p]
 
     def reader(ends, inside, low):
         def load(c, p):
@@ -525,7 +498,7 @@
             device = index * EDGE_UNROLL + sub
             own = pl.ds(device * 6, 6)
             out[own, :] = partial[own, :] + window_sums(
-                table, rows, device, stacks[device], weights
+                table, rows, device, stacks[device], weights_z, 0
             )
         return carry
 
@@ -592,7 +565,7 @@
 
 
 def body(velocity, node_coords, node_force, block_slab, block_offset):
-    picks = window_picks()
+    turned_picks = window_picks()
     sent, back = prep(
         jnp.transpose(node_coords, (1, 0, 2)),
         jnp.transpose(node_force, (1, 0, 2)),
@@ -604,12 +577,12 @@
     first, last = velocity[:, :SUBSTEPS], velocity[:, CX - SUBSTEPS :]
     cross = swap(jnp.where(odd, last, first), 1)
     same = swap(jnp.where(odd, first, last), 0)
-    grid, near, far, rows, weights, loads, stacks = spread(got, picks)
+    grid, near, far, rows, weights_z, stacks = spread(got, turned_picks)
+    near = swap(near, 0)
     far = swap(far, 1)
-    near = swap(near, 0)
-    inside = inner(velocity, same, cross, grid, rows, weights, loads, picks)
+    inside = inner(velocity, same, cross, grid, rows, weights_z, stacks)
     field, sums = edge(
-        velocity, same, cross, grid, near, far, rows, weights, stacks, picks, *inside
+        velocity, same, cross, grid, near, far, rows, weights_z, stacks, *inside
     )
     node_velocity = pick(exchange(sums), back)
     return field, jnp.transpose(node_velocity, (1, 0, 2))

time: 69 us -> 67.1 us (0.972)
  Pallas kernels: 18.5 us -> 15.9 us
    pallas_call x1, Pallas kernels: 6.54 us -> 3.13 us  [inner(): pl.pallas_call(inner_kernel, out_shape=(jax.ShapeDtypeStruct((3, CX, NY,...]
    pallas_call x2, Pallas kernels: 5.42 us -> 6.22 us  [the longest x1 5.93 us: spread(): pl.pallas_call(spread_kernel, out_shape=(jax.ShapeDtypeStruct((CX, NY, LA...]
  transfers between devices with their start and end apart: 5 -> 5, of which waited for: 1 -> 1; matrix products, arithmetic and copies ran while one was open for 1% -> 2% of each run, Pallas kernels for 17% -> 14%
where the time goes in v3:
time: 67.1 us; the launch traced here: 66.8 us
  starting transfers between devices  21.3 us (32%)
  blocking collectives  20.2 us (30%)
  Pallas kernels  15.9 us (24%)
  waiting for transfers between devices  7.64 us (11%)
  other arithmetic  1.01 us (2%)
  between operations  0.73 us (1%)
    all_to_all x1, blocking collectives, exchange(): lax.all_to_all(values, 'slab', split_axis=0, concat_axis=0, tiled=True)  20.2 us
    all_to_all x1, starting transfers between devices, exchange(): lax.all_to_all(values, 'slab', split_axis=0, concat_axis=0, tiled=True)  11.5 us
    ppermute x4, starting transfers between devices, swap(): return lax.ppermute(values, 'slab', pairs)  9.78 us
    all_to_all x1, waiting for transfers between devices, exchange(): lax.all_to_all(values, 'slab', split_axis=0, concat_axis=0, tiled=True)  7.63 us
    pallas_call x1, Pallas kernels, spread(): pl.pallas_call(spread_kernel, out_shape=(jax.ShapeDtypeStruct((CX, NY, LA...  5.93 us
    pallas_call x1, Pallas kernels, inner(): pl.pallas_call(inner_kernel, out_shape=(jax.ShapeDtypeStruct((3, CX, NY,...  3.13 us
    pallas_call x1, Pallas kernels, edge(): pl.pallas_call(edge_kernel, out_shape=(jax.ShapeDtypeStruct((3, CX, NY, N...  2.92 us
    pallas_call x1, Pallas kernels, prep(): pl.pallas_call(prep_kernel, out_shape=(jax.ShapeDtypeStruct((SENT * LANES...  2.69 us
  transfers between devices with their start and end apart: 5, of which 1 were waited for; matrix products, arithmetic and copies ran while one was open for 2% of the time, Pallas kernels for 14%

profile of v3, /device:TPU:1, one launch (start us, length us, event | category | flops | bytes accessed | tf_op | source)
XLA Modules:
  0.0 66.8 jit_solution(7885973000742504725)
XLA Ops:
  0.6 0.0 copy-start
  0.6 2.7 %shard_map.68 = (f32[1664,128]{1,0:T(8,128)}, bf16[128,256]{1,0:T(8,128)(2,1)}) custom-call(f32[3,128,128]{2,1,0:T(8,128)} %bitcast.13, f32[3,128,128]{2,1,0:T(8,128)} %bitcast.14, s32[1,128]{1,0:T(1,128)} %bitcast.17, s32[2,128]{1,0:T(2,128)} %bitcast.16), custom_call_target="tpu_custom_call" | custom-call | tf_op jit(solution)/shard_map/pallas_call | solution.py:165
  3.3 11.5 %all-to-all-start = ((f32[128,1,1664]{2,1,0:T(1,128)}), f32[128,1,1664]{2,1,0:T(1,128)S(1)}, u32[]{:S(2)}, u32[]{:S(2)}) async-start(f32[128,1,1664]{2,1,0:T(1,128)} %bitcast.12), calls=%async_computation | async-start | bytes 1703936 | tf_op jit(solution)/shard_map/all_to_all | solution.py:554
  14.9 1.0 %slice_select_fusion = (f32[3,3,32,128]{3,2,1,0:T(8,128)S(1)}, f32[3,3,32,128]{3,2,1,0:T(8,128)S(1)}) fusion(f32[3,8,32,128]{3,2,1,0:T(8,128)} %velocity.3, pred[]{:T(512)S(6)} %eq.5), kind=kLoop, calls=%fused_computation | loop fusion | flops 73728 | bytes 589825 | tf_op jit(solution)/shard_map/jit(_where)/select_n | solution.py:578
  15.9 1.7 %collective-permute-start.1 = (f32[3,3,32,128]{3,2,1,0:T(8,128)S(1)}, f32[3,3,32,128]{3,2,1,0:T(8,128)S(1)}, u32[]{:S(2)}, u32[]{:S(2)}) collective-permute-start(f32[3,3,32,128]{3,2,1,0:T(8,128)S(1)} %get-tuple-element.32), channel_id=1, source_target_pairs={{1,2},{2,1},{3,4},{4,3},{5,6},{6,5},{7,8},{8,7},{9,10},{10,9},{11,... | collective-permute-start | bytes 442376 | tf_op jit(solution)/shard_map/ppermute | solution.py:564
  17.6 6.5 %collective-permute-start = (f32[3,3,32,128]{3,2,1,0:T(8,128)S(1)}, f32[3,3,32,128]{3,2,1,0:T(8,128)S(1)}, u32[]{:S(2)}, u32[]{:S(2)}) collective-permute-start(f32[3,3,32,128]{3,2,1,0:T(8,128)S(1)} %get-tuple-element.33), channel_id=1, source_target_pairs={{0,1},{1,0},{2,3},{3,2},{4,5},{5,4},{6,7},{7,6},{8,9},{9,8},{10,11... | collective-permute-start | bytes 442376 | tf_op jit(solution)/shard_map/ppermute | solution.py:564
  24.1 0.3 shard_map.69.turned_picks
  24.4 7.6 %all-to-all-done = f32[128,1,1664]{2,1,0:T(1,128)S(1)} async-done(((f32[128,1,1664]{2,1,0:T(1,128)}), f32[128,1,1664]{2,1,0:T(1,128)S(1)}, u32[]{:S(2)}, u32[]{:S(2)}) %all-to-all-start) | async-done | bytes 852000 | tf_op jit(solution)/shard_map/all_to_all | solution.py:554
  32.0 5.9 %shard_map.70 = (f32[8,32,128]{2,1,0:T(8,128)S(1)}, f32[2,32,128]{2,1,0:T(8,128)S(1)}, f32[2,32,128]{2,1,0:T(8,128)S(1)}, s32[8,128]{1,0:T(8,128)S(1)}, f32[128,...) custom-call(f32[1664,128]{1,0:T(8,128)S(1)} %bitcast.9, bf16[3200,256]{1,0:T(8,128)(2,1)S(1)} %shard_map.69.turned_picks), custom_call_target="tpu_custom_call" | custom-call | tf_op jit(solution)/shard_map/pallas_call | solution.py:272
  37.9 1.1 %collective-permute-start.2 = (f32[2,32,128]{2,1,0:T(8,128)S(1)}, f32[2,32,128]{2,1,0:T(8,128)S(1)}, u32[]{:S(2)}, u32[]{:S(2)}) collective-permute-start(f32[2,32,128]{2,1,0:T(8,128)S(1)} %get-tuple-element.19), channel_id=1, source_target_pairs={{0,1},{1,0},{2,3},{3,2},{4,5},{5,4},{6,7},{7,6},{8,9},{9,8},{10,11... | collective-permute-start | bytes 98312 | tf_op jit(solution)/shard_map/ppermute | solution.py:564
  39.0 0.5 collective-permute-start.3
  39.5 0.0 collective-permute-done.1.cross
  39.5 0.0 collective-permute-done.same
  39.5 0.0 copy-done
  39.5 3.1 %shard_map.71 = (f32[3,8,32,128]{3,2,1,0:T(8,128)S(1)}, f32[3,8,32,128]{3,2,1,0:T(8,128)S(1)}, f32[3,4,32,128]{3,2,1,0:T(8,128)S(1)}, f32[768,128]{1,0:T(8,128)S(1)}, bf16[128,3200]{1,0:T(8,128)(2,1)S(1)}) custom-call(f32[3,8,32,128]{3,2,1,0:T(8,128)S(1)} %copy-done, f32[3,3,32,128]{3,2,1,0:T(8,128)S(1)} %collective-permute-done.same, ...), custom_call_target="tpu_custom_call" | custom-call | flops 6000000000 | bytes 8000000 | tf_op jit(solution)/shard_map/pallas_call | solution.py:420
  42.7 0.0 copy-start.1
  42.7 0.0 collective-permute-done.2.near
  42.7 0.0 collective-permute-done.3.far
  42.7 2.9 %shard_map.72 = (f32[3,8,32,128]{3,2,1,0:T(8,128)}, f32[768,128]{1,0:T(8,128)S(1)}) custom-call(f32[3,8,32,128]{3,2,1,0:T(8,128)S(1)} %copy-done, f32[3,3,32,128]{3,2,1,0:T(8,128)S(1)} %collective-permute-done.same, f32[3,3,32,128]{3,2,1,0:T(8,128)S(1)} %collective-permute-done.1.cross, f32[8,32,128]{2,1,0:T(8,128)S(1)} %get-tuple-element.18.grid, ...), custom_call_target="tpu_custom_call" | custom-call | tf_op jit(solution)/shard_map/pallas_call | solution.py:511
  45.6 20.2 %all_to_all.10 = f32[128,1,768]{2,1,0:T(1,128)S(1)} all-to-all(f32[128,1,768]{2,1,0:T(1,128)S(1)} %bitcast.11), channel_id=1, replica_groups=mesh['slab'=128] {'slab'}, dimensions={0} | all-to-all | bytes 786432 | tf_op jit(solution)/shard_map/all_to_all | solution.py:554
  65.8 0.0 copy-done.1
  65.9 1.0 %shard_map.73 = f32[3,128,128]{2,1,0:T(8,128)} custom-call(f32[768,128]{1,0:T(8,128)S(1)} %bitcast.10, bf16[128,256]{1,0:T(8,128)(2,1)S(1)} %copy-done.1), custom_call_target="tpu_custom_call" | custom-call | tf_op jit(solution)/shard_map/pallas_call | solution.py:542
Async XLA Ops:
  0.6 38.9 %copy-start = (f32[3,8,32,128]{3,2,1,0:T(8,128)S(1)}, f32[3,8,32,128]{3,2,1,0:T(8,128)}, u32[]{:S(2)}) copy-start(f32[3,8,32,128]{3,2,1,0:T(8,128)} %velocity.3) | copy-start | bytes 1179652
  3.3 28.7 %all-to-all-start = ((f32[128,1,1664]{2,1,0:T(1,128)}), f32[128,1,1664]{2,1,0:T(1,128)S(1)}, u32[]{:S(2)}, u32[]{:S(2)}) async-start(f32[128,1,1664]{2,1,0:T(1,128)} %bitcast.12), calls=%async_computation | async-start | bytes 1703936 | tf_op jit(solution)/shard_map/all_to_all | solution.py:554
  15.9 23.6 %collective-permute-start.1 = (f32[3,3,32,128]{3,2,1,0:T(8,128)S(1)}, f32[3,3,32,128]{3,2,1,0:T(8,128)S(1)}, u32[]{:S(2)}, u32[]{:S(2)}) collective-permute-start(f32[3,3,32,128]{3,2,1,0:T(8,128)S(1)} %get-tuple-element.32), channel_id=1, source_target_pairs={{1,2},{2,1},{3,4},{4,3},{5,6},{6,5},{7,8},{8,7},{9,10},{10,9},{11,... | collective-permute-start | bytes 442376 | tf_op jit(solution)/shard_map/ppermute | solution.py:564
  17.6 21.9 %collective-permute-start = (f32[3,3,32,128]{3,2,1,0:T(8,128)S(1)}, f32[3,3,32,128]{3,2,1,0:T(8,128)S(1)}, u32[]{:S(2)}, u32[]{:S(2)}) collective-permute-start(f32[3,3,32,128]{3,2,1,0:T(8,128)S(1)} %get-tuple-element.33), channel_id=1, source_target_pairs={{0,1},{1,0},{2,3},{3,2},{4,5},{5,4},{6,7},{7,6},{8,9},{9,8},{10,11... | collective-permute-start | bytes 442376 | tf_op jit(solution)/shard_map/ppermute | solution.py:564
  37.9 4.7 %collective-permute-start.2 = (f32[2,32,128]{2,1,0:T(8,128)S(1)}, f32[2,32,128]{2,1,0:T(8,128)S(1)}, u32[]{:S(2)}, u32[]{:S(2)}) collective-permute-start(f32[2,32,128]{2,1,0:T(8,128)S(1)} %get-tuple-element.19), channel_id=1, source_target_pairs={{0,1},{1,0},{2,3},{3,2},{4,5},{5,4},{6,7},{7,6},{8,9},{9,8},{10,11... | collective-permute-start | bytes 98312 | tf_op jit(solution)/shard_map/ppermute | solution.py:564
  39.0 3.7 %collective-permute-start.3 = (f32[2,32,128]{2,1,0:T(8,128)S(1)}, f32[2,32,128]{2,1,0:T(8,128)S(1)}, u32[]{:S(2)}, u32[]{:S(2)}) collective-permute-start(f32[2,32,128]{2,1,0:T(8,128)S(1)} %get-tuple-element.20), channel_id=1, source_target_pairs={{1,2},{2,1},{3,4},{4,3},{5,6},{6,5},{7,8},{8,7},{9,10},{10,9},{11,... | collective-permute-start | bytes 98312 | tf_op jit(solution)/shard_map/ppermute | solution.py:564
  42.7 23.2 %copy-start.1 = (bf16[128,256]{1,0:T(8,128)(2,1)S(1)}, bf16[128,256]{1,0:T(8,128)(2,1)}, u32[]{:S(2)}) copy-start(bf16[128,256]{1,0:T(8,128)(2,1)} %get-tuple-element.31.back) | copy-start | bytes 196612

commit v4 on v3

--- a/solution.py
+++ b/solution.py
@@ -11,9 +11,7 @@
 SUBSTEPS = 3
 LANES = 128
 WINDOWS = 25
-SPREAD_UNROLL = 32
-INNER_UNROLL = 32
-EDGE_UNROLL = 32
+GROUP = 16
 
 time_step = 0.1
 viscosity = 0.2
@@ -196,10 +194,10 @@
     return jnp.concatenate([out[:24, :LANES], out[24:, LANES:]], axis=0)
 
 
-def gather_windows(total, rows, parts, index, unroll):
-    for sub in range(unroll):
+def gather_windows(total, rows, parts, index):
+    for sub in range(GROUP):
         for slot in range(2):
-            row = rows[slot, index * unroll + sub]
+            row = rows[slot, index * GROUP + sub]
             for c in range(3):
                 start = slot * 24 + c * 8
                 total[pl.ds(row + 32 * c, 8), :] += parts[sub, start : start + 8]
@@ -234,8 +232,8 @@
     taps = lax.broadcasted_iota(jnp.int32, (8, LANES), 0).astype(f32) - 1.0
 
     def compute(index):
-        for sub in range(SPREAD_UNROLL):
-            device = index * SPREAD_UNROLL + sub
+        for sub in range(GROUP):
+            device = index * GROUP + sub
             load, stack = [], []
             for slot in range(2):
                 source = device * SENT + slot * 6
@@ -250,15 +248,12 @@
             stacks[device] = stack
             parts[sub] = spread_pair(load, stack)
 
-    def step(index, carry):
-        gather_windows(total, rows, parts, index - 1, SPREAD_UNROLL)
-        compute(index)
-        return carry
-
     compute(0)
     copy.wait()
-    lax.fori_loop(1, LANES // SPREAD_UNROLL, step, 0)
-    gather_windows(total, rows, parts, LANES // SPREAD_UNROLL - 1, SPREAD_UNROLL)
+    for index in range(1, LANES // GROUP):
+        gather_windows(total, rows, parts, index - 1)
+        compute(index)
+    gather_windows(total, rows, parts, LANES // GROUP - 1)
     planes = spread_planes(total, turned_picks)
     odd = lax.axis_index("slab") % 2 == 1
     for a in range(CX):
@@ -283,7 +278,7 @@
         out_specs=(vmem(),) * 6,
         scratch_shapes=[
             pltpu.VMEM((TABLE, LANES), f32),
-            pltpu.VMEM((SPREAD_UNROLL, 48, LANES), f32),
+            pltpu.VMEM((GROUP, 48, LANES), f32),
             pltpu.SMEM((8, LANES), jnp.int32),
             pltpu.SemaphoreType.DMA,
         ],
@@ -405,15 +400,10 @@
     fill_table(table, planes, picks)
     copy.wait()
 
-    def step(index, carry):
-        for sub in range(INNER_UNROLL):
-            device = index * INNER_UNROLL + sub
-            partial[pl.ds(device * 6, 6), :] = window_sums(
-                table, rows, device, stacks[device], weights_z, 32
-            )
-        return carry
-
-    lax.fori_loop(0, LANES // INNER_UNROLL, step, 0)
+    for device in range(LANES):
+        partial[device * 6 : device * 6 + 6] = window_sums(
+            table, rows, device, stacks[device], weights_z, 32
+        )
 
 
 def inner(*arguments):
@@ -493,16 +483,11 @@
     fill_table(table, planes, picks)
     copies[0].wait()
 
-    def step(index, carry):
-        for sub in range(EDGE_UNROLL):
-            device = index * EDGE_UNROLL + sub
-            own = pl.ds(device * 6, 6)
-            out[own, :] = partial[own, :] + window_sums(
-                table, rows, device, stacks[device], weights_z, 0
-            )
-        return carry
-
-    lax.fori_loop(0, LANES // EDGE_UNROLL, step, 0)
+    for device in range(LANES):
+        own = slice(device * 6, device * 6 + 6)
+        out[own] = partial[own] + window_sums(
+            table, rows, device, stacks[device], weights_z, 0
+        )
     for copy in copies[1:]:
         copy.wait()
 

time: 67.1 us -> 65.6 us (0.978)
  Pallas kernels: 15.9 us -> 14 us
    pallas_call x1, Pallas kernels: 5.93 us -> 4.89 us  [spread(): pl.pallas_call(spread_kernel, out_shape=(jax.ShapeDtypeStruct((CX, NY, LA...]
  transfers between devices with their start and end apart: 5 -> 5, of which waited for: 1 -> 2; matrix products, arithmetic and copies ran while one was open for 2% -> 2% of each run, Pallas kernels for 14% -> 12%
where the time goes in v4:
time: 65.6 us; the launch traced here: 65.4 us
  starting transfers between devices  21.3 us (32%)
  blocking collectives  20.6 us (31%)
  Pallas kernels  14 us (21%)
  waiting for transfers between devices  7.73 us (12%)
  other arithmetic  1.01 us (2%)
  between operations  0.72 us (1%)
    all_to_all x1, blocking collectives, exchange(): lax.all_to_all(values, 'slab', split_axis=0, concat_axis=0, tiled=True)  20.6 us
    all_to_all x1, starting transfers between devices, exchange(): lax.all_to_all(values, 'slab', split_axis=0, concat_axis=0, tiled=True)  11.5 us
    ppermute x4, starting transfers between devices, swap(): return lax.ppermute(values, 'slab', pairs)  9.83 us
    all_to_all x1, waiting for transfers between devices, exchange(): lax.all_to_all(values, 'slab', split_axis=0, concat_axis=0, tiled=True)  7.63 us
    pallas_call x1, Pallas kernels, spread(): pl.pallas_call(spread_kernel, out_shape=(jax.ShapeDtypeStruct((CX, NY, LA...  4.89 us
    pallas_call x1, Pallas kernels, prep(): pl.pallas_call(prep_kernel, out_shape=(jax.ShapeDtypeStruct((SENT * LANES...  2.69 us
    pallas_call x1, Pallas kernels, inner(): pl.pallas_call(inner_kernel, out_shape=(jax.ShapeDtypeStruct((3, CX, NY,...  2.68 us
    pallas_call x1, Pallas kernels, edge(): pl.pallas_call(edge_kernel, out_shape=(jax.ShapeDtypeStruct((3, CX, NY, N...  2.46 us
  transfers between devices with their start and end apart: 5, of which 2 were waited for; matrix products, arithmetic and copies ran while one was open for 2% of the time, Pallas kernels for 12%

profile of v4, /device:TPU:1, one launch (start us, length us, event | category | flops | bytes accessed | tf_op | source)
XLA Modules:
  0.0 65.4 jit_solution(14523813891049972821)
XLA Ops:
  0.6 0.0 copy-start
  0.6 2.7 %shard_map.68 = (f32[1664,128]{1,0:T(8,128)}, bf16[128,256]{1,0:T(8,128)(2,1)}) custom-call(f32[3,128,128]{2,1,0:T(8,128)} %bitcast.13, f32[3,128,128]{2,1,0:T(8,128)} %bitcast.14, s32[1,128]{1,0:T(1,128)} %bitcast.17, s32[2,128]{1,0:T(2,128)} %bitcast.16), custom_call_target="tpu_custom_call" | custom-call | tf_op jit(solution)/shard_map/pallas_call | solution.py:163
  3.3 11.5 %all-to-all-start = ((f32[128,1,1664]{2,1,0:T(1,128)}), f32[128,1,1664]{2,1,0:T(1,128)S(1)}, u32[]{:S(2)}, u32[]{:S(2)}) async-start(f32[128,1,1664]{2,1,0:T(1,128)} %bitcast.12), calls=%async_computation | async-start | bytes 1703936 | tf_op jit(solution)/shard_map/all_to_all | solution.py:539
  14.9 1.0 %slice_select_fusion = (f32[3,3,32,128]{3,2,1,0:T(8,128)S(1)}, f32[3,3,32,128]{3,2,1,0:T(8,128)S(1)}) fusion(f32[3,8,32,128]{3,2,1,0:T(8,128)} %velocity.3, pred[]{:T(512)S(6)} %eq.5), kind=kLoop, calls=%fused_computation | loop fusion | flops 73728 | bytes 589825 | tf_op jit(solution)/shard_map/jit(_where)/select_n | solution.py:563
  15.9 1.7 %collective-permute-start.1 = (f32[3,3,32,128]{3,2,1,0:T(8,128)S(1)}, f32[3,3,32,128]{3,2,1,0:T(8,128)S(1)}, u32[]{:S(2)}, u32[]{:S(2)}) collective-permute-start(f32[3,3,32,128]{3,2,1,0:T(8,128)S(1)} %get-tuple-element.32), channel_id=1, source_target_pairs={{1,2},{2,1},{3,4},{4,3},{5,6},{6,5},{7,8},{8,7},{9,10},{10,9},{11,... | collective-permute-start | bytes 442376 | tf_op jit(solution)/shard_map/ppermute | solution.py:549
  17.6 6.5 %collective-permute-start = (f32[3,3,32,128]{3,2,1,0:T(8,128)S(1)}, f32[3,3,32,128]{3,2,1,0:T(8,128)S(1)}, u32[]{:S(2)}, u32[]{:S(2)}) collective-permute-start(f32[3,3,32,128]{3,2,1,0:T(8,128)S(1)} %get-tuple-element.33), channel_id=1, source_target_pairs={{0,1},{1,0},{2,3},{3,2},{4,5},{5,4},{6,7},{7,6},{8,9},{9,8},{10,11... | collective-permute-start | bytes 442376 | tf_op jit(solution)/shard_map/ppermute | solution.py:549
  24.1 0.3 shard_map.69.turned_picks
  24.4 7.6 %all-to-all-done = f32[128,1,1664]{2,1,0:T(1,128)S(1)} async-done(((f32[128,1,1664]{2,1,0:T(1,128)}), f32[128,1,1664]{2,1,0:T(1,128)S(1)}, u32[]{:S(2)}, u32[]{:S(2)}) %all-to-all-start) | async-done | bytes 852000 | tf_op jit(solution)/shard_map/all_to_all | solution.py:539
  32.0 4.9 %shard_map.70 = (f32[8,32,128]{2,1,0:T(8,128)S(1)}, f32[2,32,128]{2,1,0:T(8,128)S(1)}, f32[2,32,128]{2,1,0:T(8,128)S(1)}, s32[8,128]{1,0:T(8,128)S(1)}, f32[128,...) custom-call(f32[1664,128]{1,0:T(8,128)S(1)} %bitcast.9, bf16[3200,256]{1,0:T(8,128)(2,1)S(1)} %shard_map.69.turned_picks), custom_call_target="tpu_custom_call" | custom-call | tf_op jit(solution)/shard_map/pallas_call | solution.py:267
  36.9 1.1 %collective-permute-start.2 = (f32[2,32,128]{2,1,0:T(8,128)S(1)}, f32[2,32,128]{2,1,0:T(8,128)S(1)}, u32[]{:S(2)}, u32[]{:S(2)}) collective-permute-start(f32[2,32,128]{2,1,0:T(8,128)S(1)} %get-tuple-element.19), channel_id=1, source_target_pairs={{0,1},{1,0},{2,3},{3,2},{4,5},{5,4},{6,7},{7,6},{8,9},{9,8},{10,11... | collective-permute-start | bytes 98312 | tf_op jit(solution)/shard_map/ppermute | solution.py:549
  38.0 0.5 collective-permute-start.3
  38.5 0.0 collective-permute-done.1.cross
  38.5 0.0 collective-permute-done.same
  38.5 0.0 copy-done
  38.5 2.7 %shard_map.71 = (f32[3,8,32,128]{3,2,1,0:T(8,128)S(1)}, f32[3,8,32,128]{3,2,1,0:T(8,128)S(1)}, f32[3,4,32,128]{3,2,1,0:T(8,128)S(1)}, f32[768,128]{1,0:T(8,128)S(1)}, bf16[128,3200]{1,0:T(8,128)(2,1)S(1)}) custom-call(f32[3,8,32,128]{3,2,1,0:T(8,128)S(1)} %copy-done, f32[3,3,32,128]{3,2,1,0:T(8,128)S(1)} %collective-permute-done.same, ...), custom_call_target="tpu_custom_call" | custom-call | flops 6000000000 | bytes 8000000 | tf_op jit(solution)/shard_map/pallas_call | solution.py:410
  41.2 0.0 copy-start.1
  41.2 0.0 collective-permute-done.2.near
  41.2 0.1 collective-permute-done.3.far
  41.3 2.5 %shard_map.72 = (f32[3,8,32,128]{3,2,1,0:T(8,128)}, f32[768,128]{1,0:T(8,128)S(1)}) custom-call(f32[3,8,32,128]{3,2,1,0:T(8,128)S(1)} %copy-done, f32[3,3,32,128]{3,2,1,0:T(8,128)S(1)} %collective-permute-done.same, f32[3,3,32,128]{3,2,1,0:T(8,128)S(1)} %collective-permute-done.1.cross, f32[8,32,128]{2,1,0:T(8,128)S(1)} %get-tuple-element.18.grid, ...), custom_call_target="tpu_custom_call" | custom-call | tf_op jit(solution)/shard_map/pallas_call | solution.py:496
  43.8 20.6 %all_to_all.10 = f32[128,1,768]{2,1,0:T(1,128)S(1)} all-to-all(f32[128,1,768]{2,1,0:T(1,128)S(1)} %bitcast.11), channel_id=1, replica_groups=mesh['slab'=128] {'slab'}, dimensions={0} | all-to-all | bytes 786432 | tf_op jit(solution)/shard_map/all_to_all | solution.py:539
  64.4 0.0 copy-done.1
  64.4 1.0 %shard_map.73 = f32[3,128,128]{2,1,0:T(8,128)} custom-call(f32[768,128]{1,0:T(8,128)S(1)} %bitcast.10, bf16[128,256]{1,0:T(8,128)(2,1)S(1)} %copy-done.1), custom_call_target="tpu_custom_call" | custom-call | tf_op jit(solution)/shard_map/pallas_call | solution.py:527
Async XLA Ops:
  0.6 37.9 %copy-start = (f32[3,8,32,128]{3,2,1,0:T(8,128)S(1)}, f32[3,8,32,128]{3,2,1,0:T(8,128)}, u32[]{:S(2)}) copy-start(f32[3,8,32,128]{3,2,1,0:T(8,128)} %velocity.3) | copy-start | bytes 1179652
  3.3 28.7 %all-to-all-start = ((f32[128,1,1664]{2,1,0:T(1,128)}), f32[128,1,1664]{2,1,0:T(1,128)S(1)}, u32[]{:S(2)}, u32[]{:S(2)}) async-start(f32[128,1,1664]{2,1,0:T(1,128)} %bitcast.12), calls=%async_computation | async-start | bytes 1703936 | tf_op jit(solution)/shard_map/all_to_all | solution.py:539
  15.9 22.6 %collective-permute-start.1 = (f32[3,3,32,128]{3,2,1,0:T(8,128)S(1)}, f32[3,3,32,128]{3,2,1,0:T(8,128)S(1)}, u32[]{:S(2)}, u32[]{:S(2)}) collective-permute-start(f32[3,3,32,128]{3,2,1,0:T(8,128)S(1)} %get-tuple-element.32), channel_id=1, source_target_pairs={{1,2},{2,1},{3,4},{4,3},{5,6},{6,5},{7,8},{8,7},{9,10},{10,9},{11,... | collective-permute-start | bytes 442376 | tf_op jit(solution)/shard_map/ppermute | solution.py:549
  17.6 20.9 %collective-permute-start = (f32[3,3,32,128]{3,2,1,0:T(8,128)S(1)}, f32[3,3,32,128]{3,2,1,0:T(8,128)S(1)}, u32[]{:S(2)}, u32[]{:S(2)}) collective-permute-start(f32[3,3,32,128]{3,2,1,0:T(8,128)S(1)} %get-tuple-element.33), channel_id=1, source_target_pairs={{0,1},{1,0},{2,3},{3,2},{4,5},{5,4},{6,7},{7,6},{8,9},{9,8},{10,11... | collective-permute-start | bytes 442376 | tf_op jit(solution)/shard_map/ppermute | solution.py:549
  36.9 4.3 %collective-permute-start.2 = (f32[2,32,128]{2,1,0:T(8,128)S(1)}, f32[2,32,128]{2,1,0:T(8,128)S(1)}, u32[]{:S(2)}, u32[]{:S(2)}) collective-permute-start(f32[2,32,128]{2,1,0:T(8,128)S(1)} %get-tuple-element.19), channel_id=1, source_target_pairs={{0,1},{1,0},{2,3},{3,2},{4,5},{5,4},{6,7},{7,6},{8,9},{9,8},{10,11... | collective-permute-start | bytes 98312 | tf_op jit(solution)/shard_map/ppermute | solution.py:549
  38.0 3.3 %collective-permute-start.3 = (f32[2,32,128]{2,1,0:T(8,128)S(1)}, f32[2,32,128]{2,1,0:T(8,128)S(1)}, u32[]{:S(2)}, u32[]{:S(2)}) collective-permute-start(f32[2,32,128]{2,1,0:T(8,128)S(1)} %get-tuple-element.20), channel_id=1, source_target_pairs={{1,2},{2,1},{3,4},{4,3},{5,6},{6,5},{7,8},{8,7},{9,10},{10,9},{11,... | collective-permute-start | bytes 98312 | tf_op jit(solution)/shard_map/ppermute | solution.py:549
  41.2 23.1 %copy-start.1 = (bf16[128,256]{1,0:T(8,128)(2,1)S(1)}, bf16[128,256]{1,0:T(8,128)(2,1)}, u32[]{:S(2)}) copy-start(bf16[128,256]{1,0:T(8,128)(2,1)} %get-tuple-element.31.back) | copy-start | bytes 196612

commit v5 on v4

--- a/solution.py
+++ b/solution.py
@@ -74,6 +74,7 @@
 
 TABLE = WINDOWS * 96
 EDGES = (0, 1, 6, 7)
+HALO = (-2, -1, CX, CX + 1)
 MIDDLE = (2, 3, 4, 5)
 ORDER = EDGES + MIDDLE
 SENT = 13
@@ -217,7 +218,7 @@
 
 
 def spread_kernel(
-    got, turned_picks, grid, near, far, rows_out, weights_z, stacks, total, parts, rows, sem
+    got, turned_picks, far, near, grid, rows_out, weights_z, stacks, total, parts, rows, sem
 ):
     tail = got[pl.ds(12, LANES, stride=SENT), :].T
     y = jnp.concatenate([tail[0:1], tail[2:3]], axis=0)
@@ -267,9 +268,9 @@
     return pl.pallas_call(
         spread_kernel,
         out_shape=(
-            jax.ShapeDtypeStruct((CX, NY, LANES), f32),
             jax.ShapeDtypeStruct((2, NY, LANES), f32),
             jax.ShapeDtypeStruct((2, NY, LANES), f32),
+            jax.ShapeDtypeStruct((CX, NY, LANES), f32),
             jax.ShapeDtypeStruct((8, LANES), jnp.int32),
             jax.ShapeDtypeStruct((LANES, 2, 8, LANES), f32),
             jax.ShapeDtypeStruct((LANES, 256, LANES), bf16),
@@ -307,12 +308,12 @@
             + centers[1] * (y_plus - y_minus)
             + centers[2] * (z_plus - z_minus)
         )
-        results.append(
+        moved = (
             (1.0 - 6.0 * time_step * viscosity) * center
             + (time_step * viscosity) * around
             - (0.5 * time_step) * advect
-            + forcing_of(cells, c)
-        )
+        )
+        results.append(moved if cells is None else moved + forcing_of(cells, c))
     return results
 
 
@@ -380,12 +381,15 @@
 
 def inner_kernel(
     velocity, same, cross, grid, rows_in, weights_z, stacks,
-    step_1, step_2, middle, partial, picks, table, rows, sem
+    step_1, step_2, middle, partial, picks, unforced, table, rows, sem
 ):
     copy = pltpu.make_async_copy(rows_in, rows, sem)
     copy.start()
     fill_picks(picks)
     load_0 = halo_reader(velocity, same, cross, SUBSTEPS)
+    for i, p in enumerate(HALO):
+        for c, value in enumerate(fluid_plane(load_0, None, p)):
+            unforced[c, i] = value
     for p in range(CX):
         for c, value in enumerate(fluid_plane(load_0, grid[p], p)):
             step_1[c, p] = value
@@ -415,9 +419,10 @@
             jax.ShapeDtypeStruct((3, len(MIDDLE), NY, NZ), f32),
             jax.ShapeDtypeStruct((6 * LANES, LANES), f32),
             jax.ShapeDtypeStruct((LANES, WINDOWS * LANES), bf16),
+            jax.ShapeDtypeStruct((3, len(HALO), NY, NZ), f32),
         ),
         in_specs=[vmem()] * 7,
-        out_specs=(vmem(),) * 5,
+        out_specs=(vmem(),) * 6,
         scratch_shapes=[
             pltpu.VMEM((TABLE, LANES), f32),
             pltpu.SMEM((8, LANES), jnp.int32),
@@ -431,8 +436,8 @@
 
 
 def edge_kernel(
-    velocity, same, cross, grid, near, far, rows_in, weights_z, stacks,
-    step_1, step_2, middle, partial, picks,
+    far, near, grid, rows_in, weights_z, stacks,
+    step_1, step_2, middle, partial, picks, unforced,
     field, out, ends_1, ends_2, ends_3, table, rows, sems
 ):
     copies = [pltpu.make_async_copy(rows_in, rows, sems.at[0])]
@@ -462,13 +467,11 @@
 
         return load
 
-    planes_1 = (-2, -1, CX, CX + 1)
     planes_2 = (-1, 0, CX - 1, CX)
-    load_0 = halo_reader(velocity, same, cross, SUBSTEPS)
-    for i, p in enumerate(planes_1):
-        for c, value in enumerate(fluid_plane(load_0, cells(p), p)):
-            ends_1[c, i] = value
-    load_1 = reader(ends_1, step_1, planes_1)
+    for i, p in enumerate(HALO):
+        for c in range(3):
+            ends_1[c, i] = unforced[c, i] + forcing_of(cells(p), c)
+    load_1 = reader(ends_1, step_1, HALO)
     for i, p in enumerate(planes_2):
         for c, value in enumerate(fluid_plane(load_1, cells(p), p)):
             ends_2[c, i] = value
@@ -499,7 +502,7 @@
             jax.ShapeDtypeStruct((3, CX, NY, NZ), f32),
             jax.ShapeDtypeStruct((6 * LANES, LANES), f32),
         ),
-        in_specs=[vmem()] * 14,
+        in_specs=[vmem()] * 12,
         out_specs=(anywhere(), vmem()),
         scratch_shapes=[
             pltpu.VMEM((3, 4, NY, NZ), f32),
@@ -562,13 +565,11 @@
     first, last = velocity[:, :SUBSTEPS], velocity[:, CX - SUBSTEPS :]
     cross = swap(jnp.where(odd, last, first), 1)
     same = swap(jnp.where(odd, first, last), 0)
-    grid, near, far, rows, weights_z, stacks = spread(got, turned_picks)
+    far, near, grid, rows, weights_z, stacks = spread(got, turned_picks)
+    far = swap(far, 1)
     near = swap(near, 0)
-    far = swap(far, 1)
     inside = inner(velocity, same, cross, grid, rows, weights_z, stacks)
-    field, sums = edge(
-        velocity, same, cross, grid, near, far, rows, weights_z, stacks, *inside
-    )
+    field, sums = edge(far, near, grid, rows, weights_z, stacks, *inside)
     node_velocity = pick(exchange(sums), back)
     return field, jnp.transpose(node_velocity, (1, 0, 2))
 

time: 65.6 us -> 65.4 us (level)
  transfers between devices with their start and end apart: 5 -> 5, of which waited for: 2 -> 1; matrix products, arithmetic and copies ran while one was open for 2% -> 2% of each run, Pallas kernels for 12% -> 12%
where the time goes in v5:
time: 65.4 us; the launch traced here: 65.1 us
  starting transfers between devices  21.7 us (33%)
  blocking collectives  20 us (31%)
  Pallas kernels  14.1 us (22%)
  waiting for transfers between devices  7.64 us (12%)
  other arithmetic  1.01 us (2%)
  between operations  0.73 us (1%)
    all_to_all x1, blocking collectives, exchange(): lax.all_to_all(values, 'slab', split_axis=0, concat_axis=0, tiled=True)  20 us
    all_to_all x1, starting transfers between devices, exchange(): lax.all_to_all(values, 'slab', split_axis=0, concat_axis=0, tiled=True)  11.5 us
    ppermute x4, starting transfers between devices, swap(): return lax.ppermute(values, 'slab', pairs)  10.2 us
    all_to_all x1, waiting for transfers between devices, exchange(): lax.all_to_all(values, 'slab', split_axis=0, concat_axis=0, tiled=True)  7.63 us
    pallas_call x1, Pallas kernels, spread(): pl.pallas_call(spread_kernel, out_shape=(jax.ShapeDtypeStruct((2, NY, LAN...  4.88 us
    pallas_call x1, Pallas kernels, inner(): pl.pallas_call(inner_kernel, out_shape=(jax.ShapeDtypeStruct((3, CX, NY,...  2.88 us
    pallas_call x1, Pallas kernels, prep(): pl.pallas_call(prep_kernel, out_shape=(jax.ShapeDtypeStruct((SENT * LANES...  2.69 us
    pallas_call x1, Pallas kernels, edge(): pl.pallas_call(edge_kernel, out_shape=(jax.ShapeDtypeStruct((3, CX, NY, N...  2.33 us
  transfers between devices with their start and end apart: 5, of which 1 were waited for; matrix products, arithmetic and copies ran while one was open for 2% of the time, Pallas kernels for 12%

profile of v5, /device:TPU:1, one launch (start us, length us, event | category | flops | bytes accessed | tf_op | source)
XLA Modules:
  0.0 65.1 jit_solution(5507669262862198881)
XLA Ops:
  0.6 0.0 copy-start
  0.6 2.7 %shard_map.68 = (f32[1664,128]{1,0:T(8,128)}, bf16[128,256]{1,0:T(8,128)(2,1)}) custom-call(f32[3,128,128]{2,1,0:T(8,128)} %bitcast.13, f32[3,128,128]{2,1,0:T(8,128)} %bitcast.14, s32[1,128]{1,0:T(1,128)} %bitcast.17, s32[2,128]{1,0:T(2,128)} %bitcast.16), custom_call_target="tpu_custom_call" | custom-call | tf_op jit(solution)/shard_map/pallas_call | solution.py:164
  3.3 11.5 %all-to-all-start = ((f32[128,1,1664]{2,1,0:T(1,128)}), f32[128,1,1664]{2,1,0:T(1,128)S(1)}, u32[]{:S(2)}, u32[]{:S(2)}) async-start(f32[128,1,1664]{2,1,0:T(1,128)} %bitcast.12), calls=%async_computation | async-start | bytes 1703936 | tf_op jit(solution)/shard_map/all_to_all | solution.py:542
  14.9 1.0 %slice_select_fusion = (f32[3,3,32,128]{3,2,1,0:T(8,128)S(1)}, f32[3,3,32,128]{3,2,1,0:T(8,128)S(1)}) fusion(f32[3,8,32,128]{3,2,1,0:T(8,128)} %velocity.1, pred[]{:T(512)S(6)} %eq.5), kind=kLoop, calls=%fused_computation | loop fusion | flops 73728 | bytes 589825 | tf_op jit(solution)/shard_map/jit(_where)/select_n | solution.py:566
  15.9 1.7 %collective-permute-start.3 = (f32[3,3,32,128]{3,2,1,0:T(8,128)S(1)}, f32[3,3,32,128]{3,2,1,0:T(8,128)S(1)}, u32[]{:S(2)}, u32[]{:S(2)}) collective-permute-start(f32[3,3,32,128]{3,2,1,0:T(8,128)S(1)} %get-tuple-element.34), channel_id=1, source_target_pairs={{1,2},{2,1},{3,4},{4,3},{5,6},{6,5},{7,8},{8,7},{9,10},{10,9},{11,... | collective-permute-start | bytes 442376 | tf_op jit(solution)/shard_map/ppermute | solution.py:552
  17.6 6.5 %collective-permute-start.2 = (f32[3,3,32,128]{3,2,1,0:T(8,128)S(1)}, f32[3,3,32,128]{3,2,1,0:T(8,128)S(1)}, u32[]{:S(2)}, u32[]{:S(2)}) collective-permute-start(f32[3,3,32,128]{3,2,1,0:T(8,128)S(1)} %get-tuple-element.35), channel_id=1, source_target_pairs={{0,1},{1,0},{2,3},{3,2},{4,5},{5,4},{6,7},{7,6},{8,9},{9,8},{10,11... | collective-permute-start | bytes 442376 | tf_op jit(solution)/shard_map/ppermute | solution.py:552
  24.1 0.3 shard_map.69.turned_picks
  24.4 7.6 %all-to-all-done = f32[128,1,1664]{2,1,0:T(1,128)S(1)} async-done(((f32[128,1,1664]{2,1,0:T(1,128)}), f32[128,1,1664]{2,1,0:T(1,128)S(1)}, u32[]{:S(2)}, u32[]{:S(2)}) %all-to-all-start) | async-done | bytes 852000 | tf_op jit(solution)/shard_map/all_to_all | solution.py:542
  32.0 4.9 %shard_map.70 = (f32[2,32,128]{2,1,0:T(8,128)S(1)}, f32[2,32,128]{2,1,0:T(8,128)S(1)}, f32[8,32,128]{2,1,0:T(8,128)S(1)}, s32[8,128]{1,0:T(8,128)S(1)}, f32[128,...) custom-call(f32[1664,128]{1,0:T(8,128)S(1)} %bitcast.9, bf16[3200,256]{1,0:T(8,128)(2,1)S(1)} %shard_map.69.turned_picks), custom_call_target="tpu_custom_call" | custom-call | tf_op jit(solution)/shard_map/pallas_call | solution.py:268
  36.9 1.5 %collective-permute-start = (f32[2,32,128]{2,1,0:T(8,128)S(1)}, f32[2,32,128]{2,1,0:T(8,128)S(1)}, u32[]{:S(2)}, u32[]{:S(2)}) collective-permute-start(f32[2,32,128]{2,1,0:T(8,128)S(1)} %get-tuple-element.19), channel_id=1, source_target_pairs={{1,2},{2,1},{3,4},{4,3},{5,6},{6,5},{7,8},{8,7},{9,10},{10,9},{11,... | collective-permute-start | bytes 98312 | tf_op jit(solution)/shard_map/ppermute | solution.py:552
  38.4 0.5 collective-permute-start.1
  38.9 0.0 collective-permute-done.3.cross
  38.9 0.0 collective-permute-done.2.same
  38.9 0.0 copy-done
  38.9 2.9 %shard_map.71 = (f32[3,8,32,128]{3,2,1,0:T(8,128)S(1)}, f32[3,8,32,128]{3,2,1,0:T(8,128)S(1)}, f32[3,4,32,128]{3,2,1,0:T(8,128)S(1)}, f32[768,128]{1,0:T(8,128)S...) custom-call(f32[3,8,32,128]{3,2,1,0:T(8,128)S(1)} %copy-done, ...), custom_call_target="tpu_custom_call" | custom-call | flops 6000000000 | bytes 8000000 | tf_op jit(solution)/shard_map/pallas_call | solution.py:414
  41.8 0.0 copy-start.1
  41.8 0.0 collective-permute-done.far
  41.8 0.0 collective-permute-done.1.near
  41.8 2.3 %shard_map.72 = (f32[3,8,32,128]{3,2,1,0:T(8,128)}, f32[768,128]{1,0:T(8,128)S(1)}) custom-call(f32[2,32,128]{2,1,0:T(8,128)S(1)} %collective-permute-done.far, f32[2,32,128]{2,1,0:T(8,128)S(1)} %collective-permute-done.1.near, f32[8,32,128]{2,1,0:T(8,128)S(1)} %get-tuple-element.21.grid, s32[8,128]{1,0:T(8,128)S(1)} %get-tuple-element.22.rows_in, ...), custom_call_target="tpu_custom_call" | custom-call | tf_op jit(solution)/shard_map/pallas_call | solution.py:499
  44.2 20.0 %all_to_all.10 = f32[128,1,768]{2,1,0:T(1,128)S(1)} all-to-all(f32[128,1,768]{2,1,0:T(1,128)S(1)} %bitcast.11), channel_id=1, replica_groups=mesh['slab'=128] {'slab'}, dimensions={0} | all-to-all | bytes 786432 | tf_op jit(solution)/shard_map/all_to_all | solution.py:542
  64.1 0.0 copy-done.1
  64.1 1.0 %shard_map.73 = f32[3,128,128]{2,1,0:T(8,128)} custom-call(f32[768,128]{1,0:T(8,128)S(1)} %bitcast.10, bf16[128,256]{1,0:T(8,128)(2,1)S(1)} %copy-done.1), custom_call_target="tpu_custom_call" | custom-call | tf_op jit(solution)/shard_map/pallas_call | solution.py:530
Async XLA Ops:
  0.6 38.3 %copy-start = (f32[3,8,32,128]{3,2,1,0:T(8,128)S(1)}, f32[3,8,32,128]{3,2,1,0:T(8,128)}, u32[]{:S(2)}) copy-start(f32[3,8,32,128]{3,2,1,0:T(8,128)} %velocity.1) | copy-start | bytes 1179652
  3.3 28.7 %all-to-all-start = ((f32[128,1,1664]{2,1,0:T(1,128)}), f32[128,1,1664]{2,1,0:T(1,128)S(1)}, u32[]{:S(2)}, u32[]{:S(2)}) async-start(f32[128,1,1664]{2,1,0:T(1,128)} %bitcast.12), calls=%async_computation | async-start | bytes 1703936 | tf_op jit(solution)/shard_map/all_to_all | solution.py:542
  15.9 23.0 %collective-permute-start.3 = (f32[3,3,32,128]{3,2,1,0:T(8,128)S(1)}, f32[3,3,32,128]{3,2,1,0:T(8,128)S(1)}, u32[]{:S(2)}, u32[]{:S(2)}) collective-permute-start(f32[3,3,32,128]{3,2,1,0:T(8,128)S(1)} %get-tuple-element.34), channel_id=1, source_target_pairs={{1,2},{2,1},{3,4},{4,3},{5,6},{6,5},{7,8},{8,7},{9,10},{10,9},{11,... | collective-permute-start | bytes 442376 | tf_op jit(solution)/shard_map/ppermute | solution.py:552
  17.6 21.3 %collective-permute-start.2 = (f32[3,3,32,128]{3,2,1,0:T(8,128)S(1)}, f32[3,3,32,128]{3,2,1,0:T(8,128)S(1)}, u32[]{:S(2)}, u32[]{:S(2)}) collective-permute-start(f32[3,3,32,128]{3,2,1,0:T(8,128)S(1)} %get-tuple-element.35), channel_id=1, source_target_pairs={{0,1},{1,0},{2,3},{3,2},{4,5},{5,4},{6,7},{7,6},{8,9},{9,8},{10,11... | collective-permute-start | bytes 442376 | tf_op jit(solution)/shard_map/ppermute | solution.py:552
  36.9 4.9 %collective-permute-start = (f32[2,32,128]{2,1,0:T(8,128)S(1)}, f32[2,32,128]{2,1,0:T(8,128)S(1)}, u32[]{:S(2)}, u32[]{:S(2)}) collective-permute-start(f32[2,32,128]{2,1,0:T(8,128)S(1)} %get-tuple-element.19), channel_id=1, source_target_pairs={{1,2},{2,1},{3,4},{4,3},{5,6},{6,5},{7,8},{8,7},{9,10},{10,9},{11,... | collective-permute-start | bytes 98312 | tf_op jit(solution)/shard_map/ppermute | solution.py:552
  38.4 3.4 %collective-permute-start.1 = (f32[2,32,128]{2,1,0:T(8,128)S(1)}, f32[2,32,128]{2,1,0:T(8,128)S(1)}, u32[]{:S(2)}, u32[]{:S(2)}) collective-permute-start(f32[2,32,128]{2,1,0:T(8,128)S(1)} %get-tuple-element.20), channel_id=1, source_target_pairs={{0,1},{1,0},{2,3},{3,2},{4,5},{5,4},{6,7},{7,6},{8,9},{9,8},{10,11... | collective-permute-start | bytes 98312 | tf_op jit(solution)/shard_map/ppermute | solution.py:552
  41.8 22.4 %copy-start.1 = (bf16[128,256]{1,0:T(8,128)(2,1)S(1)}, bf16[128,256]{1,0:T(8,128)(2,1)}, u32[]{:S(2)}) copy-start(bf16[128,256]{1,0:T(8,128)(2,1)} %get-tuple-element.33.back) | copy-start | bytes 196612

commit v6 on v5

--- a/solution.py
+++ b/solution.py
@@ -82,9 +82,9 @@
 
 
 def fill_picks(picks):
-    row = lax.broadcasted_iota(jnp.int32, (LANES, LANES), 0)
-    lane = lax.broadcasted_iota(jnp.int32, (LANES, LANES), 1)
-    apart = row - ((lane >> 3) & 3) * 32 - (lane & 7)
+    row = lax.broadcasted_iota(jnp.int32, (2 * LANES, LANES), 0)
+    lane = lax.broadcasted_iota(jnp.int32, (2 * LANES, LANES), 1)
+    apart = row - (lane >> 6) * 128 - ((lane >> 3) & 3) * 32 - (lane & 7)
     for start in range(WINDOWS):
         chosen = jnp.where(apart == start, 1.0, 0.0)
         picks[:, start * LANES : (start + 1) * LANES] = chosen.astype(bf16)
@@ -217,6 +217,22 @@
     return {p: cells[i * NY : (i + 1) * NY] for i, p in enumerate(ORDER)}
 
 
+def pack_planes(planes):
+    rows = jnp.concatenate(planes, axis=0)
+    rest = rows[48:]
+    moved = jnp.concatenate([pltpu.roll(rest, shift, 1) for shift in (96, 64, 32)], axis=0)
+    lane = lax.broadcasted_iota(jnp.int32, (48, LANES), 1)
+    return jnp.where(lane < 96, rows[:48], moved)
+
+
+def unpack_planes(packed):
+    lane = lax.broadcasted_iota(jnp.int32, (16, LANES), 1)
+    parts = [pltpu.roll(packed[16 * i : 16 * i + 16], 32 * i + 32, 1) for i in range(3)]
+    rest = jnp.where(lane < 32, parts[0], jnp.where(lane < 64, parts[1], parts[2]))
+    rows = jnp.concatenate([packed, rest], axis=0)
+    return rows[:NY], rows[NY:]
+
+
 def spread_kernel(
     got, turned_picks, far, near, grid, rows_out, weights_z, stacks, total, parts, rows, sem
 ):
@@ -259,17 +275,18 @@
     odd = lax.axis_index("slab") % 2 == 1
     for a in range(CX):
         grid[a] = planes[a]
-    for a in range(2):
-        near[a] = jnp.where(odd, planes[a], planes[CX - 2 + a])
-        far[a] = jnp.where(odd, planes[CX - 2 + a], planes[a])
+    first = pack_planes([planes[0], planes[1]])
+    last = pack_planes([planes[CX - 2], planes[CX - 1]])
+    near[...] = jnp.where(odd, first, last)
+    far[...] = jnp.where(odd, last, first)
 
 
 def spread(got, turned_picks):
     return pl.pallas_call(
         spread_kernel,
         out_shape=(
-            jax.ShapeDtypeStruct((2, NY, LANES), f32),
-            jax.ShapeDtypeStruct((2, NY, LANES), f32),
+            jax.ShapeDtypeStruct((48, LANES), f32),
+            jax.ShapeDtypeStruct((48, LANES), f32),
             jax.ShapeDtypeStruct((CX, NY, LANES), f32),
             jax.ShapeDtypeStruct((8, LANES), jnp.int32),
             jax.ShapeDtypeStruct((LANES, 2, 8, LANES), f32),
@@ -328,14 +345,12 @@
 
 def fill_table(table, planes, picks):
     cells = jnp.concatenate([packed_plane(parts) for parts in planes], axis=0).T[:96]
-    split = stack_2(cells)
-    lane = lax.broadcasted_iota(jnp.int32, (96, LANES), 1)
+    split = jnp.concatenate(split_2(cells), axis=1).astype(bf16)
     for y in range(0, WINDOWS, 2):
         wide = min(2, WINDOWS - y)
         both = dot(split, picks[:, y * LANES : (y + wide) * LANES], NN)
         for i in range(wide):
-            part = both[:, i * LANES : (i + 1) * LANES]
-            table[(y + i) * 96 : (y + i + 1) * 96] = jnp.where(lane < 64, part[:96], part[96:])
+            table[(y + i) * 96 : (y + i + 1) * 96] = both[:, i * LANES : (i + 1) * LANES]
 
 
 def fold(a, b, width):
@@ -418,7 +433,7 @@
             jax.ShapeDtypeStruct((3, CX, NY, NZ), f32),
             jax.ShapeDtypeStruct((3, len(MIDDLE), NY, NZ), f32),
             jax.ShapeDtypeStruct((6 * LANES, LANES), f32),
-            jax.ShapeDtypeStruct((LANES, WINDOWS * LANES), bf16),
+            jax.ShapeDtypeStruct((2 * LANES, WINDOWS * LANES), bf16),
             jax.ShapeDtypeStruct((3, len(HALO), NY, NZ), f32),
         ),
         in_specs=[vmem()] * 7,
@@ -451,11 +466,14 @@
     copies[1].start()
     odd = lax.axis_index("slab") % 2 == 1
 
+    behind = unpack_planes(jnp.where(odd, near[...], far[...]))
+    ahead = unpack_planes(jnp.where(odd, far[...], near[...]))
+
     def cells(p):
         if p < 0:
-            return jnp.where(odd, near[p + 2], far[p + 2])
+            return behind[p + 2]
         if p >= CX:
-            return jnp.where(odd, far[p - CX], near[p - CX])
+            return ahead[p - CX]
         return grid[p]
 
     def reader(ends, inside, low):

time: 65.4 us -> 65.3 us (level)
  other arithmetic: 1.01 us -> 0.02 us
  waiting for transfers between devices: 7.64 us -> 8.61 us
    select_n x1, other arithmetic: 1.01 us -> 0.02 us  [body(): cross = swap(jnp.where(odd, last, first), 1)]
    all_to_all x1, waiting for transfers between devices: 7.63 us -> 8.6 us  [exchange(): lax.all_to_all(values, 'slab', split_axis=0, concat_axis=0, tiled=True)]
  transfers between devices with their start and end apart: 5 -> 5, of which waited for: 1 -> 1; matrix products, arithmetic and copies ran while one was open for 2% -> 0% of each run, Pallas kernels for 12% -> 13%
where the time goes in v6:
time: 65.3 us; the launch traced here: 65 us
  starting transfers between devices  21.9 us (34%)
  blocking collectives  19.5 us (30%)
  Pallas kernels  14.2 us (22%)
  waiting for transfers between devices  8.61 us (13%)
  between operations  0.74 us (1%)
    all_to_all x1, blocking collectives, exchange(): lax.all_to_all(values, 'slab', split_axis=0, concat_axis=0, tiled=True)  19.5 us
    all_to_all x1, starting transfers between devices, exchange(): lax.all_to_all(values, 'slab', split_axis=0, concat_axis=0, tiled=True)  11.5 us
    ppermute x4, starting transfers between devices, swap(): return lax.ppermute(values, 'slab', pairs)  10.4 us
    all_to_all x1, waiting for transfers between devices, exchange(): lax.all_to_all(values, 'slab', split_axis=0, concat_axis=0, tiled=True)  8.6 us
    pallas_call x1, Pallas kernels, spread(): pl.pallas_call(spread_kernel, out_shape=(jax.ShapeDtypeStruct((48, LANES)...  4.95 us
    pallas_call x1, Pallas kernels, inner(): pl.pallas_call(inner_kernel, out_shape=(jax.ShapeDtypeStruct((3, CX, NY,...  3.03 us
    pallas_call x1, Pallas kernels, prep(): pl.pallas_call(prep_kernel, out_shape=(jax.ShapeDtypeStruct((SENT * LANES...  2.69 us
    pallas_call x1, Pallas kernels, edge(): pl.pallas_call(edge_kernel, out_shape=(jax.ShapeDtypeStruct((3, CX, NY, N...  2.23 us
  transfers between devices with their start and end apart: 5, of which 1 were waited for; matrix products, arithmetic and copies ran while one was open for 0% of the time, Pallas kernels for 13%

profile of v6, /device:TPU:1, one launch (start us, length us, event | category | flops | bytes accessed | tf_op | source)
XLA Modules:
  0.0 65.0 jit_solution(14879169870964639474)
XLA Ops:
  0.6 0.0 copy-start
  0.6 2.7 %shard_map.68 = (f32[1664,128]{1,0:T(8,128)}, bf16[128,256]{1,0:T(8,128)(2,1)}) custom-call(f32[3,128,128]{2,1,0:T(8,128)} %bitcast.13, f32[3,128,128]{2,1,0:T(8,128)} %bitcast.14, s32[1,128]{1,0:T(1,128)} %bitcast.17, s32[2,128]{1,0:T(2,128)} %bitcast.16), custom_call_target="tpu_custom_call" | custom-call | tf_op jit(solution)/shard_map/pallas_call | solution.py:164
  3.3 11.5 %all-to-all-start = ((f32[128,1,1664]{2,1,0:T(1,128)}), f32[128,1,1664]{2,1,0:T(1,128)S(1)}, u32[]{:S(2)}, u32[]{:S(2)}) async-start(f32[128,1,1664]{2,1,0:T(1,128)} %bitcast.12), calls=%async_computation | async-start | bytes 1703936 | tf_op jit(solution)/shard_map/all_to_all | solution.py:560
  14.9 0.0 copy-done
  14.9 1.7 %collective-permute-start.3 = (f32[3,3,32,128]{3,2,1,0:T(8,128)S(1)}, f32[3,3,32,128]{3,2,1,0:T(8,128)S(1)}, u32[]{:S(2)}, u32[]{:S(2)}) collective-permute-start(f32[3,3,32,128]{3,2,1,0:T(8,128)S(1)} %get-tuple-element.34), channel_id=1, source_target_pairs={{1,2},{2,1},{3,4},{4,3},{5,6},{6,5},{7,8},{8,7},{9,10},{10,9},{11,... | collective-permute-start | bytes 442376 | tf_op jit(solution)/shard_map/ppermute | solution.py:570
  16.6 6.5 %collective-permute-start.2 = (f32[3,3,32,128]{3,2,1,0:T(8,128)S(1)}, f32[3,3,32,128]{3,2,1,0:T(8,128)S(1)}, u32[]{:S(2)}, u32[]{:S(2)}) collective-permute-start(f32[3,3,32,128]{3,2,1,0:T(8,128)S(1)} %get-tuple-element.35), channel_id=1, source_target_pairs={{0,1},{1,0},{2,3},{3,2},{4,5},{5,4},{6,7},{7,6},{8,9},{9,8},{10,11... | collective-permute-start | bytes 442376 | tf_op jit(solution)/shard_map/ppermute | solution.py:570
  23.1 0.3 shard_map.69.turned_picks
  23.4 8.6 %all-to-all-done = f32[128,1,1664]{2,1,0:T(1,128)S(1)} async-done(((f32[128,1,1664]{2,1,0:T(1,128)}), f32[128,1,1664]{2,1,0:T(1,128)S(1)}, u32[]{:S(2)}, u32[]{:S(2)}) %all-to-all-start) | async-done | bytes 852000 | tf_op jit(solution)/shard_map/all_to_all | solution.py:560
  32.0 5.0 %shard_map.70 = (f32[48,128]{1,0:T(8,128)S(1)}, f32[48,128]{1,0:T(8,128)S(1)}, f32[8,32,128]{2,1,0:T(8,128)S(1)}, s32[8,128]{1,0:T(8,128)S(1)}, f32[128,2,8,128]...) custom-call(f32[1664,128]{1,0:T(8,128)S(1)} %bitcast.9, bf16[3200,256]{1,0:T(8,128)(2,1)S(1)} %shard_map.69.turned_picks), custom_call_target="tpu_custom_call" | custom-call | tf_op jit(solution)/shard_map/pallas_call | solution.py:285
  37.0 1.5 %collective-permute-start = (f32[48,128]{1,0:T(8,128)S(1)}, f32[48,128]{1,0:T(8,128)S(1)}, u32[]{:S(2)}, u32[]{:S(2)}) collective-permute-start(f32[48,128]{1,0:T(8,128)S(1)} %get-tuple-element.19), channel_id=1, source_target_pairs={{1,2},{2,1},{3,4},{4,3},{5,6},{6,5},{7,8},{8,7},{9,10},{10,9},{11,... | collective-permute-start | bytes 73736 | tf_op jit(solution)/shard_map/ppermute | solution.py:570
  38.5 0.7 %collective-permute-start.1 = (f32[48,128]{1,0:T(8,128)S(1)}, f32[48,128]{1,0:T(8,128)S(1)}, u32[]{:S(2)}, u32[]{:S(2)}) collective-permute-start(f32[48,128]{1,0:T(8,128)S(1)} %get-tuple-element.20), channel_id=1, source_target_pairs={{0,1},{1,0},{2,3},{3,2},{4,5},{5,4},{6,7},{7,6},{8,9},{9,8},{10,11... | collective-permute-start | bytes 73736 | tf_op jit(solution)/shard_map/ppermute | solution.py:570
  39.2 0.0 collective-permute-done.3.cross
  39.2 0.0 collective-permute-done.2.same
  39.2 3.0 %shard_map.71 = (f32[3,8,32,128]{3,2,1,0:T(8,128)S(1)}, f32[3,8,32,128]{3,2,1,0:T(8,128)S(1)}, f32[3,4,32,128]{3,2,1,0:T(8,128)S(1)}, f32[768,128]{1,0:T(8,128)S...) custom-call(f32[3,8,32,128]{3,2,1,0:T(8,128)S(1)} %copy-done, ...), custom_call_target="tpu_custom_call" | custom-call | flops 6000000000 | bytes 8000000 | tf_op jit(solution)/shard_map/pallas_call | solution.py:429
  42.2 0.0 collective-permute-done.far
  42.2 0.0 collective-permute-done.1.near
  42.3 0.0 copy-start.1
  42.3 2.2 %shard_map.72 = (f32[3,8,32,128]{3,2,1,0:T(8,128)}, f32[768,128]{1,0:T(8,128)S(1)}) custom-call(f32[48,128]{1,0:T(8,128)S(1)} %collective-permute-done.far, f32[48,128]{1,0:T(8,128)S(1)} %collective-permute-done.1.near, f32[8,32,128]{2,1,0:T(8,128)S(1)} %get-tuple-element.21.grid, s32[8,128]{1,0:T(8,128)S(1)} %get-tuple-element.22.rows_in, ...), custom_call_target="tpu_custom_call" | custom-call | tf_op jit(solution)/shard_map/pallas_call | solution.py:517
  44.5 19.5 %all_to_all.10 = f32[128,1,768]{2,1,0:T(1,128)S(1)} all-to-all(f32[128,1,768]{2,1,0:T(1,128)S(1)} %bitcast.11), channel_id=1, replica_groups=mesh['slab'=128] {'slab'}, dimensions={0} | all-to-all | bytes 786432 | tf_op jit(solution)/shard_map/all_to_all | solution.py:560
  64.0 0.0 copy-done.1
  64.0 1.0 %shard_map.73 = f32[3,128,128]{2,1,0:T(8,128)} custom-call(f32[768,128]{1,0:T(8,128)S(1)} %bitcast.10, bf16[128,256]{1,0:T(8,128)(2,1)S(1)} %copy-done.1), custom_call_target="tpu_custom_call" | custom-call | tf_op jit(solution)/shard_map/pallas_call | solution.py:548
  (1 shorter events, 0.0 us)
Async XLA Ops:
  0.6 14.2 %copy-start = (f32[3,8,32,128]{3,2,1,0:T(8,128)S(1)}, f32[3,8,32,128]{3,2,1,0:T(8,128)}, u32[]{:S(2)}) copy-start(f32[3,8,32,128]{3,2,1,0:T(8,128)} %velocity.1) | copy-start | bytes 1179652
  3.3 28.7 %all-to-all-start = ((f32[128,1,1664]{2,1,0:T(1,128)}), f32[128,1,1664]{2,1,0:T(1,128)S(1)}, u32[]{:S(2)}, u32[]{:S(2)}) async-start(f32[128,1,1664]{2,1,0:T(1,128)} %bitcast.12), calls=%async_computation | async-start | bytes 1703936 | tf_op jit(solution)/shard_map/all_to_all | solution.py:560
  14.9 24.3 %collective-permute-start.3 = (f32[3,3,32,128]{3,2,1,0:T(8,128)S(1)}, f32[3,3,32,128]{3,2,1,0:T(8,128)S(1)}, u32[]{:S(2)}, u32[]{:S(2)}) collective-permute-start(f32[3,3,32,128]{3,2,1,0:T(8,128)S(1)} %get-tuple-element.34), channel_id=1, source_target_pairs={{1,2},{2,1},{3,4},{4,3},{5,6},{6,5},{7,8},{8,7},{9,10},{10,9},{11,... | collective-permute-start | bytes 442376 | tf_op jit(solution)/shard_map/ppermute | solution.py:570
  16.6 22.6 %collective-permute-start.2 = (f32[3,3,32,128]{3,2,1,0:T(8,128)S(1)}, f32[3,3,32,128]{3,2,1,0:T(8,128)S(1)}, u32[]{:S(2)}, u32[]{:S(2)}) collective-permute-start(f32[3,3,32,128]{3,2,1,0:T(8,128)S(1)} %get-tuple-element.35), channel_id=1, source_target_pairs={{0,1},{1,0},{2,3},{3,2},{4,5},{5,4},{6,7},{7,6},{8,9},{9,8},{10,11... | collective-permute-start | bytes 442376 | tf_op jit(solution)/shard_map/ppermute | solution.py:570
  37.0 5.3 %collective-permute-start = (f32[48,128]{1,0:T(8,128)S(1)}, f32[48,128]{1,0:T(8,128)S(1)}, u32[]{:S(2)}, u32[]{:S(2)}) collective-permute-start(f32[48,128]{1,0:T(8,128)S(1)} %get-tuple-element.19), channel_id=1, source_target_pairs={{1,2},{2,1},{3,4},{4,3},{5,6},{6,5},{7,8},{8,7},{9,10},{10,9},{11,... | collective-permute-start | bytes 73736 | tf_op jit(solution)/shard_map/ppermute | solution.py:570
  38.5 3.8 %collective-permute-start.1 = (f32[48,128]{1,0:T(8,128)S(1)}, f32[48,128]{1,0:T(8,128)S(1)}, u32[]{:S(2)}, u32[]{:S(2)}) collective-permute-start(f32[48,128]{1,0:T(8,128)S(1)} %get-tuple-element.20), channel_id=1, source_target_pairs={{0,1},{1,0},{2,3},{3,2},{4,5},{5,4},{6,7},{7,6},{8,9},{9,8},{10,11... | collective-permute-start | bytes 73736 | tf_op jit(solution)/shard_map/ppermute | solution.py:570
  42.3 21.8 %copy-start.1 = (bf16[128,256]{1,0:T(8,128)(2,1)S(1)}, bf16[128,256]{1,0:T(8,128)(2,1)}, u32[]{:S(2)}) copy-start(bf16[128,256]{1,0:T(8,128)(2,1)} %get-tuple-element.33.back) | copy-start | bytes 196612

commit v7 on v6

--- a/solution.py
+++ b/solution.py
@@ -77,7 +77,7 @@
 HALO = (-2, -1, CX, CX + 1)
 MIDDLE = (2, 3, 4, 5)
 ORDER = EDGES + MIDDLE
-SENT = 13
+SENT = 12
 REACH = (CX - 4.0, 5.0, 5.0)
 
 
@@ -131,23 +131,16 @@
     both = jnp.concatenate([first, second], axis=0).astype(bf16)
     copies[1].wait()
     offsets = offset[...].astype(f32)
-    rows = lax.broadcasted_iota(jnp.int32, (8, LANES), 0)
-    spread_y = jnp.broadcast_to(offsets[0:1], (8, LANES))
-    spread_z = jnp.broadcast_to(offsets[1:2], (8, LANES))
-    tail = jnp.zeros((LANES, LANES), f32)
-    empty = jnp.zeros((LANES - 8, LANES), f32)
-    for slot, chosen in ((0, first), (1, second)):
-        table = jnp.where(rows == 2 * slot, spread_y, 0.0) + jnp.where(
-            rows == 2 * slot + 1, spread_z, 0.0
-        )
-        table = jnp.concatenate([table, empty], axis=0).astype(bf16)
-        tail = tail + dot(chosen.astype(bf16), table, NT)
-    out[pl.ds(12, LANES, stride=SENT), :] = tail
+    corners = [None] + [
+        jnp.broadcast_to(offsets[i : i + 1], (LANES, LANES)).T for i in range(2)
+    ]
     for quantity in range(6):
         if quantity % 3 == 0:
             copies[2 + quantity // 3].wait()
         if quantity < 3:
             source = coords[quantity] * REACH[quantity]
+            if quantity:
+                source = source + corners[quantity]
         else:
             source = force[quantity - 3]
         high, middle, low = split_3(source)
@@ -234,19 +227,23 @@
 
 
 def spread_kernel(
-    got, turned_picks, far, near, grid, rows_out, weights_z, stacks, total, parts, rows, sem
+    got, turned_picks, far, near, grid, rows_out, weights_z, stacks, total, places, parts, rows, sem
 ):
-    tail = got[pl.ds(12, LANES, stride=SENT), :].T
-    y = jnp.concatenate([tail[0:1], tail[2:3]], axis=0)
-    z = jnp.concatenate([tail[1:2], tail[3:4]], axis=0)
-    y = jnp.clip(y - 1.0, 0.0, WINDOWS - 1.0)
-    z = jnp.clip(z - 1.0, 0.0, WINDOWS - 1.0)
-    start = (y * 96.0 + z).astype(jnp.int32)
-    rows_out[...] = jnp.concatenate([start, jnp.zeros((6, LANES), jnp.int32)], axis=0)
+    lane = lax.broadcasted_iota(jnp.int32, (LANES, LANES), 1)
+    start = jnp.zeros((LANES, LANES), f32)
+    for slot in range(2):
+        firsts = []
+        for dim in (1, 2):
+            place = got[pl.ds(slot * 6 + dim, LANES, stride=SENT), :]
+            least = jnp.floor(jnp.min(place, axis=1, keepdims=True)) - 1.0
+            firsts.append(jnp.clip(least, 0.0, WINDOWS - 1.0))
+            places[slot * 2 + dim - 1] = place - firsts[-1]
+        start = jnp.where(lane == slot, firsts[0] * 96.0 + firsts[1], start)
+    rows_out[...] = start.T[:8].astype(jnp.int32)
     copy = pltpu.make_async_copy(rows_out, rows, sem)
     copy.start()
     total[...] = jnp.zeros_like(total)
-    taps = lax.broadcasted_iota(jnp.int32, (8, LANES), 0).astype(f32) - 1.0
+    taps = lax.broadcasted_iota(jnp.int32, (8, LANES), 0).astype(f32)
 
     def compute(index):
         for sub in range(GROUP):
@@ -254,9 +251,9 @@
             load, stack = [], []
             for slot in range(2):
                 source = device * SENT + slot * 6
-                weight_x, weight_y, weight_z = [
-                    phi(taps - got[pl.ds(source + dim, 1), :]) for dim in range(3)
-                ]
+                weight_x = phi(taps - 1.0 - got[pl.ds(source, 1), :])
+                weight_y = phi(taps - places[slot * 2, pl.ds(device, 1), :])
+                weight_z = phi(taps - places[slot * 2 + 1, pl.ds(device, 1), :])
                 weights_z[device, slot] = weight_z
                 stack.append(joint_stack(weight_x, weight_y))
                 load += [got[pl.ds(source + 3 + c, 1), :] * weight_z for c in range(3)]
@@ -296,6 +293,7 @@
         out_specs=(vmem(),) * 6,
         scratch_shapes=[
             pltpu.VMEM((TABLE, LANES), f32),
+            pltpu.VMEM((4, LANES, LANES), f32),
             pltpu.VMEM((GROUP, 48, LANES), f32),
             pltpu.SMEM((8, LANES), jnp.int32),
             pltpu.SemaphoreType.DMA,

time: 65.3 us -> 64.6 us (0.989)
  waiting for transfers between devices: 8.61 us -> 7.95 us
    all_to_all x1, waiting for transfers between devices: 8.6 us -> 7.94 us  [exchange(): lax.all_to_all(values, 'slab', split_axis=0, concat_axis=0, tiled=True)]
where the time goes in v7:
time: 64.6 us; the launch traced here: 64.4 us
  starting transfers between devices  21.8 us (34%)
  blocking collectives  19.7 us (30%)
  Pallas kernels  14.3 us (22%)
  waiting for transfers between devices  7.95 us (12%)
  between operations  0.74 us (1%)
    all_to_all x1, blocking collectives, exchange(): lax.all_to_all(values, 'slab', split_axis=0, concat_axis=0, tiled=True)  19.7 us
    all_to_all x1, starting transfers between devices, exchange(): lax.all_to_all(values, 'slab', split_axis=0, concat_axis=0, tiled=True)  11.5 us
    ppermute x4, starting transfers between devices, swap(): return lax.ppermute(values, 'slab', pairs)  10.2 us
    all_to_all x1, waiting for transfers between devices, exchange(): lax.all_to_all(values, 'slab', split_axis=0, concat_axis=0, tiled=True)  7.94 us
    pallas_call x1, Pallas kernels, spread(): pl.pallas_call(spread_kernel, out_shape=(jax.ShapeDtypeStruct((48, LANES)...  5.1 us
    pallas_call x1, Pallas kernels, inner(): pl.pallas_call(inner_kernel, out_shape=(jax.ShapeDtypeStruct((3, CX, NY,...  3.04 us
    pallas_call x1, Pallas kernels, prep(): pl.pallas_call(prep_kernel, out_shape=(jax.ShapeDtypeStruct((SENT * LANES...  2.65 us
    pallas_call x1, Pallas kernels, edge(): pl.pallas_call(edge_kernel, out_shape=(jax.ShapeDtypeStruct((3, CX, NY, N...  2.24 us
  transfers between devices with their start and end apart: 5, of which 1 were waited for; matrix products, arithmetic and copies ran while one was open for 0% of the time, Pallas kernels for 13%

profile of v7, /device:TPU:1, one launch (start us, length us, event | category | flops | bytes accessed | tf_op | source)
XLA Modules:
  0.0 64.4 jit_solution(15306922300294662352)
XLA Ops:
  0.6 0.0 copy-start
  0.6 2.6 %shard_map.68 = (f32[1536,128]{1,0:T(8,128)}, bf16[128,256]{1,0:T(8,128)(2,1)}) custom-call(f32[3,128,128]{2,1,0:T(8,128)} %bitcast.13, f32[3,128,128]{2,1,0:T(8,128)} %bitcast.14, s32[1,128]{1,0:T(1,128)} %bitcast.17, s32[2,128]{1,0:T(2,128)} %bitcast.16), custom_call_target="tpu_custom_call" | custom-call | tf_op jit(solution)/shard_map/pallas_call | solution.py:157
  3.3 11.5 %all-to-all-start = ((f32[128,1,1536]{2,1,0:T(1,128)}), f32[128,1,1536]{2,1,0:T(1,128)S(1)}, u32[]{:S(2)}, u32[]{:S(2)}) async-start(f32[128,1,1536]{2,1,0:T(1,128)} %bitcast.12), calls=%async_computation | async-start | bytes 1572864 | tf_op jit(solution)/shard_map/all_to_all | solution.py:558
  14.8 0.0 copy-done
  14.9 1.7 %collective-permute-start.3 = (f32[3,3,32,128]{3,2,1,0:T(8,128)S(1)}, f32[3,3,32,128]{3,2,1,0:T(8,128)S(1)}, u32[]{:S(2)}, u32[]{:S(2)}) collective-permute-start(f32[3,3,32,128]{3,2,1,0:T(8,128)S(1)} %get-tuple-element.34), channel_id=1, source_target_pairs={{1,2},{2,1},{3,4},{4,3},{5,6},{6,5},{7,8},{8,7},{9,10},{10,9},{11,... | collective-permute-start | bytes 442376 | tf_op jit(solution)/shard_map/ppermute | solution.py:568
  16.6 6.5 %collective-permute-start.2 = (f32[3,3,32,128]{3,2,1,0:T(8,128)S(1)}, f32[3,3,32,128]{3,2,1,0:T(8,128)S(1)}, u32[]{:S(2)}, u32[]{:S(2)}) collective-permute-start(f32[3,3,32,128]{3,2,1,0:T(8,128)S(1)} %get-tuple-element.35), channel_id=1, source_target_pairs={{0,1},{1,0},{2,3},{3,2},{4,5},{5,4},{6,7},{7,6},{8,9},{9,8},{10,11... | collective-permute-start | bytes 442376 | tf_op jit(solution)/shard_map/ppermute | solution.py:568
  23.1 0.3 shard_map.69.turned_picks
  23.4 7.9 %all-to-all-done = f32[128,1,1536]{2,1,0:T(1,128)S(1)} async-done(((f32[128,1,1536]{2,1,0:T(1,128)}), f32[128,1,1536]{2,1,0:T(1,128)S(1)}, u32[]{:S(2)}, u32[]{:S(2)}) %all-to-all-start) | async-done | bytes 786464 | tf_op jit(solution)/shard_map/all_to_all | solution.py:558
  31.3 5.1 %shard_map.70 = (f32[48,128]{1,0:T(8,128)S(1)}, f32[48,128]{1,0:T(8,128)S(1)}, f32[8,32,128]{2,1,0:T(8,128)S(1)}, s32[8,128]{1,0:T(8,128)S(1)}, f32[128,2,8,128]...) custom-call(f32[1536,128]{1,0:T(8,128)S(1)} %bitcast.9, bf16[3200,256]{1,0:T(8,128)(2,1)S(1)} %shard_map.69.turned_picks), custom_call_target="tpu_custom_call" | custom-call | tf_op jit(solution)/shard_map/pallas_call | solution.py:282
  36.4 1.5 %collective-permute-start = (f32[48,128]{1,0:T(8,128)S(1)}, f32[48,128]{1,0:T(8,128)S(1)}, u32[]{:S(2)}, u32[]{:S(2)}) collective-permute-start(f32[48,128]{1,0:T(8,128)S(1)} %get-tuple-element.19), channel_id=1, source_target_pairs={{1,2},{2,1},{3,4},{4,3},{5,6},{6,5},{7,8},{8,7},{9,10},{10,9},{11,... | collective-permute-start | bytes 73736 | tf_op jit(solution)/shard_map/ppermute | solution.py:568
  37.9 0.6 collective-permute-start.1
  38.4 0.0 collective-permute-done.3.cross
  38.5 0.0 collective-permute-done.2.same
  38.5 3.0 %shard_map.71 = (f32[3,8,32,128]{3,2,1,0:T(8,128)S(1)}, f32[3,8,32,128]{3,2,1,0:T(8,128)S(1)}, f32[3,4,32,128]{3,2,1,0:T(8,128)S(1)}, f32[768,128]{1,0:T(8,128)S...) custom-call(f32[3,8,32,128]{3,2,1,0:T(8,128)S(1)} %copy-done, ...), custom_call_target="tpu_custom_call" | custom-call | flops 6000000000 | bytes 8000000 | tf_op jit(solution)/shard_map/pallas_call | solution.py:427
  41.5 0.0 collective-permute-done.far
  41.5 0.0 collective-permute-done.1.near
  41.5 0.0 copy-start.1
  41.5 2.2 %shard_map.72 = (f32[3,8,32,128]{3,2,1,0:T(8,128)}, f32[768,128]{1,0:T(8,128)S(1)}) custom-call(f32[48,128]{1,0:T(8,128)S(1)} %collective-permute-done.far, f32[48,128]{1,0:T(8,128)S(1)} %collective-permute-done.1.near, f32[8,32,128]{2,1,0:T(8,128)S(1)} %get-tuple-element.21.grid, s32[8,128]{1,0:T(8,128)S(1)} %get-tuple-element.22.rows_in, ...), custom_call_target="tpu_custom_call" | custom-call | tf_op jit(solution)/shard_map/pallas_call | solution.py:515
  43.8 19.7 %all_to_all.10 = f32[128,1,768]{2,1,0:T(1,128)S(1)} all-to-all(f32[128,1,768]{2,1,0:T(1,128)S(1)} %bitcast.11), channel_id=1, replica_groups=mesh['slab'=128] {'slab'}, dimensions={0} | all-to-all | bytes 786432 | tf_op jit(solution)/shard_map/all_to_all | solution.py:558
  63.4 0.0 copy-done.1
  63.4 1.0 %shard_map.73 = f32[3,128,128]{2,1,0:T(8,128)} custom-call(f32[768,128]{1,0:T(8,128)S(1)} %bitcast.10, bf16[128,256]{1,0:T(8,128)(2,1)S(1)} %copy-done.1), custom_call_target="tpu_custom_call" | custom-call | tf_op jit(solution)/shard_map/pallas_call | solution.py:546
  (1 shorter events, 0.0 us)
Async XLA Ops:
  0.6 14.2 %copy-start = (f32[3,8,32,128]{3,2,1,0:T(8,128)S(1)}, f32[3,8,32,128]{3,2,1,0:T(8,128)}, u32[]{:S(2)}) copy-start(f32[3,8,32,128]{3,2,1,0:T(8,128)} %velocity.1) | copy-start | bytes 1179652
  3.3 28.0 %all-to-all-start = ((f32[128,1,1536]{2,1,0:T(1,128)}), f32[128,1,1536]{2,1,0:T(1,128)S(1)}, u32[]{:S(2)}, u32[]{:S(2)}) async-start(f32[128,1,1536]{2,1,0:T(1,128)} %bitcast.12), calls=%async_computation | async-start | bytes 1572864 | tf_op jit(solution)/shard_map/all_to_all | solution.py:558
  14.9 23.6 %collective-permute-start.3 = (f32[3,3,32,128]{3,2,1,0:T(8,128)S(1)}, f32[3,3,32,128]{3,2,1,0:T(8,128)S(1)}, u32[]{:S(2)}, u32[]{:S(2)}) collective-permute-start(f32[3,3,32,128]{3,2,1,0:T(8,128)S(1)} %get-tuple-element.34), channel_id=1, source_target_pairs={{1,2},{2,1},{3,4},{4,3},{5,6},{6,5},{7,8},{8,7},{9,10},{10,9},{11,... | collective-permute-start | bytes 442376 | tf_op jit(solution)/shard_map/ppermute | solution.py:568
  16.6 21.9 %collective-permute-start.2 = (f32[3,3,32,128]{3,2,1,0:T(8,128)S(1)}, f32[3,3,32,128]{3,2,1,0:T(8,128)S(1)}, u32[]{:S(2)}, u32[]{:S(2)}) collective-permute-start(f32[3,3,32,128]{3,2,1,0:T(8,128)S(1)} %get-tuple-element.35), channel_id=1, source_target_pairs={{0,1},{1,0},{2,3},{3,2},{4,5},{5,4},{6,7},{7,6},{8,9},{9,8},{10,11... | collective-permute-start | bytes 442376 | tf_op jit(solution)/shard_map/ppermute | solution.py:568
  36.4 5.1 %collective-permute-start = (f32[48,128]{1,0:T(8,128)S(1)}, f32[48,128]{1,0:T(8,128)S(1)}, u32[]{:S(2)}, u32[]{:S(2)}) collective-permute-start(f32[48,128]{1,0:T(8,128)S(1)} %get-tuple-element.19), channel_id=1, source_target_pairs={{1,2},{2,1},{3,4},{4,3},{5,6},{6,5},{7,8},{8,7},{9,10},{10,9},{11,... | collective-permute-start | bytes 73736 | tf_op jit(solution)/shard_map/ppermute | solution.py:568
  37.9 3.6 %collective-permute-start.1 = (f32[48,128]{1,0:T(8,128)S(1)}, f32[48,128]{1,0:T(8,128)S(1)}, u32[]{:S(2)}, u32[]{:S(2)}) collective-permute-start(f32[48,128]{1,0:T(8,128)S(1)} %get-tuple-element.20), channel_id=1, source_target_pairs={{0,1},{1,0},{2,3},{3,2},{4,5},{5,4},{6,7},{7,6},{8,9},{9,8},{10,11... | collective-permute-start | bytes 73736 | tf_op jit(solution)/shard_map/ppermute | solution.py:568
  41.5 21.9 %copy-start.1 = (bf16[128,256]{1,0:T(8,128)(2,1)S(1)}, bf16[128,256]{1,0:T(8,128)(2,1)}, u32[]{:S(2)}) copy-start(bf16[128,256]{1,0:T(8,128)(2,1)} %get-tuple-element.33.back) | copy-start | bytes 196612

commit v8 on v7

--- a/solution.py
+++ b/solution.py
@@ -210,22 +210,6 @@
     return {p: cells[i * NY : (i + 1) * NY] for i, p in enumerate(ORDER)}
 
 
-def pack_planes(planes):
-    rows = jnp.concatenate(planes, axis=0)
-    rest = rows[48:]
-    moved = jnp.concatenate([pltpu.roll(rest, shift, 1) for shift in (96, 64, 32)], axis=0)
-    lane = lax.broadcasted_iota(jnp.int32, (48, LANES), 1)
-    return jnp.where(lane < 96, rows[:48], moved)
-
-
-def unpack_planes(packed):
-    lane = lax.broadcasted_iota(jnp.int32, (16, LANES), 1)
-    parts = [pltpu.roll(packed[16 * i : 16 * i + 16], 32 * i + 32, 1) for i in range(3)]
-    rest = jnp.where(lane < 32, parts[0], jnp.where(lane < 64, parts[1], parts[2]))
-    rows = jnp.concatenate([packed, rest], axis=0)
-    return rows[:NY], rows[NY:]
-
-
 def spread_kernel(
     got, turned_picks, far, near, grid, rows_out, weights_z, stacks, total, places, parts, rows, sem
 ):
@@ -272,18 +256,17 @@
     odd = lax.axis_index("slab") % 2 == 1
     for a in range(CX):
         grid[a] = planes[a]
-    first = pack_planes([planes[0], planes[1]])
-    last = pack_planes([planes[CX - 2], planes[CX - 1]])
-    near[...] = jnp.where(odd, first, last)
-    far[...] = jnp.where(odd, last, first)
+    for a in range(2):
+        near[a] = jnp.where(odd, planes[a], planes[CX - 2 + a])
+        far[a] = jnp.where(odd, planes[CX - 2 + a], planes[a])
 
 
 def spread(got, turned_picks):
     return pl.pallas_call(
         spread_kernel,
         out_shape=(
-            jax.ShapeDtypeStruct((48, LANES), f32),
-            jax.ShapeDtypeStruct((48, LANES), f32),
+            jax.ShapeDtypeStruct((2, NY, LANES), f32),
+            jax.ShapeDtypeStruct((2, NY, LANES), f32),
             jax.ShapeDtypeStruct((CX, NY, LANES), f32),
             jax.ShapeDtypeStruct((8, LANES), jnp.int32),
             jax.ShapeDtypeStruct((LANES, 2, 8, LANES), f32),
@@ -464,14 +447,11 @@
     copies[1].start()
     odd = lax.axis_index("slab") % 2 == 1
 
-    behind = unpack_planes(jnp.where(odd, near[...], far[...]))
-    ahead = unpack_planes(jnp.where(odd, far[...], near[...]))
-
     def cells(p):
         if p < 0:
-            return behind[p + 2]
+            return jnp.where(odd, near[p + 2], far[p + 2])
         if p >= CX:
-            return ahead[p - CX]
+            return jnp.where(odd, far[p - CX], near[p - CX])
         return grid[p]
 
     def reader(ends, inside, low):

time: 64.6 us -> 64.7 us (level)
  no operation moved by 1% of the time
where the time goes in v8:
time: 64.7 us; the launch traced here: 64.6 us
  starting transfers between devices  21.8 us (34%)
  blocking collectives  19.8 us (31%)
  Pallas kernels  14.2 us (22%)
  waiting for transfers between devices  7.95 us (12%)
  between operations  0.74 us (1%)
    all_to_all x1, blocking collectives, exchange(): lax.all_to_all(values, 'slab', split_axis=0, concat_axis=0, tiled=True)  19.8 us
    all_to_all x1, starting transfers between devices, exchange(): lax.all_to_all(values, 'slab', split_axis=0, concat_axis=0, tiled=True)  11.5 us
    ppermute x4, starting transfers between devices, swap(): return lax.ppermute(values, 'slab', pairs)  10.2 us
    all_to_all x1, waiting for transfers between devices, exchange(): lax.all_to_all(values, 'slab', split_axis=0, concat_axis=0, tiled=True)  7.94 us
    pallas_call x1, Pallas kernels, spread(): pl.pallas_call(spread_kernel, out_shape=(jax.ShapeDtypeStruct((2, NY, LAN...  5.03 us
    pallas_call x1, Pallas kernels, inner(): pl.pallas_call(inner_kernel, out_shape=(jax.ShapeDtypeStruct((3, CX, NY,...  3.04 us
    pallas_call x1, Pallas kernels, prep(): pl.pallas_call(prep_kernel, out_shape=(jax.ShapeDtypeStruct((SENT * LANES...  2.65 us
    pallas_call x1, Pallas kernels, edge(): pl.pallas_call(edge_kernel, out_shape=(jax.ShapeDtypeStruct((3, CX, NY, N...  2.24 us
  transfers between devices with their start and end apart: 5, of which 1 were waited for; matrix products, arithmetic and copies ran while one was open for 0% of the time, Pallas kernels for 13%

profile of v8, /device:TPU:1, one launch (start us, length us, event | category | flops | bytes accessed | tf_op | source)
XLA Modules:
  0.0 64.6 jit_solution(2427718907895706605)
XLA Ops:
  0.6 0.0 copy-start
  0.6 2.6 %shard_map.68 = (f32[1536,128]{1,0:T(8,128)}, bf16[128,256]{1,0:T(8,128)(2,1)}) custom-call(f32[3,128,128]{2,1,0:T(8,128)} %bitcast.13, f32[3,128,128]{2,1,0:T(8,128)} %bitcast.14, s32[1,128]{1,0:T(1,128)} %bitcast.17, s32[2,128]{1,0:T(2,128)} %bitcast.16), custom_call_target="tpu_custom_call" | custom-call | tf_op jit(solution)/shard_map/pallas_call | solution.py:157
  3.3 11.5 %all-to-all-start = ((f32[128,1,1536]{2,1,0:T(1,128)}), f32[128,1,1536]{2,1,0:T(1,128)S(1)}, u32[]{:S(2)}, u32[]{:S(2)}) async-start(f32[128,1,1536]{2,1,0:T(1,128)} %bitcast.12), calls=%async_computation | async-start | bytes 1572864 | tf_op jit(solution)/shard_map/all_to_all | solution.py:538
  14.8 0.0 copy-done
  14.9 1.7 %collective-permute-start.3 = (f32[3,3,32,128]{3,2,1,0:T(8,128)S(1)}, f32[3,3,32,128]{3,2,1,0:T(8,128)S(1)}, u32[]{:S(2)}, u32[]{:S(2)}) collective-permute-start(f32[3,3,32,128]{3,2,1,0:T(8,128)S(1)} %get-tuple-element.34), channel_id=1, source_target_pairs={{1,2},{2,1},{3,4},{4,3},{5,6},{6,5},{7,8},{8,7},{9,10},{10,9},{11,... | collective-permute-start | bytes 442376 | tf_op jit(solution)/shard_map/ppermute | solution.py:548
  16.6 6.5 %collective-permute-start.2 = (f32[3,3,32,128]{3,2,1,0:T(8,128)S(1)}, f32[3,3,32,128]{3,2,1,0:T(8,128)S(1)}, u32[]{:S(2)}, u32[]{:S(2)}) collective-permute-start(f32[3,3,32,128]{3,2,1,0:T(8,128)S(1)} %get-tuple-element.35), channel_id=1, source_target_pairs={{0,1},{1,0},{2,3},{3,2},{4,5},{5,4},{6,7},{7,6},{8,9},{9,8},{10,11... | collective-permute-start | bytes 442376 | tf_op jit(solution)/shard_map/ppermute | solution.py:548
  23.1 0.3 shard_map.69.turned_picks
  23.4 7.9 %all-to-all-done = f32[128,1,1536]{2,1,0:T(1,128)S(1)} async-done(((f32[128,1,1536]{2,1,0:T(1,128)}), f32[128,1,1536]{2,1,0:T(1,128)S(1)}, u32[]{:S(2)}, u32[]{:S(2)}) %all-to-all-start) | async-done | bytes 786464 | tf_op jit(solution)/shard_map/all_to_all | solution.py:538
  31.3 5.0 %shard_map.70 = (f32[2,32,128]{2,1,0:T(8,128)S(1)}, f32[2,32,128]{2,1,0:T(8,128)S(1)}, f32[8,32,128]{2,1,0:T(8,128)S(1)}, s32[8,128]{1,0:T(8,128)S(1)}, f32[128,...) custom-call(f32[1536,128]{1,0:T(8,128)S(1)} %bitcast.9, bf16[3200,256]{1,0:T(8,128)(2,1)S(1)} %shard_map.69.turned_picks), custom_call_target="tpu_custom_call" | custom-call | tf_op jit(solution)/shard_map/pallas_call | solution.py:265
  36.3 1.5 %collective-permute-start = (f32[2,32,128]{2,1,0:T(8,128)S(1)}, f32[2,32,128]{2,1,0:T(8,128)S(1)}, u32[]{:S(2)}, u32[]{:S(2)}) collective-permute-start(f32[2,32,128]{2,1,0:T(8,128)S(1)} %get-tuple-element.19), channel_id=1, source_target_pairs={{1,2},{2,1},{3,4},{4,3},{5,6},{6,5},{7,8},{8,7},{9,10},{10,9},{11,... | collective-permute-start | bytes 98312 | tf_op jit(solution)/shard_map/ppermute | solution.py:548
  37.8 0.6 collective-permute-start.1
  38.4 0.0 collective-permute-done.3.cross
  38.4 0.0 collective-permute-done.2.same
  38.4 3.0 %shard_map.71 = (f32[3,8,32,128]{3,2,1,0:T(8,128)S(1)}, f32[3,8,32,128]{3,2,1,0:T(8,128)S(1)}, f32[3,4,32,128]{3,2,1,0:T(8,128)S(1)}, f32[768,128]{1,0:T(8,128)S...) custom-call(f32[3,8,32,128]{3,2,1,0:T(8,128)S(1)} %copy-done, ...), custom_call_target="tpu_custom_call" | custom-call | flops 6000000000 | bytes 8000000 | tf_op jit(solution)/shard_map/pallas_call | solution.py:410
  41.4 0.0 collective-permute-done.far
  41.4 0.0 collective-permute-done.1.near
  41.5 0.0 copy-start.1
  41.5 2.2 %shard_map.72 = (f32[3,8,32,128]{3,2,1,0:T(8,128)}, f32[768,128]{1,0:T(8,128)S(1)}) custom-call(f32[2,32,128]{2,1,0:T(8,128)S(1)} %collective-permute-done.far, f32[2,32,128]{2,1,0:T(8,128)S(1)} %collective-permute-done.1.near, f32[8,32,128]{2,1,0:T(8,128)S(1)} %get-tuple-element.21.grid, s32[8,128]{1,0:T(8,128)S(1)} %get-tuple-element.22.rows_in, ...), custom_call_target="tpu_custom_call" | custom-call | tf_op jit(solution)/shard_map/pallas_call | solution.py:495
  43.7 19.8 %all_to_all.10 = f32[128,1,768]{2,1,0:T(1,128)S(1)} all-to-all(f32[128,1,768]{2,1,0:T(1,128)S(1)} %bitcast.11), channel_id=1, replica_groups=mesh['slab'=128] {'slab'}, dimensions={0} | all-to-all | bytes 786432 | tf_op jit(solution)/shard_map/all_to_all | solution.py:538
  63.6 0.0 copy-done.1
  63.6 1.0 %shard_map.73 = f32[3,128,128]{2,1,0:T(8,128)} custom-call(f32[768,128]{1,0:T(8,128)S(1)} %bitcast.10, bf16[128,256]{1,0:T(8,128)(2,1)S(1)} %copy-done.1), custom_call_target="tpu_custom_call" | custom-call | tf_op jit(solution)/shard_map/pallas_call | solution.py:526
  (1 shorter events, 0.0 us)
Async XLA Ops:
  0.6 14.2 %copy-start = (f32[3,8,32,128]{3,2,1,0:T(8,128)S(1)}, f32[3,8,32,128]{3,2,1,0:T(8,128)}, u32[]{:S(2)}) copy-start(f32[3,8,32,128]{3,2,1,0:T(8,128)} %velocity.1) | copy-start | bytes 1179652
  3.3 28.0 %all-to-all-start = ((f32[128,1,1536]{2,1,0:T(1,128)}), f32[128,1,1536]{2,1,0:T(1,128)S(1)}, u32[]{:S(2)}, u32[]{:S(2)}) async-start(f32[128,1,1536]{2,1,0:T(1,128)} %bitcast.12), calls=%async_computation | async-start | bytes 1572864 | tf_op jit(solution)/shard_map/all_to_all | solution.py:538
  14.9 23.5 %collective-permute-start.3 = (f32[3,3,32,128]{3,2,1,0:T(8,128)S(1)}, f32[3,3,32,128]{3,2,1,0:T(8,128)S(1)}, u32[]{:S(2)}, u32[]{:S(2)}) collective-permute-start(f32[3,3,32,128]{3,2,1,0:T(8,128)S(1)} %get-tuple-element.34), channel_id=1, source_target_pairs={{1,2},{2,1},{3,4},{4,3},{5,6},{6,5},{7,8},{8,7},{9,10},{10,9},{11,... | collective-permute-start | bytes 442376 | tf_op jit(solution)/shard_map/ppermute | solution.py:548
  16.6 21.8 %collective-permute-start.2 = (f32[3,3,32,128]{3,2,1,0:T(8,128)S(1)}, f32[3,3,32,128]{3,2,1,0:T(8,128)S(1)}, u32[]{:S(2)}, u32[]{:S(2)}) collective-permute-start(f32[3,3,32,128]{3,2,1,0:T(8,128)S(1)} %get-tuple-element.35), channel_id=1, source_target_pairs={{0,1},{1,0},{2,3},{3,2},{4,5},{5,4},{6,7},{7,6},{8,9},{9,8},{10,11... | collective-permute-start | bytes 442376 | tf_op jit(solution)/shard_map/ppermute | solution.py:548
  36.3 5.1 %collective-permute-start = (f32[2,32,128]{2,1,0:T(8,128)S(1)}, f32[2,32,128]{2,1,0:T(8,128)S(1)}, u32[]{:S(2)}, u32[]{:S(2)}) collective-permute-start(f32[2,32,128]{2,1,0:T(8,128)S(1)} %get-tuple-element.19), channel_id=1, source_target_pairs={{1,2},{2,1},{3,4},{4,3},{5,6},{6,5},{7,8},{8,7},{9,10},{10,9},{11,... | collective-permute-start | bytes 98312 | tf_op jit(solution)/shard_map/ppermute | solution.py:548
  37.8 3.6 %collective-permute-start.1 = (f32[2,32,128]{2,1,0:T(8,128)S(1)}, f32[2,32,128]{2,1,0:T(8,128)S(1)}, u32[]{:S(2)}, u32[]{:S(2)}) collective-permute-start(f32[2,32,128]{2,1,0:T(8,128)S(1)} %get-tuple-element.20), channel_id=1, source_target_pairs={{0,1},{1,0},{2,3},{3,2},{4,5},{5,4},{6,7},{7,6},{8,9},{9,8},{10,11... | collective-permute-start | bytes 98312 | tf_op jit(solution)/shard_map/ppermute | solution.py:548
  41.5 22.1 %copy-start.1 = (bf16[128,256]{1,0:T(8,128)(2,1)S(1)}, bf16[128,256]{1,0:T(8,128)(2,1)}, u32[]{:S(2)}) copy-start(bf16[128,256]{1,0:T(8,128)(2,1)} %get-tuple-element.33.back) | copy-start | bytes 196612
